TPU v7x, 32 devices: a whole 2x2x4 slice. The times are simulated.
32 devices in a mesh: groups: 1, dp: 8 (over z, y), head: 2 (over x), pair: 2 (over core).
Axes of the slice: x: 2, y: 2, z: 4, core: 2. Of those that a mesh axis runs over, the one named last changes fastest.
Arguments:
- queries: bfloat16 [128, 64, 128], P(('groups', 'dp', 'pair'), 'head'), may hold values from -5 to 5
- key_cache: bfloat16 [128, 4, 64, 128], P(('groups', 'dp', 'pair'), 'head'), may hold values from -5 to 5
- value_cache: bfloat16 [128, 4, 64, 128], P(('groups', 'dp', 'pair'), 'head'), may hold values from -6 to 6
- new_key: bfloat16 [128, 4, 128], P(('groups', 'dp', 'pair'), 'head'), may hold values from -5 to 5
- new_value: bfloat16 [128, 4, 128], P(('groups', 'dp', 'pair'), 'head'), may hold values from -6 to 6
- lengths: int32 [128], P(('groups', 'dp', 'pair')), may hold values from 2 to 64, as said below
- expert_input: bfloat16 [128, 4096], P(('groups', 'dp', 'pair')), may hold values from -6 to 6
- routes: int32 [128, 8], P(('groups', 'dp', 'pair')), may hold values from 0 to 15, all different within a row; in each aligned block of 8 rows (0 to 7, 8 to 15, ...) at most 4 rows name the same one
- gate_weights: float32 [128, 8], P(('groups', 'dp', 'pair')), may hold values from 0.05 to 1
- gate_matrix: bfloat16 [16, 768, 4096], P(('dp', 'pair'), 'head'), may hold values from -0.09375 to 0.09375
- up_matrix: bfloat16 [16, 768, 4096], P(('dp', 'pair'), 'head'), may hold values from -0.09375 to 0.09375
- down_matrix: bfloat16 [16, 768, 4096], P(('dp', 'pair'), 'head'), may hold values from -0.21875 to 0.21875
Outputs:
- attention: bfloat16 [128, 64, 128], P(('groups', 'dp', 'pair'), 'head')
- expert_output: bfloat16 [128, 4096], P(('groups', 'dp', 'pair'), 'head')
Inputs may be any that keep to these rules, and one draw needn't show every extreme that they name: `routes`: each row names 8 different experts; in each aligned block of 8 rows (the rows of one device) no expert is named by more than 4 rows, and in every draw some block has an expert named by exactly 4 rows. `lengths`: some request has all 64 positions valid.
All inputs are finite; a program needn't handle non-finite values.
Results may differ from a plain program's by a relative error of at most 0.0051.
Values may be sent and summed in bfloat16 or wider, within the bound.
No kernel may reach another device: no remote copies, remote signals or barrier semaphores. Data moves between devices by JAX's collectives and lax.ppermute only.
A program may use at most 64 MiB of HBM per device.

v0:
```python
import jax
import jax.numpy as jnp
from jax import lax
from jax.sharding import PartitionSpec as P


def attend_local(queries, key_cache, value_cache, new_key, new_value, lengths):
    row_count, head_count, head_size = queries.shape
    kv_heads = key_cache.shape[1]
    cache_len = key_cache.shape[2]
    grouping = head_count // kv_heads
    scaling = head_size ** (-0.5)
    grouped = queries.reshape(row_count, kv_heads, grouping, head_size)
    scores = (
        jnp.einsum("rgqd,rgld->rgql", grouped, key_cache, preferred_element_type=jnp.float32)
        * scaling
    )
    fresh_score = (
        jnp.einsum("rgqd,rgd->rgq", grouped, new_key, preferred_element_type=jnp.float32) * scaling
    )
    valid_mask = (jnp.arange(cache_len)[None, :] < lengths[:, None])[:, None, None, :]
    masked = jnp.where(valid_mask, scores, jnp.float32(-1e30))
    highest = jnp.maximum(jnp.max(masked, axis=-1), fresh_score)
    weights = jnp.where(valid_mask, jnp.exp(masked - highest[..., None]), jnp.float32(0.0))
    fresh_weight = jnp.exp(fresh_score - highest)
    totals = jnp.sum(weights, axis=-1) + fresh_weight
    accumulated = jnp.einsum(
        "rgql,rgld->rgqd",
        weights.astype(jnp.bfloat16),
        value_cache,
        preferred_element_type=jnp.float32,
    )
    accumulated = accumulated + jnp.einsum(
        "rgq,rgd->rgqd",
        fresh_weight.astype(jnp.bfloat16),
        new_value,
        preferred_element_type=jnp.float32,
    )
    return (
        (accumulated / totals[..., None])
        .reshape(row_count, head_count, head_size)
        .astype(jnp.bfloat16)
    )


def expert_block(received, gate_matrix, up_matrix, down_matrix):
    sources, item_count, model_width = received.shape
    flattened = received.reshape(sources * item_count, model_width)
    contract = (((1,), (1,)), ((), ()))
    gate_part = lax.dot_general(
        flattened, gate_matrix[0], contract, preferred_element_type=jnp.float32
    )
    up_part = lax.dot_general(flattened, up_matrix[0], contract, preferred_element_type=jnp.float32)
    hidden = (jax.nn.silu(gate_part) * up_part).astype(jnp.bfloat16)
    result = jnp.dot(hidden, down_matrix[0], preferred_element_type=jnp.float32)
    return result.reshape(sources, item_count, model_width)


def body(
    queries,
    key_cache,
    value_cache,
    new_key,
    new_value,
    lengths,
    expert_input,
    routes,
    gate_weights,
    gate_matrix,
    up_matrix,
    down_matrix,
):
    attention = attend_local(queries, key_cache, value_cache, new_key, new_value, lengths)
    dev_rows, route_count = routes.shape
    model_width = expert_input.shape[1]
    expert_count = lax.axis_size("dp") * lax.axis_size("pair")
    capacity = max(2, dev_rows * route_count // expert_count)
    slot_total = expert_count * capacity
    flat_routes = routes.reshape(-1)
    one_hot = (flat_routes[:, None] == jnp.arange(expert_count)[None, :]).astype(jnp.int32)
    earlier = jnp.cumsum(one_hot, axis=0) - one_hot
    slot_index = jnp.sum(earlier * one_hot, axis=1)
    position = (flat_routes * capacity + slot_index).reshape(dev_rows, route_count)
    targets = jnp.arange(slot_total)
    placing = jnp.sum(
        (position[None, :, :] == targets[:, None, None]).astype(jnp.int32), axis=2
    ).astype(jnp.bfloat16)
    outgoing = jnp.dot(placing, expert_input, preferred_element_type=jnp.float32).astype(
        jnp.bfloat16
    )
    outgoing = outgoing.reshape(expert_count, capacity, model_width)
    weighting = jnp.sum(
        jnp.where(position[:, :, None] == targets[None, None, :], gate_weights[:, :, None], 0.0),
        axis=1,
    )
    partial_value = expert_block(
        lax.all_to_all(outgoing, ("dp", "pair"), split_axis=0, concat_axis=0, tiled=True),
        gate_matrix,
        up_matrix,
        down_matrix,
    )
    shares = lax.psum_scatter(partial_value, "head", scatter_dimension=2, tiled=True)
    returned = lax.all_to_all(shares, ("dp", "pair"), split_axis=0, concat_axis=0, tiled=True)
    weighted = jnp.dot(
        weighting,
        returned.reshape(slot_total, -1),
        precision=lax.Precision.HIGHEST,
        preferred_element_type=jnp.float32,
    )
    expert_output = weighted.astype(jnp.bfloat16)
    return (attention, expert_output)


def solution(mesh):
    placed = (
        P(("groups", "dp", "pair"), "head", None),
        P(("groups", "dp", "pair"), "head", None, None),
        P(("groups", "dp", "pair"), "head", None, None),
        P(("groups", "dp", "pair"), "head", None),
        P(("groups", "dp", "pair"), "head", None),
        P(("groups", "dp", "pair")),
        P(("groups", "dp", "pair"), None),
        P(("groups", "dp", "pair"), None),
        P(("groups", "dp", "pair"), None),
        P(("dp", "pair"), "head", None),
        P(("dp", "pair"), "head", None),
        P(("dp", "pair"), "head", None),
    )
    return jax.shard_map(
        body,
        mesh=mesh,
        in_specs=placed,
        out_specs=(P(("groups", "dp", "pair"), "head", None), P(("groups", "dp", "pair"), "head")),
        check_vma=False,
    )
```

profile of v0, /device:TPU:1, one launch (start us, length us, event | category | flops | bytes accessed | tf_op | source)
XLA Modules:
  0.0 96.2 jit_solution(3214432619196327199)
XLA Ops:
  7.2 0.0 copy-start
  7.2 0.0 reduce-scatter.2.cloned.1.call-start
  7.2 0.9 eq.20
  8.1 0.1 fusion.22
  8.2 0.1 reduce_window_sum.11
  8.3 0.2 select_reduce_fusion.1
  8.5 0.1 reduce_sum.40
  8.6 0.7 multiply_add_fusion
  9.3 0.1 convert_reduce_fusion
  9.4 2.0 %convolution_convert_fusion = bf16[64,4096]{1,0:T(8,128)(2,1)} fusion(bf16[8,4096]{1,0:T(8,128)(2,1)} %param.18, s32[64,8]{0,1:T(8,128)S(1)} %convert_reduce_fusion), kind=kOutput, calls=%fused_computation | convolution fusion | flops 4456960 | bytes 591872 | tf_op jit(solution)/shard_map/dot_general | solution.py:88
  11.4 2.0 %reshape.55 = bf16[16,4,4096]{2,1,0:T(4,128)(2,1)} reshape(bf16[64,4096]{1,0:T(8,128)(2,1)} %convolution_convert_fusion) | data formatting | bytes 1048576 | tf_op jit(solution)/shard_map/reshape | solution.py:91
  13.4 21.5 %all_to_all.10 = bf16[16,4,4096]{2,1,0:T(4,128)(2,1)} all-to-all(bf16[16,4,4096]{2,1,0:T(4,128)(2,1)} %reshape.55), channel_id=1, replica_groups=mesh['groups'=1,'dp'=8,'head'=2,'pair'=2] {'dp','pair'}, dimensions={0} | all-to-all | bytes 1048576 | tf_op jit(solution)/shard_map/all_to_all | solution.py:97
  34.9 2.0 %reshape.56 = bf16[64,4096]{1,0:T(8,128)(2,1)} reshape(bf16[16,4,4096]{2,1,0:T(4,128)(2,1)} %all_to_all.10) | data formatting | bytes 1048576 | tf_op jit(solution)/shard_map/reshape | solution.py:48
  36.9 0.0 copy-start.1
  36.9 0.0 copy-start.2
  36.9 3.3 %fusion.4 = f32[64,384]{1,0:T(8,128)S(1)} fusion(bf16[64,4096]{1,0:T(8,128)(2,1)} %reshape.56, bf16[1,384,4096]{2,1,0:T(8,128)(2,1)} %param.21), kind=kOutput, calls=%fused_computation.5 | convolution fusion | flops 201326592 | bytes 3768320 | tf_op jit(solution)/shard_map/dot_general | solution.py:50
  40.2 0.0 copy-done.1
  40.2 0.0 copy-done.2
  40.2 1.1 %fusion.12 = bf16[64,384]{1,0:T(8,128)(2,1)S(1)} fusion(bf16[64,4096]{1,0:T(8,128)(2,1)S(1)} %copy-done.1, bf16[1,384,4096]{2,1,0:T(8,128)(2,1)S(1)} %copy-done.2, f32[64,384]{1,0:T(8,128)S(1)} %fusion.4), kind=kOutput, calls=%fused_computation.14 | convolution fusion | flops 201474048 | bytes 3817472 | tf_op jit(solution)/shard_map/dot_general | solution.py:53
  41.3 0.0 copy-done
  41.3 0.0 copy-start.4
  41.3 0.0 copy-start.3
  41.3 1.7 %fusion = f32[16,4,4096]{2,0,1:T(8,128)} fusion(bf16[1,384,4096]{2,1,0:T(8,128)(2,1)S(1)} %copy-done, bf16[16,4,384]{2,1,0:T(4,128)(2,1)S(1)} %dot_general.42), kind=kOutput, calls=%fused_computation.1 | convolution fusion | flops 201326592 | bytes 4243456 | tf_op jit(solution)/shard_map/dot_general | solution.py:55
  43.0 0.0 reduce-scatter.2.cloned.1.call-update
  43.0 0.0 copy-done.4
  43.0 0.1 iota_compare_fusion.3
  43.1 0.0 copy-done.3
  43.1 1.2 %fusion.28 = (f32[8,2,16]{2,1,0:T(2,128)S(1)}, f32[8,2,16,64]{3,2,1,0:T(8,128)S(1)}) fusion(bf16[8,2,16,128]{3,2,1,0:T(8,128)(2,1)} %bitcast.28, bf16[8,2,64,128]{3,2,1,0:T(8,128)(2,1)S(1)} %copy-done.3, pred[8,64]{1,0:T(8,128)(4,1)S(1)} %iota_compare_fusion.3), kind=kOutput, calls=%fused_computation.39 | convolution fusion | flops 4243200 | bytes 394752 | tf_op jit(solution)/shard_map/rgqd,rgld->rgql/dot_general | solution.py:15
  44.3 18.4 %reduce-scatter.2.cloned.1.call-done = f32[16,4,2048]{2,0,1:T(8,128)} async-done(((f32[16,4,4096]{2,0,1:T(8,128)}), f32[16,4,2048]{2,0,1:T(8,128)}) %reduce-scatter.2.cloned.1.call-update) | async-done | bytes 524304 | tf_op jit(solution)/shard_map/reduce_scatter | solution.py:102
  62.7 2.2 %copy.20 = f32[16,4,2048]{2,1,0:T(4,128)} copy(f32[16,4,2048]{2,0,1:T(8,128)} %reduce-scatter.2.cloned.1.call-done) | data formatting | bytes 1048576 | tf_op jit(solution)/shard_map/reduce_scatter | solution.py:102
  64.9 6.2 %all-to-all-start.1 = ((f32[16,4,2048]{2,1,0:T(4,128)}), f32[16,4,2048]{2,1,0:T(4,128)}, u32[]{:S(2)}, u32[]{:S(2)}) async-start(f32[16,4,2048]{2,1,0:T(4,128)} %copy.20), calls=%async_computation.2 | async-start | bytes 1048576 | tf_op jit(solution)/shard_map/all_to_all | solution.py:103
  71.1 1.0 %fusion.23 = f32[8,2,1,16]{3,2,1,0:T(1,128)S(1)} fusion(bf16[8,2,16,128]{3,2,1,0:T(8,128)(2,1)} %bitcast.29, bf16[8,2,128,1]{2,1,0,3:T(2,128)(2,1)} %bitcast.32), kind=kOutput, calls=%fused_computation.29 | convolution fusion | flops 65536 | bytes 70656 | tf_op jit(solution)/shard_map/rgqd,rgd->rgq/dot_general | solution.py:19
  72.1 0.7 convert.7
  72.8 0.8 select_reduce_fusion
  73.6 0.2 fusion.15
  73.8 1.8 %fusion.8 = bf16[8,2,16,128]{3,2,1,0:T(8,128)(2,1)} fusion(bf16[8,2,64,128]{3,2,1,0:T(8,128)(2,1)} %param.14, f32[8,2,16,64]{3,2,1,0:T(8,128)S(1)} %get-tuple-element.5, f32[8,2,16]{2,1,0:T(2,128)S(1)} %get-tuple-element.3, f32[8,2,128]{2,1,0:T(2,128)S(1)} %convert.7, f32[8,2,16]{2,1,0:T(2,128)S(1)} %get-tuple-element.2, ...), kind=kOutput, calls=%fused_computation.12 | convolution fusion | flops 4374528 | bytes 404992 | tf_op jit(solution)/shard_map/rgql,rgld->rgqd/dot_general | solution.py:27
  75.7 9.6 %all-to-all-done.1 = f32[16,4,2048]{2,1,0:T(4,128)} async-done(((f32[16,4,2048]{2,1,0:T(4,128)}), f32[16,4,2048]{2,1,0:T(4,128)}, u32[]{:S(2)}, u32[]{:S(2)}) %all-to-all-start.1) | async-done | bytes 524320 | tf_op jit(solution)/shard_map/all_to_all | solution.py:103
  85.3 2.0 %reshape.57 = f32[64,2048]{1,0:T(8,128)} reshape(f32[16,4,2048]{2,1,0:T(4,128)} %all-to-all-done.1) | data formatting | bytes 1048576 | tf_op jit(solution)/shard_map/reshape | solution.py:106
  87.3 2.0 %convolution_convert_fusion.1 = bf16[8,2048]{1,0:T(8,128)(2,1)} fusion(f32[8,64]{1,0:T(8,128)S(1)} %select_reduce_fusion, f32[64,2048]{1,0:T(8,128)} %reshape.57), kind=kOutput, calls=%fused_computation.7 | convolution fusion | flops 12599296 | bytes 559104 | tf_op jit(solution)/shard_map/dot_general | solution.py:104
  (3 shorter events, 0.0 us)
Async XLA Ops:
  7.2 34.1 %copy-start = (bf16[1,384,4096]{2,1,0:T(8,128)(2,1)S(1)}, bf16[1,384,4096]{2,1,0:T(8,128)(2,1)}, u32[]{:S(2)}) copy-start(bf16[1,384,4096]{2,1,0:T(8,128)(2,1)} %param.23) | copy-start | bytes 9437188
  7.2 55.5 %reduce-scatter.2.cloned.1.call-start = ((), (), s32[]{:S(2)}) async-start(), calls=%async_computation.3 | async-start | bytes 1572864 | tf_op jit(solution)/shard_map/reduce_scatter | solution.py:102
  36.9 3.3 %copy-start.1 = (bf16[64,4096]{1,0:T(8,128)(2,1)S(1)}, bf16[64,4096]{1,0:T(8,128)(2,1)}, u32[]{:S(2)}) copy-start(bf16[64,4096]{1,0:T(8,128)(2,1)} %reshape.56) | copy-start | bytes 1572868
  36.9 3.3 %copy-start.2 = (bf16[1,384,4096]{2,1,0:T(8,128)(2,1)S(1)}, bf16[1,384,4096]{2,1,0:T(8,128)(2,1)}, u32[]{:S(2)}) copy-start(bf16[1,384,4096]{2,1,0:T(8,128)(2,1)} %param.22) | copy-start | bytes 9437188
  41.3 1.7 %copy-start.4 = (s32[8]{0:T(128)S(1)}, s32[8]{0:T(128)}, u32[]{:S(2)}) copy-start(s32[8]{0:T(128)} %param.17) | copy-start | bytes 100
  41.3 1.8 %copy-start.3 = (bf16[8,2,64,128]{3,2,1,0:T(8,128)(2,1)S(1)}, bf16[8,2,64,128]{3,2,1,0:T(8,128)(2,1)}, u32[]{:S(2)}) copy-start(bf16[8,2,64,128]{3,2,1,0:T(8,128)(2,1)} %param.13) | copy-start | bytes 786436
  64.9 20.4 %all-to-all-start.1 = ((f32[16,4,2048]{2,1,0:T(4,128)}), f32[16,4,2048]{2,1,0:T(4,128)}, u32[]{:S(2)}, u32[]{:S(2)}) async-start(f32[16,4,2048]{2,1,0:T(4,128)} %copy.20), calls=%async_computation.2 | async-start | bytes 1048576 | tf_op jit(solution)/shard_map/all_to_all | solution.py:103
Sparse Core Ops, SparseCore 0:
  43.1 19.5 reduce-scatter.1
where the time goes:
time: 97.4 us; the launch traced here: 96.2 us
  waiting for transfers between devices  28.1 us (29%)
  blocking collectives  21.5 us (22%)
  between operations  14.1 us (14%)
  matrix products  14 us (14%)
  local copies, waits for them, and re-layouts  9.24 us (9%)
  starting transfers between devices  6.25 us (6%)
  other arithmetic  2.95 us (3%)
    all_to_all x1, blocking collectives, body(): lax.all_to_all(outgoing, ('dp', 'pair'), split_axis=0, concat_axis=0, til...  21.5 us
    reduce_scatter x1, waiting for transfers between devices, body(): lax.psum_scatter(partial_value, 'head', scatter_dimension=2, tiled=True)  18.4 us
    all_to_all x1, waiting for transfers between devices, body(): lax.all_to_all(shares, ('dp', 'pair'), split_axis=0, concat_axis=0, tiled...  9.6 us
    all_to_all x1, starting transfers between devices, body(): lax.all_to_all(shares, ('dp', 'pair'), split_axis=0, concat_axis=0, tiled...  6.21 us
    dot_general x1, matrix products, expert_block(): lax.dot_general(flattened, gate_matrix[0], contract, preferred_element_ty...  3.28 us
    reduce_scatter x1, local copies, waits for them, and re-layouts, body(): lax.psum_scatter(partial_value, 'head', scatter_dimension=2, tiled=True)  2.19 us
    reshape x1, local copies, waits for them, and re-layouts, body(): returned.reshape(slot_total, -1)  2.03 us
    reshape x1, local copies, waits for them, and re-layouts, body(): outgoing = outgoing.reshape(expert_count, capacity, model_width)  2.02 us
  transfers between devices with their start and end apart: 2, of which 2 were waited for; matrix products, arithmetic and copies ran while one was open for 6% of the time, Pallas kernels for 0%

commit v1 on v0

v1 whole, which is shorter than its diff:
```python
import functools

import jax
import jax.numpy as jnp
from jax import lax
from jax.experimental import pallas as pl
from jax.experimental.pallas import tpu as pltpu
from jax.sharding import PartitionSpec as P

LANES = 128
BF16 = jnp.bfloat16
F32 = jnp.float32


def attend_local(queries, key_cache, value_cache, new_key, new_value, lengths):
    row_count, head_count, head_size = queries.shape
    kv_heads = key_cache.shape[1]
    cache_len = key_cache.shape[2]
    grouping = head_count // kv_heads
    scaling = head_size ** (-0.5)
    grouped = queries.reshape(row_count, kv_heads, grouping, head_size)
    scores = (
        jnp.einsum("rgqd,rgld->rgql", grouped, key_cache, preferred_element_type=jnp.float32)
        * scaling
    )
    fresh_score = (
        jnp.einsum("rgqd,rgd->rgq", grouped, new_key, preferred_element_type=jnp.float32) * scaling
    )
    valid_mask = (jnp.arange(cache_len)[None, :] < lengths[:, None])[:, None, None, :]
    masked = jnp.where(valid_mask, scores, jnp.float32(-1e30))
    highest = jnp.maximum(jnp.max(masked, axis=-1), fresh_score)
    weights = jnp.where(valid_mask, jnp.exp(masked - highest[..., None]), jnp.float32(0.0))
    fresh_weight = jnp.exp(fresh_score - highest)
    totals = jnp.sum(weights, axis=-1) + fresh_weight
    accumulated = jnp.einsum(
        "rgql,rgld->rgqd",
        weights.astype(jnp.bfloat16),
        value_cache,
        preferred_element_type=jnp.float32,
    )
    accumulated = accumulated + jnp.einsum(
        "rgq,rgd->rgqd",
        fresh_weight.astype(jnp.bfloat16),
        new_value,
        preferred_element_type=jnp.float32,
    )
    return (
        (accumulated / totals[..., None])
        .reshape(row_count, head_count, head_size)
        .astype(jnp.bfloat16)
    )


def partner(index, step, count):
    if count & (count - 1) == 0:
        return index ^ step
    return (index + step) % count


def home_of(index, step, count):
    if count & (count - 1) == 0:
        return index ^ step
    return (index - step + count) % count


def ffn_kernel(dims, expert_ref, base_ref, own_ref, other_ref, gate_hbm, up_hbm, down_hbm, out_ref,
               gate, up, down, gate_sems, up_sems, down_sems):
    dev_rows, width, route_count, capacity, heads, sources = dims
    hidden_size = gate.shape[0]
    chunks = gate_sems.shape[0]
    chunk = hidden_size // chunks
    share = width // heads
    copies = []
    for i in range(chunks):
        part = pl.ds(i * chunk, chunk)
        a = pltpu.make_async_copy(gate_hbm.at[0, part], gate.at[part], gate_sems.at[i])
        b = pltpu.make_async_copy(up_hbm.at[0, part], up.at[part], up_sems.at[i])
        a.start()
        b.start()
        copies.append((a, b))
    down_copies = []
    for h in range(heads):
        part = pl.ds(h * share, share)
        a = pltpu.make_async_copy(down_hbm.at[0, :, part], down.at[:, part], down_sems.at[h])
        a.start()
        down_copies.append(a)

    rows = sources * dev_rows
    slots = sources * capacity
    names = jnp.concatenate([own_ref[:, width:], other_ref[:, width:]], axis=0)
    lane = lax.broadcasted_iota(jnp.int32, names.shape, 1)
    expert = expert_ref[0].astype(F32)
    named = jnp.where((lane < route_count) & (names.astype(F32) == expert), 1.0, 0.0).astype(BF16)
    member = lax.dot_general(
        jnp.ones((8, names.shape[1]), BF16), named, (((1,), (1,)), ((), ())),
        preferred_element_type=F32,
    )
    above = lax.broadcasted_iota(jnp.int32, (rows, rows), 0)
    below = lax.broadcasted_iota(jnp.int32, (rows, rows), 1)
    earlier = (above < below) & (above // dev_rows == below // dev_rows)
    rank = jnp.dot(
        member.astype(BF16), jnp.where(earlier, 1.0, 0.0).astype(BF16), preferred_element_type=F32
    )
    target = jnp.where(member > 0.5, base_ref[...] + rank.astype(jnp.int32), -1)
    slot = lax.broadcasted_iota(jnp.int32, (slots, rows), 0)
    placing = jnp.where(slot == target[0:1], 1.0, 0.0).astype(BF16)

    inputs = jnp.concatenate([own_ref[:, :width], other_ref[:, :width]], axis=0)
    contract = (((1,), (1,)), ((), ()))
    parts = []
    for i in range(chunks):
        copies[i][0].wait()
        copies[i][1].wait()
        part = pl.ds(i * chunk, chunk)
        gate_part = lax.dot_general(inputs, gate[part], contract, preferred_element_type=F32)
        up_part = lax.dot_general(inputs, up[part], contract, preferred_element_type=F32)
        hidden = (gate_part / (1.0 + jnp.exp(-gate_part)) * up_part).astype(BF16)
        parts.append(jnp.dot(placing, hidden, preferred_element_type=F32).astype(BF16))
    hidden = jnp.concatenate(parts, axis=1)

    pieces = 8 // capacity
    piece = share // pieces
    row = lax.broadcasted_iota(jnp.int32, (8, piece), 0)
    for h in range(heads):
        down_copies[h].wait()
        result = jnp.dot(hidden, down[:, h * share : (h + 1) * share], preferred_element_type=F32)
        for block in range(slots // 8):
            columns = [
                result[block * 8 : block * 8 + 8, k * piece : (k + 1) * piece]
                for k in range(pieces)
            ]
            for j in range(pieces):
                packed = None
                for k in range(pieces):
                    shift = (k - j) * capacity % 8
                    moved = pltpu.roll(columns[k], shift, 0) if shift else columns[k]
                    packed = moved if packed is None else jnp.where(row // capacity == k, moved, packed)
                out_ref[(block * pieces + j) * heads + h] = packed.astype(BF16)


def expert_block(expert, base, own, other, gate_matrix, up_matrix, down_matrix, dims):
    dev_rows, width, route_count, capacity, heads, sources = dims
    hidden_size = gate_matrix.shape[1]
    chunks = max(1, hidden_size // 128)
    while hidden_size % chunks:
        chunks -= 1
    piece = width // heads * capacity // 8
    return pl.pallas_call(
        functools.partial(ffn_kernel, dims),
        out_shape=jax.ShapeDtypeStruct((sources * heads, 8, piece), BF16),
        in_specs=[
            pl.BlockSpec(memory_space=pltpu.SMEM),
            pl.BlockSpec(memory_space=pltpu.VMEM),
            pl.BlockSpec(memory_space=pltpu.VMEM),
            pl.BlockSpec(memory_space=pltpu.VMEM),
            pl.BlockSpec(memory_space=pl.ANY),
            pl.BlockSpec(memory_space=pl.ANY),
            pl.BlockSpec(memory_space=pl.ANY),
        ],
        out_specs=pl.BlockSpec(memory_space=pltpu.VMEM),
        scratch_shapes=[
            pltpu.VMEM((hidden_size, width), BF16),
            pltpu.VMEM((hidden_size, width), BF16),
            pltpu.VMEM((hidden_size, width), BF16),
            pltpu.SemaphoreType.DMA((chunks,)),
            pltpu.SemaphoreType.DMA((chunks,)),
            pltpu.SemaphoreType.DMA((heads,)),
        ],
        compiler_params=pltpu.CompilerParams(vmem_limit_bytes=40 * 1024 * 1024),
        cost_estimate=pl.CostEstimate(
            flops=2 * sources * dev_rows * width * hidden_size * 3,
            bytes_accessed=hidden_size * width * 6,
            transcendentals=sources * dev_rows * hidden_size,
        ),
    )(expert, base, own, other, gate_matrix, up_matrix, down_matrix)


def combine_kernel(pieces, terms, lhs_ref, got_ref, out_ref):
    blocks, rows, piece = got_ref.shape
    got = got_ref[...].reshape(blocks * rows, piece)
    sums = jnp.dot(lhs_ref[...], got, preferred_element_type=F32)
    height = out_ref.shape[0]
    for k in range(pieces):
        total = None
        for t in range(terms):
            start = (k * terms + t) * height
            term = sums[start : start + height]
            total = term if total is None else total + term
        out_ref[:, k * piece : (k + 1) * piece] = total.astype(BF16)


def body(
    queries,
    key_cache,
    value_cache,
    new_key,
    new_value,
    lengths,
    expert_input,
    routes,
    gate_weights,
    gate_matrix,
    up_matrix,
    down_matrix,
):
    dev_rows, route_count = routes.shape
    width = expert_input.shape[1]
    steps, pairs, heads = lax.axis_size("dp"), lax.axis_size("pair"), lax.axis_size("head")
    sources = steps * pairs
    capacity = max(2, dev_rows * route_count // sources)
    my_dp, my_pair = lax.axis_index("dp"), lax.axis_index("pair")

    labels = jnp.pad(routes.astype(BF16), ((0, 0), (0, LANES - route_count)))
    block = jnp.concatenate([expert_input, labels], axis=1)
    order = sorted(range(1, steps), key=lambda s: (-(s // 4), -(s // 2), s))
    arrived = [block]
    for step in order:
        pairs_of = [(i, partner(i, step, steps)) for i in range(steps)]
        arrived.append(lax.ppermute(block, "dp", pairs_of))
    own = jnp.concatenate(arrived, axis=0)
    other = lax.ppermute(own, "pair", [(0, 1), (1, 0)])
    homes = jnp.stack([home_of(my_dp, step, steps) for step in [0] + order])
    homes = jnp.stack([homes * pairs + my_pair, homes * pairs + (1 - my_pair)])
    base = jnp.broadcast_to(homes[:, :, None] * capacity, homes.shape + (dev_rows,))
    base = jnp.broadcast_to(base.reshape(1, -1).astype(jnp.int32), (8, sources * dev_rows))
    expert = (my_dp * pairs + my_pair).astype(jnp.int32).reshape(1)

    dims = (dev_rows, width, route_count, capacity, heads, sources)
    sent = expert_block(expert, base, own, other, gate_matrix, up_matrix, down_matrix, dims)
    got = lax.all_to_all(sent, ("dp", "pair", "head"), split_axis=0, concat_axis=0, tiled=True)

    attention = attend_local(queries, key_cache, value_cache, new_key, new_value, lengths)

    named = routes[:, :, None] == jnp.arange(sources)[None, None, :]
    member = jnp.any(named, axis=1)
    coefficient = jnp.sum(jnp.where(named, gate_weights[:, :, None], 0.0), axis=1)
    slot = jnp.cumsum(member.astype(jnp.int32), axis=0) - 1
    pieces = 8 // capacity
    terms = []
    rest = coefficient
    for _ in range(3):
        term = lax.reduce_precision(rest, 8, 7)
        terms.append(term)
        rest = rest - term
    terms = jnp.stack(terms)
    place = jnp.arange(8)
    hit = (
        (place[None, None, None, :] // capacity == jnp.arange(pieces)[:, None, None, None])
        & (place[None, None, None, :] % capacity == slot[None, :, :, None])
        & member[None, :, :, None]
    )
    lhs = jnp.where(hit[:, None], terms[None, :, :, :, None], 0.0)
    lhs = jnp.broadcast_to(lhs[:, :, :, :, None, :], lhs.shape[:4] + (heads, 8))
    lhs = lhs.reshape(pieces * 3 * dev_rows, sources * heads * 8).astype(BF16)
    expert_output = pl.pallas_call(
        functools.partial(combine_kernel, pieces, 3),
        out_shape=jax.ShapeDtypeStruct((dev_rows, width // heads), BF16),
    )(lhs, got)
    return (attention, expert_output)


def solution(mesh):
    placed = (
        P(("groups", "dp", "pair"), "head", None),
        P(("groups", "dp", "pair"), "head", None, None),
        P(("groups", "dp", "pair"), "head", None, None),
        P(("groups", "dp", "pair"), "head", None),
        P(("groups", "dp", "pair"), "head", None),
        P(("groups", "dp", "pair")),
        P(("groups", "dp", "pair"), None),
        P(("groups", "dp", "pair"), None),
        P(("groups", "dp", "pair"), None),
        P(("dp", "pair"), "head", None),
        P(("dp", "pair"), "head", None),
        P(("dp", "pair"), "head", None),
    )
    return jax.shard_map(
        body,
        mesh=mesh,
        in_specs=placed,
        out_specs=(P(("groups", "dp", "pair"), "head", None), P(("groups", "dp", "pair"), "head")),
        check_vma=False,
    )
```

time: 97.4 us -> 60.4 us (0.62)
  blocking collectives: 21.5 us -> 0 us
  between operations: 14.1 us -> 0.85 us
  matrix products: 14 us -> 2.35 us
  starting transfers between devices: 6.25 us -> 15.9 us
  waiting for transfers between devices: 28.1 us -> 20.4 us
  Pallas kernels: 0 us -> 7.01 us
  other arithmetic: 2.95 us -> 5.19 us
  local copies, waits for them, and re-layouts: 9.24 us -> 8.19 us
    all_to_all x1 -> x0, blocking collectives: 21.5 us -> none  [body(): lax.all_to_all(outgoing, ('dp', 'pair'), split_axis=0, concat_axis=0, til...]
    reduce_scatter x1 -> x0, waiting for transfers between devices: 18.4 us -> none  [body(): lax.psum_scatter(partial_value, 'head', scatter_dimension=2, tiled=True)]
    ppermute x0 -> x8, starting transfers between devices: none -> 11.4 us  [the longest x7 10.3 us: body(): arrived.append(lax.ppermute(block, 'dp', pairs_of))]
    dot_general x5 -> x0, matrix products: 10 us -> none  [the longest x1 3.28 us: expert_block(): lax.dot_general(flattened, gate_matrix[0], contract, preferred_element_ty...]
    pallas_call x0 -> x2, Pallas kernels: none -> 7.01 us  [the longest x1 5.13 us: expert_block(): pl.pallas_call(functools.partial(ffn_kernel, dims), out_shape=jax.ShapeDt...]
    unnamed x10 -> x20, local copies, waits for them, and re-layouts: 0.03 us -> 6.54 us
    reshape x3 -> x0, local copies, waits for them, and re-layouts: 6.01 us -> none  [the longest x1 2.03 us: body(): returned.reshape(slot_total, -1)]
    ppermute x0 -> x8, waiting for transfers between devices: none -> 5.88 us  [the longest x7 5.87 us: body(): arrived.append(lax.ppermute(block, 'dp', pairs_of))]
  transfers between devices with their start and end apart: 2 -> 9, of which waited for: 2 -> 4; matrix products, arithmetic and copies ran while one was open for 6% -> 13% of each run, Pallas kernels for 0% -> 0%
where the time goes in v1:
time: 60.4 us; the launch traced here: 59.9 us
  waiting for transfers between devices  20.4 us (34%)
  starting transfers between devices  15.9 us (26%)
  local copies, waits for them, and re-layouts  8.19 us (14%)
  Pallas kernels  7.01 us (12%)
  other arithmetic  5.19 us (9%)
  matrix products  2.35 us (4%)
  between operations  0.85 us (1%)
    all_to_all x1, waiting for transfers between devices, body(): lax.all_to_all(sent, ('dp', 'pair', 'head'), split_axis=0, concat_axis=0,...  14.5 us
    ppermute x7, starting transfers between devices, body(): arrived.append(lax.ppermute(block, 'dp', pairs_of))  10.3 us
    unnamed x20, local copies, waits for them, and re-layouts  6.54 us
    ppermute x7, waiting for transfers between devices, body(): arrived.append(lax.ppermute(block, 'dp', pairs_of))  5.87 us
    pallas_call x1, Pallas kernels, expert_block(): pl.pallas_call(functools.partial(ffn_kernel, dims), out_shape=jax.ShapeDt...  5.13 us
    all_to_all x1, starting transfers between devices, body(): lax.all_to_all(sent, ('dp', 'pair', 'head'), split_axis=0, concat_axis=0,...  4.55 us
    pallas_call x1, Pallas kernels, body(): pl.pallas_call(functools.partial(combine_kernel, pieces, 3), out_shape=ja...  1.88 us
    dot_general x1, matrix products, attend_local(): jnp.einsum('rgqd,rgld->rgql', grouped, key_cache, preferred_element_type=...  1.31 us
  transfers between devices with their start and end apart: 9, of which 4 were waited for; matrix products, arithmetic and copies ran while one was open for 13% of the time, Pallas kernels for 0%

profile of v1, /device:TPU:1, one launch (start us, length us, event | category | flops | bytes accessed | tf_op | source)
XLA Modules:
  0.0 59.9 jit_solution(7798082567291865391)
XLA Ops:
  0.6 0.0 copy-start
  0.6 0.7 %convert_element_type.36 = bf16[8,8]{1,0:T(8,128)(2,1)S(1)} convert(s32[8,8]{1,0:T(8,128)} %param.19) | non-fusion elementwise | flops 64 | bytes 384 | tf_op jit(solution)/shard_map/convert_element_type | solution.py:213
  1.4 0.8 %fusion.6 = (bf16[8,4224]{1,0:T(8,128)(2,1)S(1)}, bf16[64,4224]{1,0:T(8,128)(2,1)S(1)}) fusion(bf16[8,8]{1,0:T(8,128)(2,1)S(1)} %convert_element_type.36, bf16[8,4096]{1,0:T(8,128)(2,1)} %param.18), kind=kLoop, calls=%fused_computation.12 | loop fusion | flops 202751 | bytes 200832 | tf_op jit(solution)/shard_map/concatenate | solution.py:214
  2.2 4.2 %collective-permute-start = (bf16[8,4224]{1,0:T(8,128)(2,1)S(1)}, bf16[8,4224]{1,0:T(8,128)(2,1)S(1)}, u32[]{:S(2)}, u32[]{:S(2)}) collective-permute-start(bf16[8,4224]{1,0:T(8,128)(2,1)S(1)} %get-tuple-element.2), channel_id=1, source_target_pairs={{0,24},{4,28},{8,16},{12,20},{16,8},{20,12},{24,0},{28,4},{1,25},{... | collective-permute-start | bytes 202760 | tf_op jit(solution)/shard_map/ppermute | solution.py:219
  6.4 1.0 %collective-permute-start.1 = (bf16[8,4224]{1,0:T(8,128)(2,1)S(1)}, bf16[8,4224]{1,0:T(8,128)(2,1)S(1)}, u32[]{:S(2)}, u32[]{:S(2)}) collective-permute-start(bf16[8,4224]{1,0:T(8,128)(2,1)S(1)} %get-tuple-element.2), channel_id=1, source_target_pairs={{0,28},{4,24},{8,20},{12,16},{16,12},{20,8},{24,4},{28,0},{1,29},{... | collective-permute-start | bytes 202760 | tf_op jit(solution)/shard_map/ppermute | solution.py:219
  7.5 0.4 collective-permute-start.2
  7.9 1.9 %collective-permute-start.3 = (bf16[8,4224]{1,0:T(8,128)(2,1)S(1)}, bf16[8,4224]{1,0:T(8,128)(2,1)S(1)}, u32[]{:S(2)}, u32[]{:S(2)}) collective-permute-start(bf16[8,4224]{1,0:T(8,128)(2,1)S(1)} %get-tuple-element.2), channel_id=1, source_target_pairs={{0,20},{4,16},{8,28},{12,24},{16,4},{20,0},{24,12},{28,8},{1,21},{... | collective-permute-start | bytes 202760 | tf_op jit(solution)/shard_map/ppermute | solution.py:219
  9.8 1.2 %collective-permute-start.4 = (bf16[8,4224]{1,0:T(8,128)(2,1)S(1)}, bf16[8,4224]{1,0:T(8,128)(2,1)S(1)}, u32[]{:S(2)}, u32[]{:S(2)}) collective-permute-start(bf16[8,4224]{1,0:T(8,128)(2,1)S(1)} %get-tuple-element.2), channel_id=1, source_target_pairs={{0,8},{4,12},{8,0},{12,4},{16,24},{20,28},{24,16},{28,20},{1,9},{5... | collective-permute-start | bytes 202760 | tf_op jit(solution)/shard_map/ppermute | solution.py:219
  11.0 0.8 %fusion.11 = pred[8,16]{1,0:T(8,128)(4,1)S(1)} fusion(s32[8,8]{1,0:T(8,128)} %param.19), kind=kLoop, calls=%fused_computation.19 | loop fusion | flops 1920 | bytes 384 | tf_op jit(solution)/shard_map/reduce_or | solution.py:235
  11.8 0.8 %select_reduce_fusion = f32[8,16]{1,0:T(8,128)S(1)} fusion(f32[8,8]{1,0:T(8,128)} %param.20, s32[8,8]{1,0:T(8,128)} %param.19), kind=kLoop, calls=%fused_computation.16 | loop fusion | flops 2944 | bytes 1024 | tf_op jit(solution)/shard_map/reduce_sum | solution.py:236
  12.6 0.1 broadcast_compare_fusion
  12.7 0.1 and_and_fusion
  12.8 0.1 select_convert_fusion
  13.0 0.1 stack.47
  13.1 0.0 collective-permute-done
  13.1 1.3 %collective-permute-start.5 = (bf16[8,4224]{1,0:T(8,128)(2,1)S(1)}, bf16[8,4224]{1,0:T(8,128)(2,1)S(1)}, u32[]{:S(2)}, u32[]{:S(2)}) collective-permute-start(bf16[8,4224]{1,0:T(8,128)(2,1)S(1)} %get-tuple-element.2), channel_id=1, source_target_pairs={{0,12},{4,8},{8,4},{12,0},{16,28},{20,24},{24,20},{28,16},{1,13},{... | collective-permute-start | bytes 202760 | tf_op jit(solution)/shard_map/ppermute | solution.py:219
  14.4 0.0 collective-permute-done.1
  14.4 0.3 collective-permute-start.6
  14.7 0.7 %collective-permute-done.2 = bf16[8,4224]{1,0:T(8,128)(2,1)S(1)} collective-permute-done((bf16[8,4224]{1,0:T(8,128)(2,1)S(1)}, bf16[8,4224]{1,0:T(8,128)(2,1)S(1)}, u32[]{:S(2)}, u32[]{:S(2)}) %collective-permute-start.2) | collective-permute-done | bytes 67616 | tf_op jit(solution)/shard_map/ppermute | solution.py:219
  15.4 3.2 %collective-permute-done.3 = bf16[8,4224]{1,0:T(8,128)(2,1)S(1)} collective-permute-done((bf16[8,4224]{1,0:T(8,128)(2,1)S(1)}, bf16[8,4224]{1,0:T(8,128)(2,1)S(1)}, u32[]{:S(2)}, u32[]{:S(2)}) %collective-permute-start.3) | collective-permute-done | bytes 67616 | tf_op jit(solution)/shard_map/ppermute | solution.py:219
  18.5 0.0 collective-permute-done.4
  18.6 0.0 collective-permute-done.5
  18.6 2.1 %collective-permute-done.6 = bf16[8,4224]{1,0:T(8,128)(2,1)S(1)} collective-permute-done((bf16[8,4224]{1,0:T(8,128)(2,1)S(1)}, bf16[8,4224]{1,0:T(8,128)(2,1)S(1)}, u32[]{:S(2)}, u32[]{:S(2)}) %collective-permute-start.6) | collective-permute-done | bytes 67616 | tf_op jit(solution)/shard_map/ppermute | solution.py:219
  20.7 1.0 %collective-permute-start.7 = (bf16[64,4224]{1,0:T(8,128)(2,1)S(1)}, bf16[64,4224]{1,0:T(8,128)(2,1)S(1)}, u32[]{:S(2)}, u32[]{:S(2)}) collective-permute-start(bf16[64,4224]{1,0:T(8,128)(2,1)S(1)} %constant_dynamic-update-slice_fusion.own_ref), channel_id=1, source_target_pairs={{0,1},{1,0},{2,3},{3,2},{4,5},{5,4},{6,7},{7,6},{8,9},{9,8},{10,11... | collective-permute-start | bytes 1622024 | tf_op jit(solution)/shard_map/ppermute | solution.py:221
  21.7 0.1 broadcast_in_dim.93
  21.8 0.1 broadcast_in_dim.94
  21.9 0.3 broadcast_in_dim.92
  22.1 1.1 %convert_element_type.35.lhs_ref = bf16[48,256]{1,0:T(8,128)(2,1)} reshape(bf16[2,3,8,16,2,8]{5,4,3,2,1,0:T(2,128)(2,1)S(1)} %broadcast_in_dim.92) | data formatting | bytes 49152 | tf_op jit(solution)/shard_map/convert_element_type | solution.py:254
  23.3 0.7 %convert.7 = f32[8,2,128]{2,1,0:T(2,128)S(1)} convert(bf16[8,2,128]{2,1,0:T(2,128)(2,1)} %param.16) | non-fusion elementwise | flops 2048 | bytes 12288 | tf_op jit(solution)/shard_map/convert.1
  23.9 0.7 %iota_compare_fusion.2 = pred[8,64]{1,0:T(8,128)(4,1)S(1)} fusion(s32[8]{0:T(128)} %param.17), kind=kLoop, calls=%fused_computation.37 | loop fusion | flops 512 | bytes 544 | tf_op jit(solution)/shard_map/lt | solution.py:29
  24.7 1.3 %fusion.17 = (f32[8,2,16]{2,1,0:T(2,128)S(1)}, f32[8,2,16,64]{3,2,1,0:T(8,128)S(1)}) fusion(bf16[8,2,16,128]{3,2,1,0:T(8,128)(2,1)} %bitcast.31, bf16[8,2,64,128]{3,2,1,0:T(8,128)(2,1)} %param.13, pred[8,64]{1,0:T(8,128)(4,1)S(1)} %iota_compare_fusion.2), kind=kOutput, calls=%fused_computation.51 | convolution fusion | flops 4243200 | bytes 394752 | tf_op jit(solution)/shard_map/rgqd,rgld->rgql/dot_general | solution.py:23
  26.0 0.0 collective-permute-done.7.other_ref
  26.0 0.0 copy-start.1
  26.0 1.9 %copy-done.1 = bf16[1,384,4096]{2,1,0:T(8,128)(2,1)S(1)} copy-done((bf16[1,384,4096]{2,1,0:T(8,128)(2,1)S(1)}, bf16[1,384,4096]{2,1,0:T(8,128)(2,1)}, u32[]{:S(2)}) %copy-start.1) | copy-done | bytes 3145752
  27.9 0.0 copy-start.2
  27.9 1.9 %copy-done.2 = bf16[1,384,4096]{2,1,0:T(8,128)(2,1)S(1)} copy-done((bf16[1,384,4096]{2,1,0:T(8,128)(2,1)S(1)}, bf16[1,384,4096]{2,1,0:T(8,128)(2,1)}, u32[]{:S(2)}) %copy-start.2) | copy-done | bytes 3145752
  29.8 1.9 %copy-done.3 = bf16[1,384,4096]{2,1,0:T(8,128)(2,1)S(1)} copy-done((bf16[1,384,4096]{2,1,0:T(8,128)(2,1)S(1)}, bf16[1,384,4096]{2,1,0:T(8,128)(2,1)}, u32[]{:S(2)}) %copy-start.3) | copy-done | bytes 3145752
  31.7 5.1 %shard_map.131 = bf16[32,8,1024]{2,1,0:T(8,128)(2,1)} custom-call(s32[1]{0:T(128)} %bitcast.6.expert_ref, s32[8,128]{1,0:T(8,128)S(1)} %broadcast_in_dim.95.base_ref, bf16[64,4224]{1,0:T(8,128)(2,1)S(1)} %constant_dynamic-update-slice_fusion.own_ref, bf16[64,4224]{1,0:T(8,128)(2,1)S(1)} %collective-permute-done.7.other_ref, ...), custom_call_target="tpu_custom_call" | custom-call | flops 1207959552 | bytes 9437184 | tf_op jit(solution)/shard_map/pallas_call | solution.py:148
  36.8 4.6 %all-to-all-start = ((bf16[32,8,1024]{2,1,0:T(8,128)(2,1)}), bf16[32,8,1024]{2,1,0:T(8,128)(2,1)S(1)}, u32[]{:S(2)}, u32[]{:S(2)}) async-start(bf16[32,8,1024]{2,1,0:T(8,128)(2,1)} %shard_map.131), calls=%async_computation | async-start | bytes 1048576 | tf_op jit(solution)/shard_map/all_to_all | solution.py:230
  41.4 0.0 copy-done.5
  41.4 0.0 copy-done.6
  41.4 0.1 fusion.12
  41.6 0.2 fusion.4
  41.8 0.0 copy-done
  41.8 0.9 %fusion.2 = bf16[8,2,16,128]{3,2,1,0:T(8,128)(2,1)} fusion(bf16[8,2,64,128]{3,2,1,0:T(8,128)(2,1)S(1)} %copy-done, f32[8,2,16,64]{3,2,1,0:T(8,128)S(1)} %get-tuple-element.12, f32[8,2,16]{2,1,0:T(2,128)S(1)} %get-tuple-element.5, f32[8,2,128]{2,1,0:T(2,128)S(1)} %convert.7, f32[8,2,16]{2,1,0:T(2,128)S(1)} %get-tuple-element.4, ...), kind=kOutput, calls=%fused_computation.4 | convolution fusion | flops 4374528 | bytes 404992 | tf_op jit(solution)/shard_map/rgql,rgld->rgqd/dot_general | solution.py:35
  42.7 14.5 %all-to-all-done.got_ref = bf16[32,8,1024]{2,1,0:T(8,128)(2,1)S(1)} async-done(((bf16[32,8,1024]{2,1,0:T(8,128)(2,1)}), bf16[32,8,1024]{2,1,0:T(8,128)(2,1)S(1)}, u32[]{:S(2)}, u32[]{:S(2)}) %all-to-all-start) | async-done | bytes 524320 | tf_op jit(solution)/shard_map/all_to_all | solution.py:230
  57.2 0.8 %copy-done.4 = bf16[32,8,1024]{2,1,0:T(8,128)(2,1)} copy-done((bf16[32,8,1024]{2,1,0:T(8,128)(2,1)}, bf16[32,8,1024]{2,1,0:T(8,128)(2,1)S(1)}, u32[]{:S(2)}) %copy-start.4) | copy-done | bytes 524312
  58.0 1.9 %shard_map.132 = bf16[8,2048]{1,0:T(8,128)(2,1)} custom-call(bf16[48,256]{1,0:T(8,128)(2,1)} %convert_element_type.35.lhs_ref, bf16[32,8,1024]{2,1,0:T(8,128)(2,1)} %copy-done.4), custom_call_target="tpu_custom_call" | custom-call | tf_op jit(solution)/shard_map/pallas_call | solution.py:255
  (24 shorter events, 0.2 us)
Async XLA Ops:
  0.6 41.2 %copy-start = (bf16[8,2,64,128]{3,2,1,0:T(8,128)(2,1)S(1)}, bf16[8,2,64,128]{3,2,1,0:T(8,128)(2,1)}, u32[]{:S(2)}) copy-start(bf16[8,2,64,128]{3,2,1,0:T(8,128)(2,1)} %param.14) | copy-start | bytes 786436
  2.2 10.8 %collective-permute-start = (bf16[8,4224]{1,0:T(8,128)(2,1)S(1)}, bf16[8,4224]{1,0:T(8,128)(2,1)S(1)}, u32[]{:S(2)}, u32[]{:S(2)}) collective-permute-start(bf16[8,4224]{1,0:T(8,128)(2,1)S(1)} %get-tuple-element.2), channel_id=1, source_target_pairs={{0,24},{4,28},{8,16},{12,20},{16,8},{20,12},{24,0},{28,4},{1,25},{... | collective-permute-start | bytes 202760 | tf_op jit(solution)/shard_map/ppermute | solution.py:219
  6.4 8.0 %collective-permute-start.1 = (bf16[8,4224]{1,0:T(8,128)(2,1)S(1)}, bf16[8,4224]{1,0:T(8,128)(2,1)S(1)}, u32[]{:S(2)}, u32[]{:S(2)}) collective-permute-start(bf16[8,4224]{1,0:T(8,128)(2,1)S(1)} %get-tuple-element.2), channel_id=1, source_target_pairs={{0,28},{4,24},{8,20},{12,16},{16,12},{20,8},{24,4},{28,0},{1,29},{... | collective-permute-start | bytes 202760 | tf_op jit(solution)/shard_map/ppermute | solution.py:219
  7.5 7.9 %collective-permute-start.2 = (bf16[8,4224]{1,0:T(8,128)(2,1)S(1)}, bf16[8,4224]{1,0:T(8,128)(2,1)S(1)}, u32[]{:S(2)}, u32[]{:S(2)}) collective-permute-start(bf16[8,4224]{1,0:T(8,128)(2,1)S(1)} %get-tuple-element.2), channel_id=1, source_target_pairs={{0,16},{4,20},{8,24},{12,28},{16,0},{20,4},{24,8},{28,12},{1,17},{... | collective-permute-start | bytes 202760 | tf_op jit(solution)/shard_map/ppermute | solution.py:219
  7.9 10.7 %collective-permute-start.3 = (bf16[8,4224]{1,0:T(8,128)(2,1)S(1)}, bf16[8,4224]{1,0:T(8,128)(2,1)S(1)}, u32[]{:S(2)}, u32[]{:S(2)}) collective-permute-start(bf16[8,4224]{1,0:T(8,128)(2,1)S(1)} %get-tuple-element.2), channel_id=1, source_target_pairs={{0,20},{4,16},{8,28},{12,24},{16,4},{20,0},{24,12},{28,8},{1,21},{... | collective-permute-start | bytes 202760 | tf_op jit(solution)/shard_map/ppermute | solution.py:219
  9.8 8.8 %collective-permute-start.4 = (bf16[8,4224]{1,0:T(8,128)(2,1)S(1)}, bf16[8,4224]{1,0:T(8,128)(2,1)S(1)}, u32[]{:S(2)}, u32[]{:S(2)}) collective-permute-start(bf16[8,4224]{1,0:T(8,128)(2,1)S(1)} %get-tuple-element.2), channel_id=1, source_target_pairs={{0,8},{4,12},{8,0},{12,4},{16,24},{20,28},{24,16},{28,20},{1,9},{5... | collective-permute-start | bytes 202760 | tf_op jit(solution)/shard_map/ppermute | solution.py:219
  13.1 5.5 %collective-permute-start.5 = (bf16[8,4224]{1,0:T(8,128)(2,1)S(1)}, bf16[8,4224]{1,0:T(8,128)(2,1)S(1)}, u32[]{:S(2)}, u32[]{:S(2)}) collective-permute-start(bf16[8,4224]{1,0:T(8,128)(2,1)S(1)} %get-tuple-element.2), channel_id=1, source_target_pairs={{0,12},{4,8},{8,4},{12,0},{16,28},{20,24},{24,20},{28,16},{1,13},{... | collective-permute-start | bytes 202760 | tf_op jit(solution)/shard_map/ppermute | solution.py:219
  14.4 6.2 %collective-permute-start.6 = (bf16[8,4224]{1,0:T(8,128)(2,1)S(1)}, bf16[8,4224]{1,0:T(8,128)(2,1)S(1)}, u32[]{:S(2)}, u32[]{:S(2)}) collective-permute-start(bf16[8,4224]{1,0:T(8,128)(2,1)S(1)} %get-tuple-element.2), channel_id=1, source_target_pairs={{0,4},{4,0},{8,12},{12,8},{16,20},{20,16},{24,28},{28,24},{1,5},{5... | collective-permute-start | bytes 202760 | tf_op jit(solution)/shard_map/ppermute | solution.py:219
  20.7 5.3 %collective-permute-start.7 = (bf16[64,4224]{1,0:T(8,128)(2,1)S(1)}, bf16[64,4224]{1,0:T(8,128)(2,1)S(1)}, u32[]{:S(2)}, u32[]{:S(2)}) collective-permute-start(bf16[64,4224]{1,0:T(8,128)(2,1)S(1)} %constant_dynamic-update-slice_fusion.own_ref), channel_id=1, source_target_pairs={{0,1},{1,0},{2,3},{3,2},{4,5},{5,4},{6,7},{7,6},{8,9},{9,8},{10,11... | collective-permute-start | bytes 1622024 | tf_op jit(solution)/shard_map/ppermute | solution.py:221
  26.0 1.9 %copy-start.1 = (bf16[1,384,4096]{2,1,0:T(8,128)(2,1)S(1)}, bf16[1,384,4096]{2,1,0:T(8,128)(2,1)}, u32[]{:S(2)}) copy-start(bf16[1,384,4096]{2,1,0:T(8,128)(2,1)} %gate_hbm.1) | copy-start | bytes 9437188
  27.9 1.9 %copy-start.2 = (bf16[1,384,4096]{2,1,0:T(8,128)(2,1)S(1)}, bf16[1,384,4096]{2,1,0:T(8,128)(2,1)}, u32[]{:S(2)}) copy-start(bf16[1,384,4096]{2,1,0:T(8,128)(2,1)} %up_hbm.1) | copy-start | bytes 9437188
  29.8 1.9 %copy-start.3 = (bf16[1,384,4096]{2,1,0:T(8,128)(2,1)S(1)}, bf16[1,384,4096]{2,1,0:T(8,128)(2,1)}, u32[]{:S(2)}) copy-start(bf16[1,384,4096]{2,1,0:T(8,128)(2,1)} %down_hbm.1) | copy-start | bytes 9437188
  31.7 9.7 %copy-start.5 = (bf16[8,32,128]{2,1,0:T(8,128)(2,1)S(1)}, bf16[8,32,128]{2,1,0:T(8,128)(2,1)}, u32[]{:S(2)}) copy-start(bf16[8,32,128]{2,1,0:T(8,128)(2,1)} %param.12) | copy-start | bytes 196612
  31.7 9.7 %copy-start.6 = (bf16[8,2,128]{2,1,0:T(2,128)(2,1)S(1)}, bf16[8,2,128]{2,1,0:T(2,128)(2,1)}, u32[]{:S(2)}) copy-start(bf16[8,2,128]{2,1,0:T(2,128)(2,1)} %param.15) | copy-start | bytes 12292
  36.8 20.4 %all-to-all-start = ((bf16[32,8,1024]{2,1,0:T(8,128)(2,1)}), bf16[32,8,1024]{2,1,0:T(8,128)(2,1)S(1)}, u32[]{:S(2)}, u32[]{:S(2)}) async-start(bf16[32,8,1024]{2,1,0:T(8,128)(2,1)} %shard_map.131), calls=%async_computation | async-start | bytes 1048576 | tf_op jit(solution)/shard_map/all_to_all | solution.py:230
  57.2 0.8 %copy-start.4 = (bf16[32,8,1024]{2,1,0:T(8,128)(2,1)}, bf16[32,8,1024]{2,1,0:T(8,128)(2,1)S(1)}, u32[]{:S(2)}) copy-start(bf16[32,8,1024]{2,1,0:T(8,128)(2,1)S(1)} %all-to-all-done.got_ref) | copy-start | bytes 1572868

commit v2 on v1

v2 whole, which is shorter than its diff:
```python
import functools

import jax
import jax.numpy as jnp
from jax import lax
from jax.experimental import pallas as pl
from jax.experimental.pallas import tpu as pltpu
from jax.sharding import PartitionSpec as P

BF16 = jnp.bfloat16
F32 = jnp.float32


def attend_local(queries, key_cache, value_cache, new_key, new_value, lengths):
    row_count, head_count, head_size = queries.shape
    kv_heads = key_cache.shape[1]
    cache_len = key_cache.shape[2]
    grouping = head_count // kv_heads
    scaling = head_size ** (-0.5)
    grouped = queries.reshape(row_count, kv_heads, grouping, head_size)
    scores = (
        jnp.einsum("rgqd,rgld->rgql", grouped, key_cache, preferred_element_type=jnp.float32)
        * scaling
    )
    fresh_score = (
        jnp.einsum("rgqd,rgd->rgq", grouped, new_key, preferred_element_type=jnp.float32) * scaling
    )
    valid_mask = (jnp.arange(cache_len)[None, :] < lengths[:, None])[:, None, None, :]
    masked = jnp.where(valid_mask, scores, jnp.float32(-1e30))
    highest = jnp.maximum(jnp.max(masked, axis=-1), fresh_score)
    weights = jnp.where(valid_mask, jnp.exp(masked - highest[..., None]), jnp.float32(0.0))
    fresh_weight = jnp.exp(fresh_score - highest)
    totals = jnp.sum(weights, axis=-1) + fresh_weight
    accumulated = jnp.einsum(
        "rgql,rgld->rgqd",
        weights.astype(jnp.bfloat16),
        value_cache,
        preferred_element_type=jnp.float32,
    )
    accumulated = accumulated + jnp.einsum(
        "rgq,rgd->rgqd",
        fresh_weight.astype(jnp.bfloat16),
        new_value,
        preferred_element_type=jnp.float32,
    )
    return (
        (accumulated / totals[..., None])
        .reshape(row_count, head_count, head_size)
        .astype(jnp.bfloat16)
    )


def dispatch_kernel(capacity, routes_ref, rows_ref, out_ref):
    dev_rows, route_count = routes_ref.shape
    total, piece = out_ref.shape
    pieces = 8 // capacity
    target = lax.broadcasted_iota(jnp.int32, (dev_rows, total), 1)
    named = jnp.zeros((dev_rows, total), jnp.bool_)
    for j in range(route_count):
        named = named | (routes_ref[:, j : j + 1] == target // 8)
    member = jnp.where(named, 1.0, 0.0)
    above = lax.broadcasted_iota(jnp.int32, (dev_rows, dev_rows), 0)
    below = lax.broadcasted_iota(jnp.int32, (dev_rows, dev_rows), 1)
    earlier = jnp.where(below < above, 1.0, 0.0).astype(BF16)
    rank = jnp.dot(earlier, member.astype(BF16), preferred_element_type=F32)
    taken = jnp.where(rank == (target % capacity).astype(F32), member, 0.0)
    cut = target % 8 // capacity
    placing = jnp.concatenate(
        [jnp.where(cut == k, taken, 0.0) for k in range(pieces)], axis=0
    ).astype(BF16)
    rows = jnp.concatenate(
        [rows_ref[:, k * piece : (k + 1) * piece] for k in range(pieces)], axis=0
    )
    contract = (((0,), (0,)), ((), ()))
    out_ref[...] = lax.dot_general(
        placing, rows, contract, preferred_element_type=F32
    ).astype(BF16)


def ffn_kernel(dims, got_ref, gate_hbm, up_hbm, down_hbm, out_ref,
               gate, up, down, gate_sems, up_sems, down_sems):
    capacity, heads, sources = dims
    hidden_size, width = gate.shape
    chunks = gate_sems.shape[0]
    chunk = hidden_size // chunks
    share = width // heads
    pieces = 8 // capacity
    copies = []
    for i in range(chunks):
        part = pl.ds(i * chunk, chunk)
        a = pltpu.make_async_copy(gate_hbm.at[0, part], gate.at[part], gate_sems.at[i])
        b = pltpu.make_async_copy(up_hbm.at[0, part], up.at[part], up_sems.at[i])
        a.start()
        b.start()
        copies.append((a, b))
    down_copies = []
    for h in range(heads):
        part = pl.ds(h * share, share)
        a = pltpu.make_async_copy(down_hbm.at[0, :, part], down.at[:, part], down_sems.at[h])
        a.start()
        down_copies.append(a)

    rows = got_ref[...]
    total, piece = rows.shape
    contract = (((1,), (1,)), ((), ()))

    def project(matrix, part):
        terms = [
            lax.dot_general(
                rows, matrix[part, k * piece : (k + 1) * piece], contract,
                preferred_element_type=F32,
            )
            for k in range(pieces)
        ]
        cut = lax.broadcasted_iota(jnp.int32, terms[0].shape, 0) % 8 // capacity
        result = None
        for j in range(pieces):
            summed = None
            for k in range(pieces):
                shift = (j - k) * capacity % total
                moved = pltpu.roll(terms[k], shift, 0) if shift else terms[k]
                summed = moved if summed is None else summed + moved
            result = summed if result is None else jnp.where(cut == j, summed, result)
        return result

    parts = []
    for i in range(chunks):
        part = pl.ds(i * chunk, chunk)
        copies[i][0].wait()
        gate_part = project(gate, part)
        copies[i][1].wait()
        up_part = project(up, part)
        parts.append((gate_part / (1.0 + jnp.exp(-gate_part)) * up_part).astype(BF16))
    hidden = jnp.concatenate(parts, axis=1)

    width_out = share // pieces
    cut = lax.broadcasted_iota(jnp.int32, (total, width_out), 0) % 8 // capacity
    for h in range(heads):
        down_copies[h].wait()
        packed = None
        for k in range(pieces):
            start = h * share + k * width_out
            result = jnp.dot(
                hidden, down[:, start : start + width_out], preferred_element_type=F32
            )
            packed = result if packed is None else jnp.where(cut == k, result, packed)
        packed = packed.astype(BF16)
        for q in range(sources):
            out_ref[q * heads + h] = packed[q * 8 : q * 8 + 8]


def expert_block(got, gate_matrix, up_matrix, down_matrix, capacity, heads):
    sources = got.shape[0]
    hidden_size, width = gate_matrix.shape[1:]
    chunks = max(1, hidden_size // 128)
    while hidden_size % chunks:
        chunks -= 1
    piece = width // heads * capacity // 8
    return pl.pallas_call(
        functools.partial(ffn_kernel, (capacity, heads, sources)),
        out_shape=jax.ShapeDtypeStruct((sources * heads, 8, piece), BF16),
        in_specs=[
            pl.BlockSpec(memory_space=pltpu.VMEM),
            pl.BlockSpec(memory_space=pl.ANY),
            pl.BlockSpec(memory_space=pl.ANY),
            pl.BlockSpec(memory_space=pl.ANY),
        ],
        out_specs=pl.BlockSpec(memory_space=pltpu.VMEM),
        scratch_shapes=[
            pltpu.VMEM((hidden_size, width), BF16),
            pltpu.VMEM((hidden_size, width), BF16),
            pltpu.VMEM((hidden_size, width), BF16),
            pltpu.SemaphoreType.DMA((chunks,)),
            pltpu.SemaphoreType.DMA((chunks,)),
            pltpu.SemaphoreType.DMA((heads,)),
        ],
        compiler_params=pltpu.CompilerParams(vmem_limit_bytes=58 * 1024 * 1024),
        cost_estimate=pl.CostEstimate(
            flops=2 * sources * 8 * width * hidden_size * 3,
            bytes_accessed=hidden_size * width * 6,
            transcendentals=sources * 8 * hidden_size,
        ),
    )(got.reshape(sources * 8, -1), gate_matrix, up_matrix, down_matrix)


def combine_kernel(pieces, terms, lhs_ref, got_ref, out_ref):
    blocks, rows, piece = got_ref.shape
    got = got_ref[...].reshape(blocks * rows, piece)
    sums = jnp.dot(lhs_ref[...], got, preferred_element_type=F32)
    height = out_ref.shape[0]
    for k in range(pieces):
        total = None
        for t in range(terms):
            start = (k * terms + t) * height
            term = sums[start : start + height]
            total = term if total is None else total + term
        out_ref[:, k * piece : (k + 1) * piece] = total.astype(BF16)


def body(
    queries,
    key_cache,
    value_cache,
    new_key,
    new_value,
    lengths,
    expert_input,
    routes,
    gate_weights,
    gate_matrix,
    up_matrix,
    down_matrix,
):
    dev_rows, route_count = routes.shape
    width = expert_input.shape[1]
    steps, pairs, heads = lax.axis_size("dp"), lax.axis_size("pair"), lax.axis_size("head")
    sources = steps * pairs
    capacity = max(2, dev_rows * route_count // sources)
    pieces = 8 // capacity

    outgoing = pl.pallas_call(
        functools.partial(dispatch_kernel, capacity),
        out_shape=jax.ShapeDtypeStruct((sources * 8, width // pieces), BF16),
        compiler_params=pltpu.CompilerParams(vmem_limit_bytes=8 * 1024 * 1024),
    )(routes, expert_input)
    arrived = lax.all_to_all(
        outgoing.reshape(sources, 8, -1), ("dp", "pair"), split_axis=0, concat_axis=0, tiled=True
    )
    sent = expert_block(arrived, gate_matrix, up_matrix, down_matrix, capacity, heads)
    got = lax.all_to_all(sent, ("dp", "pair", "head"), split_axis=0, concat_axis=0, tiled=True)

    attention = attend_local(queries, key_cache, value_cache, new_key, new_value, lengths)

    named = routes[:, :, None] == jnp.arange(sources)[None, None, :]
    member = jnp.any(named, axis=1)
    coefficient = jnp.sum(jnp.where(named, gate_weights[:, :, None], 0.0), axis=1)
    slot = jnp.cumsum(member.astype(jnp.int32), axis=0) - 1
    terms = []
    rest = coefficient
    for _ in range(3):
        term = lax.reduce_precision(rest, 8, 7)
        terms.append(term)
        rest = rest - term
    terms = jnp.stack(terms)
    place = jnp.arange(8)
    hit = (
        (place[None, None, None, :] // capacity == jnp.arange(pieces)[:, None, None, None])
        & (place[None, None, None, :] % capacity == slot[None, :, :, None])
        & member[None, :, :, None]
    )
    lhs = jnp.where(hit[:, None], terms[None, :, :, :, None], 0.0)
    lhs = jnp.broadcast_to(lhs[:, :, :, :, None, :], lhs.shape[:4] + (heads, 8))
    lhs = lhs.reshape(pieces * 3 * dev_rows, sources * heads * 8).astype(BF16)
    expert_output = pl.pallas_call(
        functools.partial(combine_kernel, pieces, 3),
        out_shape=jax.ShapeDtypeStruct((dev_rows, width // heads), BF16),
        compiler_params=pltpu.CompilerParams(vmem_limit_bytes=8 * 1024 * 1024),
    )(lhs, got)
    return (attention, expert_output)


def solution(mesh):
    placed = (
        P(("groups", "dp", "pair"), "head", None),
        P(("groups", "dp", "pair"), "head", None, None),
        P(("groups", "dp", "pair"), "head", None, None),
        P(("groups", "dp", "pair"), "head", None),
        P(("groups", "dp", "pair"), "head", None),
        P(("groups", "dp", "pair")),
        P(("groups", "dp", "pair"), None),
        P(("groups", "dp", "pair"), None),
        P(("groups", "dp", "pair"), None),
        P(("dp", "pair"), "head", None),
        P(("dp", "pair"), "head", None),
        P(("dp", "pair"), "head", None),
    )
    return jax.shard_map(
        body,
        mesh=mesh,
        in_specs=placed,
        out_specs=(P(("groups", "dp", "pair"), "head", None), P(("groups", "dp", "pair"), "head")),
        check_vma=False,
    )
```

time: 60.4 us -> 53.9 us (0.89)
  local copies, waits for them, and re-layouts: 8.19 us -> 3.14 us
  starting transfers between devices: 15.9 us -> 11.6 us
  waiting for transfers between devices: 20.4 us -> 23.2 us
  Pallas kernels: 7.01 us -> 8.83 us
  other arithmetic: 5.19 us -> 3.6 us
    ppermute x8 -> x0, starting transfers between devices: 11.4 us -> none  [the longest x7 10.3 us: body(): arrived.append(lax.ppermute(block, 'dp', pairs_of))]
    all_to_all x0 -> x1, waiting for transfers between devices: none -> 8.7 us  [body(): lax.all_to_all(outgoing.reshape(sources, 8, -1), ('dp', 'pair'), split_ax...]
    all_to_all x0 -> x1, starting transfers between devices: none -> 7.36 us  [body(): lax.all_to_all(outgoing.reshape(sources, 8, -1), ('dp', 'pair'), split_ax...]
    ppermute x8 -> x0, waiting for transfers between devices: 5.88 us -> none  [the longest x7 5.87 us: body(): arrived.append(lax.ppermute(block, 'dp', pairs_of))]
    unnamed x20 -> x14, local copies, waits for them, and re-layouts: 6.54 us -> 2.37 us
    pallas_call x1 -> x2, Pallas kernels: 5.13 us -> 8.01 us  [the longest x1 6.71 us: expert_block(): pl.pallas_call(functools.partial(ffn_kernel, (capacity, heads, sources)),...]
    pallas_call x1, Pallas kernels: 1.88 us -> 0.82 us  [body(): pl.pallas_call(functools.partial(combine_kernel, pieces, 3), out_shape=ja...]
    concatenate x1 -> x0, other arithmetic: 0.85 us -> none  [body(): block = jnp.concatenate([expert_input, labels], axis=1)]
  transfers between devices with their start and end apart: 9 -> 2, of which waited for: 4 -> 2; matrix products, arithmetic and copies ran while one was open for 13% -> 12% of each run, Pallas kernels for 0% -> 0%
where the time goes in v2:
time: 53.9 us; the launch traced here: 53.4 us
  waiting for transfers between devices  23.2 us (43%)
  starting transfers between devices  11.6 us (22%)
  Pallas kernels  8.83 us (16%)
  other arithmetic  3.6 us (7%)
  local copies, waits for them, and re-layouts  3.14 us (6%)
  matrix products  2.21 us (4%)
  between operations  0.79 us (1%)
    all_to_all x1, waiting for transfers between devices, body(): lax.all_to_all(sent, ('dp', 'pair', 'head'), split_axis=0, concat_axis=0,...  14.5 us
    all_to_all x1, waiting for transfers between devices, body(): lax.all_to_all(outgoing.reshape(sources, 8, -1), ('dp', 'pair'), split_ax...  8.7 us
    all_to_all x1, starting transfers between devices, body(): lax.all_to_all(outgoing.reshape(sources, 8, -1), ('dp', 'pair'), split_ax...  7.36 us
    pallas_call x1, Pallas kernels, expert_block(): pl.pallas_call(functools.partial(ffn_kernel, (capacity, heads, sources)),...  6.71 us
    all_to_all x1, starting transfers between devices, body(): lax.all_to_all(sent, ('dp', 'pair', 'head'), split_axis=0, concat_axis=0,...  4.24 us
    unnamed x14, local copies, waits for them, and re-layouts  2.37 us
    pallas_call x1, Pallas kernels, body(): pl.pallas_call(functools.partial(dispatch_kernel, capacity), out_shape=ja...  1.3 us
    dot_general x1, matrix products, attend_local(): jnp.einsum('rgqd,rgld->rgql', grouped, key_cache, preferred_element_type=...  1.17 us
  transfers between devices with their start and end apart: 2, of which 2 were waited for; matrix products, arithmetic and copies ran while one was open for 12% of the time, Pallas kernels for 0%

profile of v2, /device:TPU:1, one launch (start us, length us, event | category | flops | bytes accessed | tf_op | source)
XLA Modules:
  0.0 53.4 jit_solution(9322542633646216236)
XLA Ops:
  0.6 0.0 copy-start
  0.6 0.0 copy-start.1
  0.7 0.9 %copy-done.1 = bf16[8,4096]{1,0:T(8,128)(2,1)S(1)} copy-done((bf16[8,4096]{1,0:T(8,128)(2,1)S(1)}, bf16[8,4096]{1,0:T(8,128)(2,1)}, u32[]{:S(2)}) %copy-start.1) | copy-done | bytes 65560
  1.5 0.0 copy-start.2
  1.5 0.7 %copy-done.2 = s32[8,8]{1,0:T(8,128)S(1)} copy-done((s32[8,8]{1,0:T(8,128)S(1)}, s32[8,8]{1,0:T(8,128)}, u32[]{:S(2)}) %copy-start.2) | copy-done | bytes 280
  2.2 0.0 copy-start.4
  2.2 1.3 %shard_map.131 = bf16[128,2048]{1,0:T(8,128)(2,1)} custom-call(s32[8,8]{1,0:T(8,128)S(1)} %copy-done.2, bf16[8,4096]{1,0:T(8,128)(2,1)S(1)} %copy-done.1), custom_call_target="tpu_custom_call" | custom-call | tf_op jit(solution)/shard_map/pallas_call | solution.py:221
  3.5 7.4 %all-to-all-start = ((bf16[16,8,2048]{2,1,0:T(8,128)(2,1)}), bf16[16,8,2048]{2,1,0:T(8,128)(2,1)S(1)}, u32[]{:S(2)}, u32[]{:S(2)}) async-start(bf16[16,8,2048]{2,1,0:T(8,128)(2,1)} %bitcast.6), calls=%async_computation | async-start | bytes 1048576 | tf_op jit(solution)/shard_map/all_to_all | solution.py:226
  10.9 0.8 %fusion.9 = pred[8,16]{1,0:T(8,128)(4,1)S(1)} fusion(s32[8,8]{1,0:T(8,128)} %routes_ref.1), kind=kLoop, calls=%fused_computation.16 | loop fusion | flops 1920 | bytes 384 | tf_op jit(solution)/shard_map/reduce_or | solution.py:235
  11.7 0.8 %select_reduce_fusion = f32[8,16]{1,0:T(8,128)S(1)} fusion(f32[8,8]{1,0:T(8,128)} %param.20, s32[8,8]{1,0:T(8,128)} %routes_ref.1), kind=kLoop, calls=%fused_computation.13 | loop fusion | flops 2944 | bytes 1024 | tf_op jit(solution)/shard_map/reduce_sum | solution.py:236
  12.5 0.7 %convert.7 = f32[8,2,128]{2,1,0:T(2,128)S(1)} convert(bf16[8,2,128]{2,1,0:T(2,128)(2,1)} %param.16) | non-fusion elementwise | flops 2048 | bytes 12288 | tf_op jit(solution)/shard_map/convert.1
  13.2 0.1 broadcast_compare_fusion
  13.3 0.1 and_and_fusion
  13.4 0.1 select_convert_fusion
  13.6 0.2 broadcast_in_dim.79
  13.8 0.5 convert_element_type.30.lhs_ref
  14.3 0.7 %iota_compare_fusion.1 = pred[8,64]{1,0:T(8,128)(4,1)S(1)} fusion(s32[8]{0:T(128)} %param.17), kind=kLoop, calls=%fused_computation.26 | loop fusion | flops 512 | bytes 544 | tf_op jit(solution)/shard_map/lt | solution.py:28
  15.1 0.0 copy-done.4
  15.1 1.2 %fusion.15 = (f32[8,2,16]{2,1,0:T(2,128)S(1)}, f32[8,2,16,64]{3,2,1,0:T(8,128)S(1)}) fusion(bf16[8,2,16,128]{3,2,1,0:T(8,128)(2,1)} %bitcast.25, bf16[8,2,64,128]{3,2,1,0:T(8,128)(2,1)S(1)} %copy-done.4, pred[8,64]{1,0:T(8,128)(4,1)S(1)} %iota_compare_fusion.1), kind=kOutput, calls=%fused_computation.37 | convolution fusion | flops 4243200 | bytes 394752 | tf_op jit(solution)/shard_map/rgqd,rgld->rgql/dot_general | solution.py:22
  16.2 8.7 %all-to-all-done = bf16[16,8,2048]{2,1,0:T(8,128)(2,1)S(1)} async-done(((bf16[16,8,2048]{2,1,0:T(8,128)(2,1)}), bf16[16,8,2048]{2,1,0:T(8,128)(2,1)S(1)}, u32[]{:S(2)}, u32[]{:S(2)}) %all-to-all-start) | async-done | bytes 524320 | tf_op jit(solution)/shard_map/all_to_all | solution.py:226
  25.0 0.0 copy-start.3
  25.0 0.8 %copy-done.3 = bf16[16,8,2048]{2,1,0:T(8,128)(2,1)} copy-done((bf16[16,8,2048]{2,1,0:T(8,128)(2,1)}, bf16[16,8,2048]{2,1,0:T(8,128)(2,1)S(1)}, u32[]{:S(2)}) %copy-start.3) | copy-done | bytes 524312
  25.7 0.0 copy-start.5
  25.7 0.0 copy-start.6
  25.7 6.7 %shard_map.132 = bf16[32,8,1024]{2,1,0:T(8,128)(2,1)} custom-call(bf16[128,2048]{1,0:T(8,128)(2,1)} %bitcast.24, bf16[1,384,4096]{2,1,0:T(8,128)(2,1)} %gate_hbm.1, bf16[1,384,4096]{2,1,0:T(8,128)(2,1)} %up_hbm.1, bf16[1,384,4096]{2,1,0:T(8,128)(2,1)} %down_hbm.1), custom_call_target="tpu_custom_call" | custom-call | flops 1207959552 | bytes 9437184 | tf_op jit(solution)/shard_map/pallas_call | solution.py:159
  32.5 4.2 %all-to-all-start.1 = ((bf16[32,8,1024]{2,1,0:T(8,128)(2,1)}), bf16[32,8,1024]{2,1,0:T(8,128)(2,1)S(1)}, u32[]{:S(2)}, u32[]{:S(2)}) async-start(bf16[32,8,1024]{2,1,0:T(8,128)(2,1)} %shard_map.132), calls=%async_computation.1 | async-start | bytes 1048576 | tf_op jit(solution)/shard_map/all_to_all | solution.py:230
  36.7 0.0 copy-done.5
  36.7 0.0 copy-done.6
  36.7 0.1 fusion.10
  36.9 0.2 fusion.3
  37.1 0.0 copy-done
  37.2 0.9 %fusion.2 = bf16[8,2,16,128]{3,2,1,0:T(8,128)(2,1)} fusion(bf16[8,2,64,128]{3,2,1,0:T(8,128)(2,1)S(1)} %copy-done, f32[8,2,16,64]{3,2,1,0:T(8,128)S(1)} %get-tuple-element.8, f32[8,2,16]{2,1,0:T(2,128)S(1)} %get-tuple-element.3, f32[8,2,128]{2,1,0:T(2,128)S(1)} %convert.7, f32[8,2,16]{2,1,0:T(2,128)S(1)} %get-tuple-element.2, ...), kind=kOutput, calls=%fused_computation.4 | convolution fusion | flops 4374528 | bytes 404992 | tf_op jit(solution)/shard_map/rgql,rgld->rgqd/dot_general | solution.py:34
  38.1 14.5 %all-to-all-done.1.got_ref = bf16[32,8,1024]{2,1,0:T(8,128)(2,1)S(1)} async-done(((bf16[32,8,1024]{2,1,0:T(8,128)(2,1)}), bf16[32,8,1024]{2,1,0:T(8,128)(2,1)S(1)}, u32[]{:S(2)}, u32[]{:S(2)}) %all-to-all-start.1) | async-done | bytes 524320 | tf_op jit(solution)/shard_map/all_to_all | solution.py:230
  52.5 0.8 %shard_map.133 = bf16[8,2048]{1,0:T(8,128)(2,1)} custom-call(bf16[48,256]{1,0:T(8,128)(2,1)S(1)} %convert_element_type.30.lhs_ref, bf16[32,8,1024]{2,1,0:T(8,128)(2,1)S(1)} %all-to-all-done.1.got_ref), custom_call_target="tpu_custom_call" | custom-call | tf_op jit(solution)/shard_map/pallas_call | solution.py:254
  (10 shorter events, 0.1 us)
Async XLA Ops:
  0.6 36.5 %copy-start = (bf16[8,2,64,128]{3,2,1,0:T(8,128)(2,1)S(1)}, bf16[8,2,64,128]{3,2,1,0:T(8,128)(2,1)}, u32[]{:S(2)}) copy-start(bf16[8,2,64,128]{3,2,1,0:T(8,128)(2,1)} %param.14) | copy-start | bytes 786436
  0.6 0.9 %copy-start.1 = (bf16[8,4096]{1,0:T(8,128)(2,1)S(1)}, bf16[8,4096]{1,0:T(8,128)(2,1)}, u32[]{:S(2)}) copy-start(bf16[8,4096]{1,0:T(8,128)(2,1)} %rows_ref.1) | copy-start | bytes 196612
  1.5 0.7 %copy-start.2 = (s32[8,8]{1,0:T(8,128)S(1)}, s32[8,8]{1,0:T(8,128)}, u32[]{:S(2)}) copy-start(s32[8,8]{1,0:T(8,128)} %routes_ref.1) | copy-start | bytes 772
  2.2 12.9 %copy-start.4 = (bf16[8,2,64,128]{3,2,1,0:T(8,128)(2,1)S(1)}, bf16[8,2,64,128]{3,2,1,0:T(8,128)(2,1)}, u32[]{:S(2)}) copy-start(bf16[8,2,64,128]{3,2,1,0:T(8,128)(2,1)} %param.13) | copy-start | bytes 786436
  3.5 21.4 %all-to-all-start = ((bf16[16,8,2048]{2,1,0:T(8,128)(2,1)}), bf16[16,8,2048]{2,1,0:T(8,128)(2,1)S(1)}, u32[]{:S(2)}, u32[]{:S(2)}) async-start(bf16[16,8,2048]{2,1,0:T(8,128)(2,1)} %bitcast.6), calls=%async_computation | async-start | bytes 1048576 | tf_op jit(solution)/shard_map/all_to_all | solution.py:226
  25.0 0.8 %copy-start.3 = (bf16[16,8,2048]{2,1,0:T(8,128)(2,1)}, bf16[16,8,2048]{2,1,0:T(8,128)(2,1)S(1)}, u32[]{:S(2)}) copy-start(bf16[16,8,2048]{2,1,0:T(8,128)(2,1)S(1)} %all-to-all-done) | copy-start | bytes 1572868
  25.7 11.0 %copy-start.5 = (bf16[8,32,128]{2,1,0:T(8,128)(2,1)S(1)}, bf16[8,32,128]{2,1,0:T(8,128)(2,1)}, u32[]{:S(2)}) copy-start(bf16[8,32,128]{2,1,0:T(8,128)(2,1)} %param.12) | copy-start | bytes 196612
  25.7 11.0 %copy-start.6 = (bf16[8,2,128]{2,1,0:T(2,128)(2,1)S(1)}, bf16[8,2,128]{2,1,0:T(2,128)(2,1)}, u32[]{:S(2)}) copy-start(bf16[8,2,128]{2,1,0:T(2,128)(2,1)} %param.15) | copy-start | bytes 12292
  32.5 20.1 %all-to-all-start.1 = ((bf16[32,8,1024]{2,1,0:T(8,128)(2,1)}), bf16[32,8,1024]{2,1,0:T(8,128)(2,1)S(1)}, u32[]{:S(2)}, u32[]{:S(2)}) async-start(bf16[32,8,1024]{2,1,0:T(8,128)(2,1)} %shard_map.132), calls=%async_computation.1 | async-start | bytes 1048576 | tf_op jit(solution)/shard_map/all_to_all | solution.py:230

commit v3 on v0

v3 whole, which is shorter than its diff:
```python
import functools

import jax
import jax.numpy as jnp
from jax import lax
from jax.experimental import pallas as pl
from jax.experimental.pallas import tpu as pltpu
from jax.sharding import PartitionSpec as P

LANES = 128
BF16 = jnp.bfloat16
F32 = jnp.float32


def attend_kernel(capacity, heads, lengths_ref, queries_ref, keys_ref, values_ref, new_key_ref,
                  new_value_ref, routes_ref, weights_ref, out_ref, lhs_ref):
    row_count, head_count, head_size = queries_ref.shape
    kv_heads, cache_len = keys_ref.shape[1:3]
    grouping = head_count // kv_heads
    scaling = head_size ** (-0.5)
    contract = (((1,), (1,)), ((), ()))
    spans = [
        (r, g, slice(g * grouping, (g + 1) * grouping))
        for r in range(row_count)
        for g in range(kv_heads)
    ]
    scores, fresh, valid = [], [], []
    position = lax.broadcasted_iota(jnp.int32, (grouping, cache_len), 1)
    for r, g, part in spans:
        query = queries_ref[r, part]
        scores.append(
            lax.dot_general(query, keys_ref[r, g], contract, preferred_element_type=F32)
        )
        fresh.append(
            jnp.sum(
                query.astype(F32) * new_key_ref[r, g : g + 1].astype(F32), axis=1, keepdims=True
            )
        )
        valid.append(position < lengths_ref[r])
    fresh = jnp.concatenate(fresh, axis=0) * scaling
    scores = jnp.concatenate(
        [jnp.where(v, t * scaling, -1e30) for v, t in zip(valid, scores)], axis=0
    )
    highest = jnp.maximum(jnp.max(scores, axis=1, keepdims=True), fresh)
    weights = jnp.concatenate(
        [
            jnp.where(v, jnp.exp(scores[i * grouping : (i + 1) * grouping]
                                 - highest[i * grouping : (i + 1) * grouping]), 0.0)
            for i, v in enumerate(valid)
        ],
        axis=0,
    )
    fresh_weight = jnp.exp(fresh - highest)
    inverse = 1.0 / (jnp.sum(weights, axis=1, keepdims=True) + fresh_weight)
    rounded = weights.astype(BF16)
    fresh_rounded = fresh_weight.astype(BF16).astype(F32)
    for i, (r, g, part) in enumerate(spans):
        here = slice(i * grouping, (i + 1) * grouping)
        summed = jnp.dot(rounded[here], values_ref[r, g], preferred_element_type=F32)
        summed = summed + fresh_rounded[here] * new_value_ref[r, g : g + 1].astype(F32)
        out_ref[r, part] = (summed * inverse[here]).astype(BF16)

    dev_rows, route_count = routes_ref.shape
    total = lhs_ref.shape[1]
    lane = lax.broadcasted_iota(jnp.int32, (dev_rows, total), 1)
    expert = lane // (8 * heads)
    member = jnp.zeros((dev_rows, total), F32)
    rest = jnp.zeros((dev_rows, total), F32)
    for j in range(route_count):
        named = routes_ref[:, j : j + 1] == expert
        member = jnp.where(named, 1.0, member)
        rest = jnp.where(named, weights_ref[:, j : j + 1], rest)
    above = lax.broadcasted_iota(jnp.int32, (dev_rows, dev_rows), 0)
    below = lax.broadcasted_iota(jnp.int32, (dev_rows, dev_rows), 1)
    earlier = jnp.where(below < above, 1.0, 0.0).astype(BF16)
    rank = jnp.dot(earlier, member.astype(BF16), preferred_element_type=F32)
    taken = (member > 0.5) & (rank == (lane % capacity).astype(F32))
    rest = jnp.where(taken, rest, 0.0)
    cut = lane % 8 // capacity
    terms = []
    for _ in range(3):
        term = rest.astype(BF16).astype(F32)
        terms.append(term)
        rest = rest - term
    lhs_ref[...] = jnp.concatenate(
        [jnp.where(cut == k, term, 0.0) for k in range(8 // capacity) for term in terms], axis=0
    ).astype(BF16)


def attend(lengths, queries, key_cache, value_cache, new_key, new_value, routes, gate_weights,
           capacity, heads, sources):
    dev_rows = routes.shape[0]
    vmem = pl.BlockSpec(memory_space=pltpu.VMEM)
    return pl.pallas_call(
        functools.partial(attend_kernel, capacity, heads),
        out_shape=(
            jax.ShapeDtypeStruct(queries.shape, BF16),
            jax.ShapeDtypeStruct((8 // capacity * 3 * dev_rows, sources * heads * 8), BF16),
        ),
        in_specs=[pl.BlockSpec(memory_space=pltpu.SMEM)] + [vmem] * 7,
        out_specs=(vmem, vmem),
        compiler_params=pltpu.CompilerParams(vmem_limit_bytes=16 * 1024 * 1024),
        cost_estimate=pl.CostEstimate(flops=10**9, bytes_accessed=10**6, transcendentals=0),
    )(lengths, queries, key_cache, value_cache, new_key, new_value, routes, gate_weights)


def ffn_kernel(dims, order, place_ref, *refs):
    capacity, heads, route_count, dev_rows = dims
    row_refs, (gate, up, down, out_ref) = refs[:-4], refs[-4:]
    hidden_size, width = gate.shape[1:]
    share = width // heads
    pieces = 8 // capacity
    my_dp, my_pair = place_ref[0], place_ref[1]
    steps = len(order)
    sources = 2 * steps
    rows = sources * dev_rows

    names = jnp.concatenate([ref[:, width:] for ref in row_refs], axis=0)
    lane = lax.broadcasted_iota(jnp.int32, names.shape, 1)
    expert = (2 * my_dp + my_pair).astype(F32)
    named = jnp.where((lane < route_count) & (names.astype(F32) == expert), 1.0, 0.0).astype(BF16)
    member = lax.dot_general(
        jnp.ones((8, names.shape[1]), BF16), named, (((1,), (1,)), ((), ())),
        preferred_element_type=F32,
    )
    above = lax.broadcasted_iota(jnp.int32, (rows, rows), 0)
    below = lax.broadcasted_iota(jnp.int32, (rows, rows), 1)
    earlier = (above < below) & (above // dev_rows == below // dev_rows)
    rank = jnp.dot(
        member.astype(BF16), jnp.where(earlier, 1.0, 0.0).astype(BF16), preferred_element_type=F32
    )
    block = lax.broadcasted_iota(jnp.int32, member.shape, 1) // dev_rows
    step = jnp.zeros(member.shape, jnp.int32)
    for j in range(steps):
        step = jnp.where(block % steps == j, order[j], step)
    home = 2 * (my_dp ^ step) + jnp.where(block < steps, my_pair, 1 - my_pair)
    target = jnp.where(member > 0.5, home * capacity + rank.astype(jnp.int32), -1)
    spot = lax.broadcasted_iota(jnp.int32, (sources * 8, rows), 0)
    spot = spot // 8 * capacity + spot % capacity
    placing = jnp.where(spot == target[0:1], 1.0, 0.0).astype(BF16)

    inputs = jnp.concatenate([ref[:, :width] for ref in row_refs], axis=0)
    contract = (((1,), (1,)), ((), ()))
    chunk = 128 if hidden_size % 128 == 0 else hidden_size
    parts = []
    for start in range(0, hidden_size, chunk):
        part = slice(start, start + chunk)
        gate_part = lax.dot_general(inputs, gate[0, part], contract, preferred_element_type=F32)
        up_part = lax.dot_general(inputs, up[0, part], contract, preferred_element_type=F32)
        parts.append((gate_part / (1.0 + jnp.exp(-gate_part)) * up_part).astype(BF16))
    hidden = jnp.concatenate(parts, axis=1)
    hidden = jnp.dot(placing, hidden, preferred_element_type=F32).astype(BF16)

    piece = share // pieces
    cut = lax.broadcasted_iota(jnp.int32, (sources * 8, piece), 0) % 8 // capacity
    for h in range(heads):
        packed = None
        for k in range(pieces):
            start = h * share + k * piece
            result = jnp.dot(
                hidden, down[0, :, start : start + piece], preferred_element_type=F32
            )
            packed = result if packed is None else jnp.where(cut == k, result, packed)
        packed = packed.astype(BF16)
        for q in range(sources):
            out_ref[q * heads + h] = packed[q * 8 : q * 8 + 8]


def place_kernel(out_ref):
    out_ref[0] = lax.axis_index("dp")
    out_ref[1] = lax.axis_index("pair")


def my_place():
    return pl.pallas_call(
        place_kernel,
        out_shape=jax.ShapeDtypeStruct((2,), jnp.int32),
        out_specs=pl.BlockSpec(memory_space=pltpu.SMEM),
        compiler_params=pltpu.CompilerParams(vmem_limit_bytes=1024 * 1024),
        cost_estimate=pl.CostEstimate(flops=2 * 10**10, bytes_accessed=64, transcendentals=0),
    )()


def expert_block(place, rows, gate_matrix, up_matrix, down_matrix, order, capacity, heads,
                 route_count, dev_rows):
    sources = 2 * len(order)
    hidden_size, width = gate_matrix.shape[1:]
    piece = width // heads * capacity // 8
    vmem = pl.BlockSpec(memory_space=pltpu.VMEM)
    return pl.pallas_call(
        functools.partial(ffn_kernel, (capacity, heads, route_count, dev_rows), order),
        out_shape=jax.ShapeDtypeStruct((sources * heads, 8, piece), BF16),
        in_specs=[pl.BlockSpec(memory_space=pltpu.SMEM)] + [vmem] * (len(rows) + 3),
        out_specs=vmem,
        compiler_params=pltpu.CompilerParams(vmem_limit_bytes=32 * 1024 * 1024),
        cost_estimate=pl.CostEstimate(
            flops=2 * sources * 8 * width * hidden_size * 3,
            bytes_accessed=hidden_size * width * 6,
            transcendentals=sources * 8 * hidden_size,
        ),
    )(place, *rows, gate_matrix, up_matrix, down_matrix)


def combine_kernel(pieces, terms, lhs_ref, got_ref, out_ref):
    blocks, rows, piece = got_ref.shape
    got = got_ref[...].reshape(blocks * rows, piece)
    sums = jnp.dot(lhs_ref[...], got, preferred_element_type=F32)
    height = out_ref.shape[0]
    for k in range(pieces):
        total = None
        for t in range(terms):
            start = (k * terms + t) * height
            term = sums[start : start + height]
            total = term if total is None else total + term
        out_ref[:, k * piece : (k + 1) * piece] = total.astype(BF16)


def body(
    queries,
    key_cache,
    value_cache,
    new_key,
    new_value,
    lengths,
    expert_input,
    routes,
    gate_weights,
    gate_matrix,
    up_matrix,
    down_matrix,
):
    dev_rows, route_count = routes.shape
    width = expert_input.shape[1]
    steps, pairs, heads = lax.axis_size("dp"), lax.axis_size("pair"), lax.axis_size("head")
    sources = steps * pairs
    capacity = max(2, dev_rows * route_count // sources)
    pieces = 8 // capacity

    labels = jnp.pad(routes, ((0, 0), (0, LANES - route_count))).astype(BF16)
    block = jnp.concatenate([expert_input, labels], axis=1)

    def exchange(rows, step):
        return lax.ppermute(rows, "dp", [(i, i ^ step) for i in range(steps)])

    def other_core(rows):
        return lax.ppermute(rows, "pair", [(i, i ^ 1) for i in range(pairs)])

    even = sorted(range(2, steps, 2), reverse=True)
    direct = {step: exchange(block, step) for step in even + [1]}
    far, near = even[: len(even) * 2 // 3], even[len(even) * 2 // 3 :]
    near_rows = jnp.concatenate([direct[step] for step in near], axis=0)
    far_rows = jnp.concatenate([direct[step] for step in far], axis=0)
    near_on, far_on = exchange(near_rows, 1), exchange(far_rows, 1)
    mine = [block, direct[1], near_rows, near_on, far_rows, far_on]
    order = [0, 1] + near + [s ^ 1 for s in near] + far + [s ^ 1 for s in far]
    place = my_place()

    attention, lhs = attend(
        lengths, queries, key_cache, value_cache, new_key, new_value, routes, gate_weights,
        capacity, heads, sources,
    )
    sent = expert_block(
        place, mine + [other_core(rows) for rows in mine], gate_matrix, up_matrix,
        down_matrix, order, capacity, heads, route_count, dev_rows,
    )
    got = lax.all_to_all(sent, ("dp", "pair", "head"), split_axis=0, concat_axis=0, tiled=True)

    expert_output = pl.pallas_call(
        functools.partial(combine_kernel, pieces, 3),
        out_shape=jax.ShapeDtypeStruct((dev_rows, width // heads), BF16),
        compiler_params=pltpu.CompilerParams(vmem_limit_bytes=8 * 1024 * 1024),
    )(lhs, got)
    return (attention, expert_output)


def solution(mesh):
    placed = (
        P(("groups", "dp", "pair"), "head", None),
        P(("groups", "dp", "pair"), "head", None, None),
        P(("groups", "dp", "pair"), "head", None, None),
        P(("groups", "dp", "pair"), "head", None),
        P(("groups", "dp", "pair"), "head", None),
        P(("groups", "dp", "pair")),
        P(("groups", "dp", "pair"), None),
        P(("groups", "dp", "pair"), None),
        P(("groups", "dp", "pair"), None),
        P(("dp", "pair"), "head", None),
        P(("dp", "pair"), "head", None),
        P(("dp", "pair"), "head", None),
    )
    return jax.shard_map(
        body,
        mesh=mesh,
        in_specs=placed,
        out_specs=(P(("groups", "dp", "pair"), "head", None), P(("groups", "dp", "pair"), "head")),
        check_vma=False,
    )
```

time: 97.4 us -> 47.6 us (0.49)
  blocking collectives: 21.5 us -> 0 us
  matrix products: 14 us -> 0 us
  between operations: 14.1 us -> 0.83 us
  starting transfers between devices: 6.25 us -> 16.3 us
  local copies, waits for them, and re-layouts: 9.24 us -> 0.08 us
  Pallas kernels: 0 us -> 7.47 us
  waiting for transfers between devices: 28.1 us -> 21.1 us
  other arithmetic: 2.95 us -> 1.54 us
    all_to_all x1 -> x0, blocking collectives: 21.5 us -> none  [body(): lax.all_to_all(outgoing, ('dp', 'pair'), split_axis=0, concat_axis=0, til...]
    reduce_scatter x1 -> x0, waiting for transfers between devices: 18.4 us -> none  [body(): lax.psum_scatter(partial_value, 'head', scatter_dimension=2, tiled=True)]
    dot_general x8 -> x0, matrix products: 14 us -> none  [the longest x1 3.28 us: expert_block(): lax.dot_general(flattened, gate_matrix[0], contract, preferred_element_ty...]
    ppermute x0 -> x12, starting transfers between devices: none -> 12.3 us  [the longest x6 7.4 us: exchange(): return lax.ppermute(rows, 'dp', [(i, i ^ step) for i in range(steps)])]
    pallas_call x0 -> x4, Pallas kernels: none -> 7.47 us  [the longest x1 4.13 us: expert_block(): pl.pallas_call(functools.partial(ffn_kernel, (capacity, heads, route_coun...]
    ppermute x0 -> x12, waiting for transfers between devices: none -> 7.29 us  [the longest x6 6.65 us: exchange(): return lax.ppermute(rows, 'dp', [(i, i ^ step) for i in range(steps)])]
    reshape x3 -> x0, local copies, waits for them, and re-layouts: 6.01 us -> none  [the longest x1 2.03 us: body(): returned.reshape(slot_total, -1)]
    all_to_all x1, waiting for transfers between devices: 9.6 us -> 13.8 us  [body(): lax.all_to_all(sent, ('dp', 'pair', 'head'), split_axis=0, concat_axis=0,...]
  transfers between devices with their start and end apart: 2 -> 13, of which waited for: 2 -> 6; matrix products, arithmetic and copies ran while one was open for 6% -> 0% of each run, Pallas kernels for 0% -> 5%
where the time goes in v3:
time: 47.6 us; the launch traced here: 47.3 us
  waiting for transfers between devices  21.1 us (44%)
  starting transfers between devices  16.3 us (34%)
  Pallas kernels  7.47 us (16%)
  other arithmetic  1.54 us (3%)
  between operations  0.83 us (2%)
    all_to_all x1, waiting for transfers between devices, body(): lax.all_to_all(sent, ('dp', 'pair', 'head'), split_axis=0, concat_axis=0,...  13.8 us
    ppermute x6, starting transfers between devices, exchange(): return lax.ppermute(rows, 'dp', [(i, i ^ step) for i in range(steps)])  7.4 us
    ppermute x6, waiting for transfers between devices, exchange(): return lax.ppermute(rows, 'dp', [(i, i ^ step) for i in range(steps)])  6.65 us
    ppermute x6, starting transfers between devices, other_core(): return lax.ppermute(rows, 'pair', [(i, i ^ 1) for i in range(pairs)])  4.88 us
    pallas_call x1, Pallas kernels, expert_block(): pl.pallas_call(functools.partial(ffn_kernel, (capacity, heads, route_coun...  4.13 us
    all_to_all x1, starting transfers between devices, body(): lax.all_to_all(sent, ('dp', 'pair', 'head'), split_axis=0, concat_axis=0,...  4.02 us
    pallas_call x1, Pallas kernels, attend(): pl.pallas_call(functools.partial(attend_kernel, capacity, heads), out_sha...  1.93 us
  transfers between devices with their start and end apart: 13, of which 6 were waited for; matrix products, arithmetic and copies ran while one was open for 0% of the time, Pallas kernels for 5%

profile of v3, /device:TPU:1, one launch (start us, length us, event | category | flops | bytes accessed | tf_op | source)
XLA Modules:
  0.0 47.3 jit_solution(15087617292521034440)
XLA Ops:
  0.6 0.7 %convert.4 = bf16[8,8]{1,0:T(8,128)(2,1)S(1)} convert(s32[8,8]{1,0:T(8,128)} %routes_ref.1) | non-fusion elementwise | flops 64 | bytes 384 | tf_op jit(solution)/shard_map/convert
  1.3 0.8 %fusion.1.refs_0_ = bf16[8,4224]{1,0:T(8,128)(2,1)S(1)} fusion(bf16[8,8]{1,0:T(8,128)(2,1)S(1)} %convert.4, bf16[8,4096]{1,0:T(8,128)(2,1)} %param.18), kind=kLoop, calls=%fused_computation.2 | loop fusion | flops 202752 | bytes 133248 | tf_op jit(solution)/shard_map/concatenate | solution.py:240
  2.2 4.2 %collective-permute-start.3 = (bf16[8,4224]{1,0:T(8,128)(2,1)S(1)}, bf16[8,4224]{1,0:T(8,128)(2,1)S(1)}, u32[]{:S(2)}, u32[]{:S(2)}) collective-permute-start(bf16[8,4224]{1,0:T(8,128)(2,1)S(1)} %fusion.1.refs_0_), channel_id=1, source_target_pairs={{0,24},{4,28},{8,16},{12,20},{16,8},{20,12},{24,0},{28,4},{1,25},{... | collective-permute-start | bytes 202760 | tf_op jit(solution)/shard_map/ppermute | solution.py:243
  6.3 0.0 collective-permute-start.4
  6.3 0.4 collective-permute-start.1
  6.7 1.4 %collective-permute-done.3 = bf16[8,4224]{1,0:T(8,128)(2,1)S(1)} collective-permute-done((bf16[8,4224]{1,0:T(8,128)(2,1)S(1)}, bf16[8,4224]{1,0:T(8,128)(2,1)S(1)}, u32[]{:S(2)}, u32[]{:S(2)}) %collective-permute-start.3) | collective-permute-done | bytes 67616 | tf_op jit(solution)/shard_map/ppermute | solution.py:243
  8.0 4.1 %collective-permute-done.4 = bf16[8,4224]{1,0:T(8,128)(2,1)S(1)} collective-permute-done((bf16[8,4224]{1,0:T(8,128)(2,1)S(1)}, bf16[8,4224]{1,0:T(8,128)(2,1)S(1)}, u32[]{:S(2)}, u32[]{:S(2)}) %collective-permute-start.4) | collective-permute-done | bytes 67616 | tf_op jit(solution)/shard_map/ppermute | solution.py:243
  12.1 0.0 copy-start.1
  12.1 0.0 copy-start.2
  12.1 1.6 %collective-permute-start.5 = (bf16[16,4224]{1,0:T(8,128)(2,1)S(1)}, bf16[16,4224]{1,0:T(8,128)(2,1)S(1)}, u32[]{:S(2)}, u32[]{:S(2)}) collective-permute-start(bf16[16,4224]{1,0:T(8,128)(2,1)S(1)} %constant_dynamic-update-slice_fusion.refs_4_), channel_id=1, source_target_pairs={{0,4},{4,0},{8,12},{12,8},{16,20},{20,16},{24,28},{28,24},{1,5},{5... | collective-permute-start | bytes 405512 | tf_op jit(solution)/shard_map/ppermute | solution.py:243
  13.7 0.1 collective-permute-start
  13.8 1.4 %collective-permute-start.6 = (bf16[8,4224]{1,0:T(8,128)(2,1)S(1)}, bf16[8,4224]{1,0:T(8,128)(2,1)S(1)}, u32[]{:S(2)}, u32[]{:S(2)}) collective-permute-start(bf16[8,4224]{1,0:T(8,128)(2,1)S(1)} %fusion.1.refs_0_), channel_id=1, source_target_pairs={{0,1},{1,0},{2,3},{3,2},{4,5},{5,4},{6,7},{7,6},{8,9},{9,8},{10,11... | collective-permute-start | bytes 202760 | tf_op jit(solution)/shard_map/ppermute | solution.py:246
  15.2 0.0 collective-permute-done.1.refs_2_
  15.2 1.2 %collective-permute-start.2 = (bf16[8,4224]{1,0:T(8,128)(2,1)S(1)}, bf16[8,4224]{1,0:T(8,128)(2,1)S(1)}, u32[]{:S(2)}, u32[]{:S(2)}) collective-permute-start(bf16[8,4224]{1,0:T(8,128)(2,1)S(1)} %collective-permute-done.1.refs_2_), channel_id=1, source_target_pairs={{0,4},{4,0},{8,12},{12,8},{16,20},{20,16},{24,28},{28,24},{1,5},{5... | collective-permute-start | bytes 202760 | tf_op jit(solution)/shard_map/ppermute | solution.py:243
  16.4 0.3 collective-permute-start.10
  16.7 1.2 %collective-permute-done.refs_1_ = bf16[8,4224]{1,0:T(8,128)(2,1)S(1)} collective-permute-done((bf16[8,4224]{1,0:T(8,128)(2,1)S(1)}, bf16[8,4224]{1,0:T(8,128)(2,1)S(1)}, u32[]{:S(2)}, u32[]{:S(2)}) %collective-permute-start) | collective-permute-done | bytes 67616 | tf_op jit(solution)/shard_map/ppermute | solution.py:243
  17.9 2.5 %collective-permute-start.8 = (bf16[8,4224]{1,0:T(8,128)(2,1)S(1)}, bf16[8,4224]{1,0:T(8,128)(2,1)S(1)}, u32[]{:S(2)}, u32[]{:S(2)}) collective-permute-start(bf16[8,4224]{1,0:T(8,128)(2,1)S(1)} %collective-permute-done.1.refs_2_), channel_id=1, source_target_pairs={{0,1},{1,0},{2,3},{3,2},{4,5},{5,4},{6,7},{7,6},{8,9},{9,8},{10,11... | collective-permute-start | bytes 202760 | tf_op jit(solution)/shard_map/ppermute | solution.py:246
  20.4 0.0 collective-permute-done.6.refs_6_
  20.4 0.0 collective-permute-start.7
  20.4 0.0 collective-permute-done.2.refs_3_
  20.4 0.7 %collective-permute-start.9 = (bf16[8,4224]{1,0:T(8,128)(2,1)S(1)}, bf16[8,4224]{1,0:T(8,128)(2,1)S(1)}, u32[]{:S(2)}, u32[]{:S(2)}) collective-permute-start(bf16[8,4224]{1,0:T(8,128)(2,1)S(1)} %collective-permute-done.2.refs_3_), channel_id=1, source_target_pairs={{0,1},{1,0},{2,3},{3,2},{4,5},{5,4},{6,7},{7,6},{8,9},{9,8},{10,11... | collective-permute-start | bytes 202760 | tf_op jit(solution)/shard_map/ppermute | solution.py:246
  21.2 0.0 collective-permute-done.5.refs_5_
  21.2 0.0 collective-permute-start.11
  21.2 0.6 %shard_map.132.place_ref = s32[2]{0:T(128)S(1)} custom-call(), custom_call_target="tpu_custom_call" | custom-call | flops 20000000000 | bytes 64 | tf_op jit(solution)/shard_map/pallas_call | solution.py:175
  21.8 0.0 copy-start.3
  21.8 0.0 copy-start.4
  21.8 0.0 copy-start.5
  21.8 0.0 copy-start.6
  21.8 0.0 copy-start.7
  21.8 0.0 copy-start.8
  21.8 0.0 copy-start.9
  21.8 0.0 copy-start.10
  21.9 0.0 collective-permute-done.8.refs_8_
  21.9 0.0 collective-permute-done.7.refs_7_
  21.9 0.0 collective-permute-done.10.refs_10_
  21.9 0.2 collective-permute-done.9.refs_9_
  22.1 0.5 collective-permute-done.11.refs_11_
  22.5 0.0 copy-done
  22.5 0.0 copy-done.1
  22.5 0.0 copy-done.2
  22.5 4.1 %shard_map.133 = bf16[32,8,1024]{2,1,0:T(8,128)(2,1)} custom-call(s32[2]{0:T(128)S(1)} %shard_map.132.place_ref, bf16[8,4224]{1,0:T(8,128)(2,1)S(1)} %fusion.1.refs_0_, bf16[8,4224]{1,0:T(8,128)(2,1)S(1)} %collective-permute-done.refs_1_, bf16[8,4224]{1,0:T(8,128)(2,1)S(1)} %collective-permute-done.1.refs_2_, ...), custom_call_target="tpu_custom_call" | custom-call | flops 1207959552 | bytes 9437184 | tf_op jit(solution)/shard_map/pallas_call | solution.py:190
  26.6 4.0 %all-to-all-start = ((bf16[32,8,1024]{2,1,0:T(8,128)(2,1)}), bf16[32,8,1024]{2,1,0:T(8,128)(2,1)S(1)}, u32[]{:S(2)}, u32[]{:S(2)}) async-start(bf16[32,8,1024]{2,1,0:T(8,128)(2,1)} %shard_map.133), calls=%async_computation | async-start | bytes 1048576 | tf_op jit(solution)/shard_map/all_to_all | solution.py:266
  30.7 0.0 copy-done.3
  30.7 0.0 copy-done.4
  30.7 0.0 copy-done.5
  30.8 1.9 %shard_map.131 = (bf16[8,32,128]{2,1,0:T(8,128)(2,1)}, bf16[48,256]{1,0:T(8,128)(2,1)S(1)}) custom-call(s32[8]{0:T(128)S(1)} %copy-done.10, bf16[8,32,128]{2,1,0:T(8,128)(2,1)S(1)} %copy-done.6, bf16[8,2,64,128]{3,2,1,0:T(8,128)(2,1)S(1)} %copy-done.4, bf16[8,2,64,128]{3,2,1,0:T(8,128)(2,1)S(1)} %copy-done.5, bf16[8,2,128]{2,1,0:T(2,128)(2,1)S(1)} %copy-done.7, ...), custom_call_target="tpu_custom_call" | custom-call | flops 1000000000 | bytes 1000000 | tf_op jit(solution)/shard_map/pallas_call | solution.py:94
  32.7 13.8 %all-to-all-done.got_ref = bf16[32,8,1024]{2,1,0:T(8,128)(2,1)S(1)} async-done(((bf16[32,8,1024]{2,1,0:T(8,128)(2,1)}), bf16[32,8,1024]{2,1,0:T(8,128)(2,1)S(1)}, u32[]{:S(2)}, u32[]{:S(2)}) %all-to-all-start) | async-done | bytes 524320 | tf_op jit(solution)/shard_map/all_to_all | solution.py:266
  46.5 0.8 %shard_map.134 = bf16[8,2048]{1,0:T(8,128)(2,1)} custom-call(bf16[48,256]{1,0:T(8,128)(2,1)S(1)} %get-tuple-element.5.lhs_ref, bf16[32,8,1024]{2,1,0:T(8,128)(2,1)S(1)} %all-to-all-done.got_ref), custom_call_target="tpu_custom_call" | custom-call | tf_op jit(solution)/shard_map/pallas_call | solution.py:268
  (8 shorter events, 0.0 us)
Async XLA Ops:
  2.2 5.9 %collective-permute-start.3 = (bf16[8,4224]{1,0:T(8,128)(2,1)S(1)}, bf16[8,4224]{1,0:T(8,128)(2,1)S(1)}, u32[]{:S(2)}, u32[]{:S(2)}) collective-permute-start(bf16[8,4224]{1,0:T(8,128)(2,1)S(1)} %fusion.1.refs_0_), channel_id=1, source_target_pairs={{0,24},{4,28},{8,16},{12,20},{16,8},{20,12},{24,0},{28,4},{1,25},{... | collective-permute-start | bytes 202760 | tf_op jit(solution)/shard_map/ppermute | solution.py:243
  6.3 5.8 %collective-permute-start.4 = (bf16[8,4224]{1,0:T(8,128)(2,1)S(1)}, bf16[8,4224]{1,0:T(8,128)(2,1)S(1)}, u32[]{:S(2)}, u32[]{:S(2)}) collective-permute-start(bf16[8,4224]{1,0:T(8,128)(2,1)S(1)} %fusion.1.refs_0_), channel_id=1, source_target_pairs={{0,16},{4,20},{8,24},{12,28},{16,0},{20,4},{24,8},{28,12},{1,17},{... | collective-permute-start | bytes 202760 | tf_op jit(solution)/shard_map/ppermute | solution.py:243
  6.3 8.8 %collective-permute-start.1 = (bf16[8,4224]{1,0:T(8,128)(2,1)S(1)}, bf16[8,4224]{1,0:T(8,128)(2,1)S(1)}, u32[]{:S(2)}, u32[]{:S(2)}) collective-permute-start(bf16[8,4224]{1,0:T(8,128)(2,1)S(1)} %fusion.1.refs_0_), channel_id=1, source_target_pairs={{0,8},{4,12},{8,0},{12,4},{16,24},{20,28},{24,16},{28,20},{1,9},{5... | collective-permute-start | bytes 202760 | tf_op jit(solution)/shard_map/ppermute | solution.py:243
  12.1 10.4 %copy-start = (bf16[1,384,4096]{2,1,0:T(8,128)(2,1)S(1)}, bf16[1,384,4096]{2,1,0:T(8,128)(2,1)}, u32[]{:S(2)}) copy-start(bf16[1,384,4096]{2,1,0:T(8,128)(2,1)} %refs_12_.1) | copy-start | bytes 9437188
  12.1 10.4 %copy-start.1 = (bf16[1,384,4096]{2,1,0:T(8,128)(2,1)S(1)}, bf16[1,384,4096]{2,1,0:T(8,128)(2,1)}, u32[]{:S(2)}) copy-start(bf16[1,384,4096]{2,1,0:T(8,128)(2,1)} %refs_13_.1) | copy-start | bytes 9437188
  12.1 10.4 %copy-start.2 = (bf16[1,384,4096]{2,1,0:T(8,128)(2,1)S(1)}, bf16[1,384,4096]{2,1,0:T(8,128)(2,1)}, u32[]{:S(2)}) copy-start(bf16[1,384,4096]{2,1,0:T(8,128)(2,1)} %refs_14_.1) | copy-start | bytes 9437188
  12.1 9.0 %collective-permute-start.5 = (bf16[16,4224]{1,0:T(8,128)(2,1)S(1)}, bf16[16,4224]{1,0:T(8,128)(2,1)S(1)}, u32[]{:S(2)}, u32[]{:S(2)}) collective-permute-start(bf16[16,4224]{1,0:T(8,128)(2,1)S(1)} %constant_dynamic-update-slice_fusion.refs_4_), channel_id=1, source_target_pairs={{0,4},{4,0},{8,12},{12,8},{16,20},{20,16},{24,28},{28,24},{1,5},{5... | collective-permute-start | bytes 405512 | tf_op jit(solution)/shard_map/ppermute | solution.py:243
  13.7 4.2 %collective-permute-start = (bf16[8,4224]{1,0:T(8,128)(2,1)S(1)}, bf16[8,4224]{1,0:T(8,128)(2,1)S(1)}, u32[]{:S(2)}, u32[]{:S(2)}) collective-permute-start(bf16[8,4224]{1,0:T(8,128)(2,1)S(1)} %fusion.1.refs_0_), channel_id=1, source_target_pairs={{0,4},{4,0},{8,12},{12,8},{16,20},{20,16},{24,28},{28,24},{1,5},{5... | collective-permute-start | bytes 202760 | tf_op jit(solution)/shard_map/ppermute | solution.py:243
  13.8 6.6 %collective-permute-start.6 = (bf16[8,4224]{1,0:T(8,128)(2,1)S(1)}, bf16[8,4224]{1,0:T(8,128)(2,1)S(1)}, u32[]{:S(2)}, u32[]{:S(2)}) collective-permute-start(bf16[8,4224]{1,0:T(8,128)(2,1)S(1)} %fusion.1.refs_0_), channel_id=1, source_target_pairs={{0,1},{1,0},{2,3},{3,2},{4,5},{5,4},{6,7},{7,6},{8,9},{9,8},{10,11... | collective-permute-start | bytes 202760 | tf_op jit(solution)/shard_map/ppermute | solution.py:246
  15.2 5.3 %collective-permute-start.2 = (bf16[8,4224]{1,0:T(8,128)(2,1)S(1)}, bf16[8,4224]{1,0:T(8,128)(2,1)S(1)}, u32[]{:S(2)}, u32[]{:S(2)}) collective-permute-start(bf16[8,4224]{1,0:T(8,128)(2,1)S(1)} %collective-permute-done.1.refs_2_), channel_id=1, source_target_pairs={{0,4},{4,0},{8,12},{12,8},{16,20},{20,16},{24,28},{28,24},{1,5},{5... | collective-permute-start | bytes 202760 | tf_op jit(solution)/shard_map/ppermute | solution.py:243
  16.4 5.5 %collective-permute-start.10 = (bf16[16,4224]{1,0:T(8,128)(2,1)S(1)}, bf16[16,4224]{1,0:T(8,128)(2,1)S(1)}, u32[]{:S(2)}, u32[]{:S(2)}) collective-permute-start(bf16[16,4224]{1,0:T(8,128)(2,1)S(1)} %constant_dynamic-update-slice_fusion.refs_4_), channel_id=1, source_target_pairs={{0,1},{1,0},{2,3},{3,2},{4,5},{5,4},{6,7},{7,6},{8,9},{9,8},{10,11... | collective-permute-start | bytes 405512 | tf_op jit(solution)/shard_map/ppermute | solution.py:246
  17.9 3.9 %collective-permute-start.8 = (bf16[8,4224]{1,0:T(8,128)(2,1)S(1)}, bf16[8,4224]{1,0:T(8,128)(2,1)S(1)}, u32[]{:S(2)}, u32[]{:S(2)}) collective-permute-start(bf16[8,4224]{1,0:T(8,128)(2,1)S(1)} %collective-permute-done.1.refs_2_), channel_id=1, source_target_pairs={{0,1},{1,0},{2,3},{3,2},{4,5},{5,4},{6,7},{7,6},{8,9},{9,8},{10,11... | collective-permute-start | bytes 202760 | tf_op jit(solution)/shard_map/ppermute | solution.py:246
  20.4 1.4 %collective-permute-start.7 = (bf16[8,4224]{1,0:T(8,128)(2,1)S(1)}, bf16[8,4224]{1,0:T(8,128)(2,1)S(1)}, u32[]{:S(2)}, u32[]{:S(2)}) collective-permute-start(bf16[8,4224]{1,0:T(8,128)(2,1)S(1)} %collective-permute-done.refs_1_), channel_id=1, source_target_pairs={{0,1},{1,0},{2,3},{3,2},{4,5},{5,4},{6,7},{7,6},{8,9},{9,8},{10,11... | collective-permute-start | bytes 202760 | tf_op jit(solution)/shard_map/ppermute | solution.py:246
  20.4 1.6 %collective-permute-start.9 = (bf16[8,4224]{1,0:T(8,128)(2,1)S(1)}, bf16[8,4224]{1,0:T(8,128)(2,1)S(1)}, u32[]{:S(2)}, u32[]{:S(2)}) collective-permute-start(bf16[8,4224]{1,0:T(8,128)(2,1)S(1)} %collective-permute-done.2.refs_3_), channel_id=1, source_target_pairs={{0,1},{1,0},{2,3},{3,2},{4,5},{5,4},{6,7},{7,6},{8,9},{9,8},{10,11... | collective-permute-start | bytes 202760 | tf_op jit(solution)/shard_map/ppermute | solution.py:246
  21.2 1.4 %collective-permute-start.11 = (bf16[16,4224]{1,0:T(8,128)(2,1)S(1)}, bf16[16,4224]{1,0:T(8,128)(2,1)S(1)}, u32[]{:S(2)}, u32[]{:S(2)}) collective-permute-start(bf16[16,4224]{1,0:T(8,128)(2,1)S(1)} %collective-permute-done.5.refs_5_), channel_id=1, source_target_pairs={{0,1},{1,0},{2,3},{3,2},{4,5},{5,4},{6,7},{7,6},{8,9},{9,8},{10,11... | collective-permute-start | bytes 405512 | tf_op jit(solution)/shard_map/ppermute | solution.py:246
  21.8 8.9 %copy-start.3 = (s32[8,8]{1,0:T(8,128)S(1)}, s32[8,8]{1,0:T(8,128)}, u32[]{:S(2)}) copy-start(s32[8,8]{1,0:T(8,128)} %routes_ref.1) | copy-start | bytes 772
  21.8 8.9 %copy-start.4 = (bf16[8,2,64,128]{3,2,1,0:T(8,128)(2,1)S(1)}, bf16[8,2,64,128]{3,2,1,0:T(8,128)(2,1)}, u32[]{:S(2)}) copy-start(bf16[8,2,64,128]{3,2,1,0:T(8,128)(2,1)} %keys_ref.1) | copy-start | bytes 786436
  21.8 8.9 %copy-start.5 = (bf16[8,2,64,128]{3,2,1,0:T(8,128)(2,1)S(1)}, bf16[8,2,64,128]{3,2,1,0:T(8,128)(2,1)}, u32[]{:S(2)}) copy-start(bf16[8,2,64,128]{3,2,1,0:T(8,128)(2,1)} %values_ref.1) | copy-start | bytes 786436
  21.8 8.9 %copy-start.6 = (bf16[8,32,128]{2,1,0:T(8,128)(2,1)S(1)}, bf16[8,32,128]{2,1,0:T(8,128)(2,1)}, u32[]{:S(2)}) copy-start(bf16[8,32,128]{2,1,0:T(8,128)(2,1)} %queries_ref.1) | copy-start | bytes 196612
  21.8 8.9 %copy-start.7 = (bf16[8,2,128]{2,1,0:T(2,128)(2,1)S(1)}, bf16[8,2,128]{2,1,0:T(2,128)(2,1)}, u32[]{:S(2)}) copy-start(bf16[8,2,128]{2,1,0:T(2,128)(2,1)} %new_key_ref.1) | copy-start | bytes 12292
  21.8 8.9 %copy-start.8 = (bf16[8,2,128]{2,1,0:T(2,128)(2,1)S(1)}, bf16[8,2,128]{2,1,0:T(2,128)(2,1)}, u32[]{:S(2)}) copy-start(bf16[8,2,128]{2,1,0:T(2,128)(2,1)} %new_value_ref.1) | copy-start | bytes 12292
  21.8 8.9 %copy-start.9 = (f32[8,8]{1,0:T(8,128)S(1)}, f32[8,8]{1,0:T(8,128)}, u32[]{:S(2)}) copy-start(f32[8,8]{1,0:T(8,128)} %weights_ref.1) | copy-start | bytes 772
  21.8 8.9 %copy-start.10 = (s32[8]{0:T(128)S(1)}, s32[8]{0:T(128)}, u32[]{:S(2)}) copy-start(s32[8]{0:T(128)} %lengths_ref.1) | copy-start | bytes 100
  26.6 19.8 %all-to-all-start = ((bf16[32,8,1024]{2,1,0:T(8,128)(2,1)}), bf16[32,8,1024]{2,1,0:T(8,128)(2,1)S(1)}, u32[]{:S(2)}, u32[]{:S(2)}) async-start(bf16[32,8,1024]{2,1,0:T(8,128)(2,1)} %shard_map.133), calls=%async_computation | async-start | bytes 1048576 | tf_op jit(solution)/shard_map/all_to_all | solution.py:266

commit v4 on v3

--- a/solution.py
+++ b/solution.py
@@ -246,21 +246,22 @@
         return lax.ppermute(rows, "pair", [(i, i ^ 1) for i in range(pairs)])
 
     even = sorted(range(2, steps, 2), reverse=True)
-    direct = {step: exchange(block, step) for step in even + [1]}
-    far, near = even[: len(even) * 2 // 3], even[len(even) * 2 // 3 :]
-    near_rows = jnp.concatenate([direct[step] for step in near], axis=0)
-    far_rows = jnp.concatenate([direct[step] for step in far], axis=0)
-    near_on, far_on = exchange(near_rows, 1), exchange(far_rows, 1)
-    mine = [block, direct[1], near_rows, near_on, far_rows, far_on]
-    order = [0, 1] + near + [s ^ 1 for s in near] + far + [s ^ 1 for s in far]
+    far = even[: len(even) * 2 // 3]
+    near = [s + odd for s in even[len(far) :] for odd in (0, 1)] + [1]
+    direct = {step: exchange(block, step) for step in far + near}
     place = my_place()
+    near_rows = jnp.concatenate([block] + [direct[step] for step in near], axis=0)
+    mine = [near_rows] + [direct[step] for step in far]
+    mine = mine + [exchange(direct[step], 1) for step in far]
+    order = [0] + near + far + [s ^ 1 for s in far]
 
     attention, lhs = attend(
         lengths, queries, key_cache, value_cache, new_key, new_value, routes, gate_weights,
         capacity, heads, sources,
     )
     sent = expert_block(
-        place, mine + [other_core(rows) for rows in mine], gate_matrix, up_matrix,
+        place, mine + [other_core(rows) for rows in mine],
+        gate_matrix, up_matrix,
         down_matrix, order, capacity, heads, route_count, dev_rows,
     )
     got = lax.all_to_all(sent, ("dp", "pair", "head"), split_axis=0, concat_axis=0, tiled=True)

time: 47.6 us -> 45.5 us (0.956)
  waiting for transfers between devices: 21.1 us -> 15.9 us
  starting transfers between devices: 16.3 us -> 18.5 us
  other arithmetic: 1.54 us -> 2.41 us
    ppermute x6 -> x7, waiting for transfers between devices: 6.65 us -> 1.9 us  [exchange(): return lax.ppermute(rows, 'dp', [(i, i ^ step) for i in range(steps)])]
    ppermute x6 -> x7, starting transfers between devices: 7.4 us -> 9.56 us  [exchange(): return lax.ppermute(rows, 'dp', [(i, i ^ step) for i in range(steps)])]
    all_to_all x1, starting transfers between devices: 4.02 us -> 6.03 us  [body(): lax.all_to_all(sent, ('dp', 'pair', 'head'), split_axis=0, concat_axis=0,...]
    ppermute x6 -> x5, starting transfers between devices: 4.88 us -> 2.94 us  [other_core(): return lax.ppermute(rows, 'pair', [(i, i ^ 1) for i in range(pairs)])]
    concatenate x0 -> x1, other arithmetic: none -> 0.87 us  [body(): jnp.concatenate([block] + [direct[step] for step in near], axis=0)]
  transfers between devices with their start and end apart: 13 -> 13, of which waited for: 6 -> 3; matrix products, arithmetic and copies ran while one was open for 0% -> 2% of each run, Pallas kernels for 5% -> 6%
where the time goes in v4:
time: 45.5 us; the launch traced here: 45.2 us
  starting transfers between devices  18.5 us (41%)
  waiting for transfers between devices  15.9 us (35%)
  Pallas kernels  7.45 us (16%)
  other arithmetic  2.41 us (5%)
  between operations  0.84 us (2%)
    all_to_all x1, waiting for transfers between devices, body(): lax.all_to_all(sent, ('dp', 'pair', 'head'), split_axis=0, concat_axis=0,...  13.8 us
    ppermute x7, starting transfers between devices, exchange(): return lax.ppermute(rows, 'dp', [(i, i ^ step) for i in range(steps)])  9.56 us
    all_to_all x1, starting transfers between devices, body(): lax.all_to_all(sent, ('dp', 'pair', 'head'), split_axis=0, concat_axis=0,...  6.03 us
    pallas_call x1, Pallas kernels, expert_block(): pl.pallas_call(functools.partial(ffn_kernel, (capacity, heads, route_coun...  4.11 us
    ppermute x5, starting transfers between devices, other_core(): return lax.ppermute(rows, 'pair', [(i, i ^ 1) for i in range(pairs)])  2.94 us
    pallas_call x1, Pallas kernels, attend(): pl.pallas_call(functools.partial(attend_kernel, capacity, heads), out_sha...  1.93 us
    ppermute x7, waiting for transfers between devices, exchange(): return lax.ppermute(rows, 'dp', [(i, i ^ step) for i in range(steps)])  1.9 us
  transfers between devices with their start and end apart: 13, of which 3 were waited for; matrix products, arithmetic and copies ran while one was open for 2% of the time, Pallas kernels for 6%

profile of v4, /device:TPU:1, one launch (start us, length us, event | category | flops | bytes accessed | tf_op | source)
XLA Modules:
  0.0 45.2 jit_solution(16488010755681471615)
XLA Ops:
  0.6 0.7 %convert.4 = bf16[8,8]{1,0:T(8,128)(2,1)S(1)} convert(s32[8,8]{1,0:T(8,128)} %routes_ref.1) | non-fusion elementwise | flops 64 | bytes 384 | tf_op jit(solution)/shard_map/convert
  1.3 0.8 %pad_maximum_fusion.1 = bf16[8,4224]{1,0:T(8,128)(2,1)S(1)} fusion(bf16[8,128]{1,0:T(8,128)(2,1)S(1)} %pad.5, bf16[8,4096]{1,0:T(8,128)(2,1)} %param.18), kind=kLoop, calls=%fused_computation.1 | loop fusion | flops 135168 | bytes 135168 | tf_op jit(solution)/shard_map/concatenate | solution.py:240
  2.2 4.2 %collective-permute-start.3 = (bf16[8,4224]{1,0:T(8,128)(2,1)S(1)}, bf16[8,4224]{1,0:T(8,128)(2,1)S(1)}, u32[]{:S(2)}, u32[]{:S(2)}) collective-permute-start(bf16[8,4224]{1,0:T(8,128)(2,1)S(1)} %pad_maximum_fusion.1), channel_id=1, source_target_pairs={{0,24},{4,28},{8,16},{12,20},{16,8},{20,12},{24,0},{28,4},{1,25},{... | collective-permute-start | bytes 202760 | tf_op jit(solution)/shard_map/ppermute | solution.py:243
  6.3 0.0 collective-permute-start.4
  6.3 0.3 collective-permute-start
  6.7 2.1 %collective-permute-start.1 = (bf16[8,4224]{1,0:T(8,128)(2,1)S(1)}, bf16[8,4224]{1,0:T(8,128)(2,1)S(1)}, u32[]{:S(2)}, u32[]{:S(2)}) collective-permute-start(bf16[8,4224]{1,0:T(8,128)(2,1)S(1)} %pad_maximum_fusion.1), channel_id=1, source_target_pairs={{0,12},{4,8},{8,4},{12,0},{16,28},{20,24},{24,20},{28,16},{1,13},{... | collective-permute-start | bytes 202760 | tf_op jit(solution)/shard_map/ppermute | solution.py:243
  8.8 0.2 collective-permute-start.2
  9.0 0.0 collective-permute-done.3.refs_1_
  9.0 1.2 %collective-permute-start.5 = (bf16[8,4224]{1,0:T(8,128)(2,1)S(1)}, bf16[8,4224]{1,0:T(8,128)(2,1)S(1)}, u32[]{:S(2)}, u32[]{:S(2)}) collective-permute-start(bf16[8,4224]{1,0:T(8,128)(2,1)S(1)} %collective-permute-done.3.refs_1_), channel_id=1, source_target_pairs={{0,4},{4,0},{8,12},{12,8},{16,20},{20,16},{24,28},{28,24},{1,5},{5... | collective-permute-start | bytes 202760 | tf_op jit(solution)/shard_map/ppermute | solution.py:243
  10.2 1.9 %collective-permute-done.4.refs_2_ = bf16[8,4224]{1,0:T(8,128)(2,1)S(1)} collective-permute-done((bf16[8,4224]{1,0:T(8,128)(2,1)S(1)}, bf16[8,4224]{1,0:T(8,128)(2,1)S(1)}, u32[]{:S(2)}, u32[]{:S(2)}) %collective-permute-start.4) | collective-permute-done | bytes 67616 | tf_op jit(solution)/shard_map/ppermute | solution.py:243
  12.1 1.5 %collective-permute-start.6 = (bf16[8,4224]{1,0:T(8,128)(2,1)S(1)}, bf16[8,4224]{1,0:T(8,128)(2,1)S(1)}, u32[]{:S(2)}, u32[]{:S(2)}) collective-permute-start(bf16[8,4224]{1,0:T(8,128)(2,1)S(1)} %collective-permute-done.4.refs_2_), channel_id=1, source_target_pairs={{0,4},{4,0},{8,12},{12,8},{16,20},{20,16},{24,28},{28,24},{1,5},{5... | collective-permute-start | bytes 202760 | tf_op jit(solution)/shard_map/ppermute | solution.py:243
  13.6 0.0 collective-permute-done
  13.6 0.0 collective-permute-done.1
  13.6 0.0 collective-permute-done.2
  13.6 0.9 %pad_maximum_fusion.refs_0_ = bf16[32,4224]{1,0:T(8,128)(2,1)S(1)} fusion(bf16[8,4224]{1,0:T(8,128)(2,1)S(1)} %collective-permute-done.2, bf16[8,4224]{1,0:T(8,128)(2,1)S(1)} %collective-permute-done.1, bf16[8,4224]{1,0:T(8,128)(2,1)S(1)} %collective-permute-done, bf16[8,128]{1,0:T(8,128)(2,1)S(1)} %pad.5, bf16[8,4096]{1,0:T(8,128)(2,1)} %param.18), kind=kLoop, calls=%fused_computation | loop fusion | flops 1351680 | bytes 540672 | tf_op jit(solution)/shard_map/concatenate | solution.py:253
  14.5 0.0 copy-start
  14.5 0.0 copy-start.1
  14.5 0.0 copy-start.2
  14.5 1.7 %collective-permute-start.7 = (bf16[32,4224]{1,0:T(8,128)(2,1)S(1)}, bf16[32,4224]{1,0:T(8,128)(2,1)S(1)}, u32[]{:S(2)}, u32[]{:S(2)}) collective-permute-start(bf16[32,4224]{1,0:T(8,128)(2,1)S(1)} %pad_maximum_fusion.refs_0_), channel_id=1, source_target_pairs={{0,1},{1,0},{2,3},{3,2},{4,5},{5,4},{6,7},{7,6},{8,9},{9,8},{10,11... | collective-permute-start | bytes 811016 | tf_op jit(solution)/shard_map/ppermute | solution.py:246
  16.3 0.1 collective-permute-start.8
  16.4 0.4 collective-permute-start.9
  16.8 0.0 collective-permute-done.5.refs_3_
  16.8 0.1 collective-permute-start.10
  16.9 0.0 collective-permute-done.6.refs_4_
  16.9 0.6 %collective-permute-start.11 = (bf16[8,4224]{1,0:T(8,128)(2,1)S(1)}, bf16[8,4224]{1,0:T(8,128)(2,1)S(1)}, u32[]{:S(2)}, u32[]{:S(2)}) collective-permute-start(bf16[8,4224]{1,0:T(8,128)(2,1)S(1)} %collective-permute-done.6.refs_4_), channel_id=1, source_target_pairs={{0,1},{1,0},{2,3},{3,2},{4,5},{5,4},{6,7},{7,6},{8,9},{9,8},{10,11... | collective-permute-start | bytes 202760 | tf_op jit(solution)/shard_map/ppermute | solution.py:246
  17.5 0.6 %shard_map.132.place_ref = s32[2]{0:T(128)S(1)} custom-call(), custom_call_target="tpu_custom_call" | custom-call | flops 20000000000 | bytes 64 | tf_op jit(solution)/shard_map/pallas_call | solution.py:175
  18.1 0.0 copy-start.3
  18.1 0.0 copy-start.4
  18.1 0.0 copy-start.5
  18.1 0.0 copy-start.6
  18.1 0.0 copy-start.7
  18.1 0.0 copy-start.8
  18.2 0.0 copy-start.9
  18.2 0.0 copy-start.10
  18.2 0.0 collective-permute-done.8.refs_6_
  18.2 0.0 collective-permute-done.9.refs_7_
  18.2 0.0 collective-permute-done.10.refs_8_
  18.2 0.2 collective-permute-done.11.refs_9_
  18.4 0.0 collective-permute-done.7.refs_5_
  18.4 0.0 copy-done
  18.4 0.0 copy-done.1
  18.4 0.0 copy-done.2
  18.4 4.1 %shard_map.133 = bf16[32,8,1024]{2,1,0:T(8,128)(2,1)} custom-call(s32[2]{0:T(128)S(1)} %shard_map.132.place_ref, bf16[32,4224]{1,0:T(8,128)(2,1)S(1)} %pad_maximum_fusion.refs_0_, bf16[8,4224]{1,0:T(8,128)(2,1)S(1)} %collective-permute-done.3.refs_1_, bf16[8,4224]{1,0:T(8,128)(2,1)S(1)} %collective-permute-done.4.refs_2_, ...), custom_call_target="tpu_custom_call" | custom-call | flops 1207959552 | bytes 9437184 | tf_op jit(solution)/shard_map/pallas_call | solution.py:190
  22.5 6.0 %all-to-all-start = ((bf16[32,8,1024]{2,1,0:T(8,128)(2,1)}), bf16[32,8,1024]{2,1,0:T(8,128)(2,1)S(1)}, u32[]{:S(2)}, u32[]{:S(2)}) async-start(bf16[32,8,1024]{2,1,0:T(8,128)(2,1)} %shard_map.133), calls=%async_computation | async-start | bytes 1048576 | tf_op jit(solution)/shard_map/all_to_all | solution.py:267
  28.5 0.0 copy-done.3
  28.6 1.9 %shard_map.131 = (bf16[8,32,128]{2,1,0:T(8,128)(2,1)}, bf16[48,256]{1,0:T(8,128)(2,1)S(1)}) custom-call(s32[8]{0:T(128)S(1)} %copy-done.10, bf16[8,32,128]{2,1,0:T(8,128)(2,1)S(1)} %copy-done.6, bf16[8,2,64,128]{3,2,1,0:T(8,128)(2,1)S(1)} %copy-done.4, bf16[8,2,64,128]{3,2,1,0:T(8,128)(2,1)S(1)} %copy-done.5, bf16[8,2,128]{2,1,0:T(2,128)(2,1)S(1)} %copy-done.7, ...), custom_call_target="tpu_custom_call" | custom-call | flops 1000000000 | bytes 1000000 | tf_op jit(solution)/shard_map/pallas_call | solution.py:94
  30.6 13.8 %all-to-all-done.got_ref = bf16[32,8,1024]{2,1,0:T(8,128)(2,1)S(1)} async-done(((bf16[32,8,1024]{2,1,0:T(8,128)(2,1)}), bf16[32,8,1024]{2,1,0:T(8,128)(2,1)S(1)}, u32[]{:S(2)}, u32[]{:S(2)}) %all-to-all-start) | async-done | bytes 524320 | tf_op jit(solution)/shard_map/all_to_all | solution.py:267
  44.4 0.8 %shard_map.134 = bf16[8,2048]{1,0:T(8,128)(2,1)} custom-call(bf16[48,256]{1,0:T(8,128)(2,1)S(1)} %get-tuple-element.5.lhs_ref, bf16[32,8,1024]{2,1,0:T(8,128)(2,1)S(1)} %all-to-all-done.got_ref), custom_call_target="tpu_custom_call" | custom-call | tf_op jit(solution)/shard_map/pallas_call | solution.py:269
  (8 shorter events, 0.0 us)
Async XLA Ops:
  2.2 6.8 %collective-permute-start.3 = (bf16[8,4224]{1,0:T(8,128)(2,1)S(1)}, bf16[8,4224]{1,0:T(8,128)(2,1)S(1)}, u32[]{:S(2)}, u32[]{:S(2)}) collective-permute-start(bf16[8,4224]{1,0:T(8,128)(2,1)S(1)} %pad_maximum_fusion.1), channel_id=1, source_target_pairs={{0,24},{4,28},{8,16},{12,20},{16,8},{20,12},{24,0},{28,4},{1,25},{... | collective-permute-start | bytes 202760 | tf_op jit(solution)/shard_map/ppermute | solution.py:243
  6.3 5.8 %collective-permute-start.4 = (bf16[8,4224]{1,0:T(8,128)(2,1)S(1)}, bf16[8,4224]{1,0:T(8,128)(2,1)S(1)}, u32[]{:S(2)}, u32[]{:S(2)}) collective-permute-start(bf16[8,4224]{1,0:T(8,128)(2,1)S(1)} %pad_maximum_fusion.1), channel_id=1, source_target_pairs={{0,16},{4,20},{8,24},{12,28},{16,0},{20,4},{24,8},{28,12},{1,17},{... | collective-permute-start | bytes 202760 | tf_op jit(solution)/shard_map/ppermute | solution.py:243
  6.3 7.3 %collective-permute-start = (bf16[8,4224]{1,0:T(8,128)(2,1)S(1)}, bf16[8,4224]{1,0:T(8,128)(2,1)S(1)}, u32[]{:S(2)}, u32[]{:S(2)}) collective-permute-start(bf16[8,4224]{1,0:T(8,128)(2,1)S(1)} %pad_maximum_fusion.1), channel_id=1, source_target_pairs={{0,8},{4,12},{8,0},{12,4},{16,24},{20,28},{24,16},{28,20},{1,9},{5... | collective-permute-start | bytes 202760 | tf_op jit(solution)/shard_map/ppermute | solution.py:243
  6.7 6.9 %collective-permute-start.1 = (bf16[8,4224]{1,0:T(8,128)(2,1)S(1)}, bf16[8,4224]{1,0:T(8,128)(2,1)S(1)}, u32[]{:S(2)}, u32[]{:S(2)}) collective-permute-start(bf16[8,4224]{1,0:T(8,128)(2,1)S(1)} %pad_maximum_fusion.1), channel_id=1, source_target_pairs={{0,12},{4,8},{8,4},{12,0},{16,28},{20,24},{24,20},{28,16},{1,13},{... | collective-permute-start | bytes 202760 | tf_op jit(solution)/shard_map/ppermute | solution.py:243
  8.8 4.9 %collective-permute-start.2 = (bf16[8,4224]{1,0:T(8,128)(2,1)S(1)}, bf16[8,4224]{1,0:T(8,128)(2,1)S(1)}, u32[]{:S(2)}, u32[]{:S(2)}) collective-permute-start(bf16[8,4224]{1,0:T(8,128)(2,1)S(1)} %pad_maximum_fusion.1), channel_id=1, source_target_pairs={{0,4},{4,0},{8,12},{12,8},{16,20},{20,16},{24,28},{28,24},{1,5},{5... | collective-permute-start | bytes 202760 | tf_op jit(solution)/shard_map/ppermute | solution.py:243
  9.0 7.8 %collective-permute-start.5 = (bf16[8,4224]{1,0:T(8,128)(2,1)S(1)}, bf16[8,4224]{1,0:T(8,128)(2,1)S(1)}, u32[]{:S(2)}, u32[]{:S(2)}) collective-permute-start(bf16[8,4224]{1,0:T(8,128)(2,1)S(1)} %collective-permute-done.3.refs_1_), channel_id=1, source_target_pairs={{0,4},{4,0},{8,12},{12,8},{16,20},{20,16},{24,28},{28,24},{1,5},{5... | collective-permute-start | bytes 202760 | tf_op jit(solution)/shard_map/ppermute | solution.py:243
  12.1 4.8 %collective-permute-start.6 = (bf16[8,4224]{1,0:T(8,128)(2,1)S(1)}, bf16[8,4224]{1,0:T(8,128)(2,1)S(1)}, u32[]{:S(2)}, u32[]{:S(2)}) collective-permute-start(bf16[8,4224]{1,0:T(8,128)(2,1)S(1)} %collective-permute-done.4.refs_2_), channel_id=1, source_target_pairs={{0,4},{4,0},{8,12},{12,8},{16,20},{20,16},{24,28},{28,24},{1,5},{5... | collective-permute-start | bytes 202760 | tf_op jit(solution)/shard_map/ppermute | solution.py:243
  14.5 3.9 %copy-start = (bf16[1,384,4096]{2,1,0:T(8,128)(2,1)S(1)}, bf16[1,384,4096]{2,1,0:T(8,128)(2,1)}, u32[]{:S(2)}) copy-start(bf16[1,384,4096]{2,1,0:T(8,128)(2,1)} %refs_10_.1) | copy-start | bytes 9437188
  14.5 3.9 %copy-start.1 = (bf16[1,384,4096]{2,1,0:T(8,128)(2,1)S(1)}, bf16[1,384,4096]{2,1,0:T(8,128)(2,1)}, u32[]{:S(2)}) copy-start(bf16[1,384,4096]{2,1,0:T(8,128)(2,1)} %refs_11_.1) | copy-start | bytes 9437188
  14.5 3.9 %copy-start.2 = (bf16[1,384,4096]{2,1,0:T(8,128)(2,1)S(1)}, bf16[1,384,4096]{2,1,0:T(8,128)(2,1)}, u32[]{:S(2)}) copy-start(bf16[1,384,4096]{2,1,0:T(8,128)(2,1)} %refs_12_.1) | copy-start | bytes 9437188
  14.5 3.9 %collective-permute-start.7 = (bf16[32,4224]{1,0:T(8,128)(2,1)S(1)}, bf16[32,4224]{1,0:T(8,128)(2,1)S(1)}, u32[]{:S(2)}, u32[]{:S(2)}) collective-permute-start(bf16[32,4224]{1,0:T(8,128)(2,1)S(1)} %pad_maximum_fusion.refs_0_), channel_id=1, source_target_pairs={{0,1},{1,0},{2,3},{3,2},{4,5},{5,4},{6,7},{7,6},{8,9},{9,8},{10,11... | collective-permute-start | bytes 811016 | tf_op jit(solution)/shard_map/ppermute | solution.py:246
  16.3 1.9 %collective-permute-start.8 = (bf16[8,4224]{1,0:T(8,128)(2,1)S(1)}, bf16[8,4224]{1,0:T(8,128)(2,1)S(1)}, u32[]{:S(2)}, u32[]{:S(2)}) collective-permute-start(bf16[8,4224]{1,0:T(8,128)(2,1)S(1)} %collective-permute-done.3.refs_1_), channel_id=1, source_target_pairs={{0,1},{1,0},{2,3},{3,2},{4,5},{5,4},{6,7},{7,6},{8,9},{9,8},{10,11... | collective-permute-start | bytes 202760 | tf_op jit(solution)/shard_map/ppermute | solution.py:246
  16.4 1.8 %collective-permute-start.9 = (bf16[8,4224]{1,0:T(8,128)(2,1)S(1)}, bf16[8,4224]{1,0:T(8,128)(2,1)S(1)}, u32[]{:S(2)}, u32[]{:S(2)}) collective-permute-start(bf16[8,4224]{1,0:T(8,128)(2,1)S(1)} %collective-permute-done.4.refs_2_), channel_id=1, source_target_pairs={{0,1},{1,0},{2,3},{3,2},{4,5},{5,4},{6,7},{7,6},{8,9},{9,8},{10,11... | collective-permute-start | bytes 202760 | tf_op jit(solution)/shard_map/ppermute | solution.py:246
  16.8 1.4 %collective-permute-start.10 = (bf16[8,4224]{1,0:T(8,128)(2,1)S(1)}, bf16[8,4224]{1,0:T(8,128)(2,1)S(1)}, u32[]{:S(2)}, u32[]{:S(2)}) collective-permute-start(bf16[8,4224]{1,0:T(8,128)(2,1)S(1)} %collective-permute-done.5.refs_3_), channel_id=1, source_target_pairs={{0,1},{1,0},{2,3},{3,2},{4,5},{5,4},{6,7},{7,6},{8,9},{9,8},{10,11... | collective-permute-start | bytes 202760 | tf_op jit(solution)/shard_map/ppermute | solution.py:246
  16.9 1.5 %collective-permute-start.11 = (bf16[8,4224]{1,0:T(8,128)(2,1)S(1)}, bf16[8,4224]{1,0:T(8,128)(2,1)S(1)}, u32[]{:S(2)}, u32[]{:S(2)}) collective-permute-start(bf16[8,4224]{1,0:T(8,128)(2,1)S(1)} %collective-permute-done.6.refs_4_), channel_id=1, source_target_pairs={{0,1},{1,0},{2,3},{3,2},{4,5},{5,4},{6,7},{7,6},{8,9},{9,8},{10,11... | collective-permute-start | bytes 202760 | tf_op jit(solution)/shard_map/ppermute | solution.py:246
  18.1 10.5 %copy-start.3 = (s32[8,8]{1,0:T(8,128)S(1)}, s32[8,8]{1,0:T(8,128)}, u32[]{:S(2)}) copy-start(s32[8,8]{1,0:T(8,128)} %routes_ref.1) | copy-start | bytes 772
  18.1 10.5 %copy-start.4 = (bf16[8,2,64,128]{3,2,1,0:T(8,128)(2,1)S(1)}, bf16[8,2,64,128]{3,2,1,0:T(8,128)(2,1)}, u32[]{:S(2)}) copy-start(bf16[8,2,64,128]{3,2,1,0:T(8,128)(2,1)} %keys_ref.1) | copy-start | bytes 786436
  18.1 10.5 %copy-start.5 = (bf16[8,2,64,128]{3,2,1,0:T(8,128)(2,1)S(1)}, bf16[8,2,64,128]{3,2,1,0:T(8,128)(2,1)}, u32[]{:S(2)}) copy-start(bf16[8,2,64,128]{3,2,1,0:T(8,128)(2,1)} %values_ref.1) | copy-start | bytes 786436
  18.1 10.5 %copy-start.6 = (bf16[8,32,128]{2,1,0:T(8,128)(2,1)S(1)}, bf16[8,32,128]{2,1,0:T(8,128)(2,1)}, u32[]{:S(2)}) copy-start(bf16[8,32,128]{2,1,0:T(8,128)(2,1)} %queries_ref.1) | copy-start | bytes 196612
  18.1 10.5 %copy-start.7 = (bf16[8,2,128]{2,1,0:T(2,128)(2,1)S(1)}, bf16[8,2,128]{2,1,0:T(2,128)(2,1)}, u32[]{:S(2)}) copy-start(bf16[8,2,128]{2,1,0:T(2,128)(2,1)} %new_key_ref.1) | copy-start | bytes 12292
  18.1 10.5 %copy-start.8 = (bf16[8,2,128]{2,1,0:T(2,128)(2,1)S(1)}, bf16[8,2,128]{2,1,0:T(2,128)(2,1)}, u32[]{:S(2)}) copy-start(bf16[8,2,128]{2,1,0:T(2,128)(2,1)} %new_value_ref.1) | copy-start | bytes 12292
  18.2 10.5 %copy-start.9 = (f32[8,8]{1,0:T(8,128)S(1)}, f32[8,8]{1,0:T(8,128)}, u32[]{:S(2)}) copy-start(f32[8,8]{1,0:T(8,128)} %weights_ref.1) | copy-start | bytes 772
  18.2 10.4 %copy-start.10 = (s32[8]{0:T(128)S(1)}, s32[8]{0:T(128)}, u32[]{:S(2)}) copy-start(s32[8]{0:T(128)} %lengths_ref.1) | copy-start | bytes 100
  22.5 21.9 %all-to-all-start = ((bf16[32,8,1024]{2,1,0:T(8,128)(2,1)}), bf16[32,8,1024]{2,1,0:T(8,128)(2,1)S(1)}, u32[]{:S(2)}, u32[]{:S(2)}) async-start(bf16[32,8,1024]{2,1,0:T(8,128)(2,1)} %shard_map.133), calls=%async_computation | async-start | bytes 1048576 | tf_op jit(solution)/shard_map/all_to_all | solution.py:267

commit v5 on v4

--- a/solution.py
+++ b/solution.py
@@ -104,40 +104,16 @@
     )(lengths, queries, key_cache, value_cache, new_key, new_value, routes, gate_weights)
 
 
-def ffn_kernel(dims, order, place_ref, *refs):
+def ffn_kernel(dims, order, dp_ref, pair_ref, *refs):
     capacity, heads, route_count, dev_rows = dims
     row_refs, (gate, up, down, out_ref) = refs[:-4], refs[-4:]
     hidden_size, width = gate.shape[1:]
     share = width // heads
     pieces = 8 // capacity
-    my_dp, my_pair = place_ref[0], place_ref[1]
+    my_dp, my_pair = dp_ref[0:1, 0:1], pair_ref[0:1, 0:1]
     steps = len(order)
     sources = 2 * steps
     rows = sources * dev_rows
-
-    names = jnp.concatenate([ref[:, width:] for ref in row_refs], axis=0)
-    lane = lax.broadcasted_iota(jnp.int32, names.shape, 1)
-    expert = (2 * my_dp + my_pair).astype(F32)
-    named = jnp.where((lane < route_count) & (names.astype(F32) == expert), 1.0, 0.0).astype(BF16)
-    member = lax.dot_general(
-        jnp.ones((8, names.shape[1]), BF16), named, (((1,), (1,)), ((), ())),
-        preferred_element_type=F32,
-    )
-    above = lax.broadcasted_iota(jnp.int32, (rows, rows), 0)
-    below = lax.broadcasted_iota(jnp.int32, (rows, rows), 1)
-    earlier = (above < below) & (above // dev_rows == below // dev_rows)
-    rank = jnp.dot(
-        member.astype(BF16), jnp.where(earlier, 1.0, 0.0).astype(BF16), preferred_element_type=F32
-    )
-    block = lax.broadcasted_iota(jnp.int32, member.shape, 1) // dev_rows
-    step = jnp.zeros(member.shape, jnp.int32)
-    for j in range(steps):
-        step = jnp.where(block % steps == j, order[j], step)
-    home = 2 * (my_dp ^ step) + jnp.where(block < steps, my_pair, 1 - my_pair)
-    target = jnp.where(member > 0.5, home * capacity + rank.astype(jnp.int32), -1)
-    spot = lax.broadcasted_iota(jnp.int32, (sources * 8, rows), 0)
-    spot = spot // 8 * capacity + spot % capacity
-    placing = jnp.where(spot == target[0:1], 1.0, 0.0).astype(BF16)
 
     inputs = jnp.concatenate([ref[:, :width] for ref in row_refs], axis=0)
     contract = (((1,), (1,)), ((), ()))
@@ -149,6 +125,29 @@
         up_part = lax.dot_general(inputs, up[0, part], contract, preferred_element_type=F32)
         parts.append((gate_part / (1.0 + jnp.exp(-gate_part)) * up_part).astype(BF16))
     hidden = jnp.concatenate(parts, axis=1)
+    names = jnp.concatenate([ref[:, width:] for ref in row_refs], axis=0)
+    lane = lax.broadcasted_iota(jnp.int32, names.shape, 1)
+    expert = (2 * my_dp + my_pair).astype(F32)
+    named = jnp.where((lane < route_count) & (names.astype(F32) == expert), 1.0, 0.0).astype(BF16)
+    member = lax.dot_general(
+        jnp.ones((8, names.shape[1]), BF16), named, (((1,), (1,)), ((), ())),
+        preferred_element_type=F32,
+    )
+    above = lax.broadcasted_iota(jnp.int32, (rows, rows), 0)
+    below = lax.broadcasted_iota(jnp.int32, (rows, rows), 1)
+    earlier = (above < below) & (above // dev_rows == below // dev_rows)
+    rank = jnp.dot(
+        member.astype(BF16), jnp.where(earlier, 1.0, 0.0).astype(BF16), preferred_element_type=F32
+    )
+    block = lax.broadcasted_iota(jnp.int32, member.shape, 1) // dev_rows
+    step = jnp.zeros(member.shape, jnp.int32)
+    for j in range(steps):
+        step = jnp.where(block % steps == j, order[j], step)
+    home = 2 * (my_dp ^ step) + jnp.where(block < steps, my_pair, 1 - my_pair)
+    target = jnp.where(member > 0.5, home * capacity + rank.astype(jnp.int32), -1)
+    spot = lax.broadcasted_iota(jnp.int32, (sources * 8, rows), 0)
+    spot = spot // 8 * capacity + spot % capacity
+    placing = jnp.where(spot == target[0:1], 1.0, 0.0).astype(BF16)
     hidden = jnp.dot(placing, hidden, preferred_element_type=F32).astype(BF16)
 
     piece = share // pieces
@@ -166,18 +165,16 @@
             out_ref[q * heads + h] = packed[q * 8 : q * 8 + 8]
 
 
-def place_kernel(out_ref):
-    out_ref[0] = lax.axis_index("dp")
-    out_ref[1] = lax.axis_index("pair")
-
-
-def my_place():
+def place_kernel(axis, out_ref):
+    out_ref[...] = jnp.full(out_ref.shape, lax.axis_index(axis), jnp.int32)
+
+
+def my_place(axis, flops):
     return pl.pallas_call(
-        place_kernel,
-        out_shape=jax.ShapeDtypeStruct((2,), jnp.int32),
-        out_specs=pl.BlockSpec(memory_space=pltpu.SMEM),
+        functools.partial(place_kernel, axis),
+        out_shape=jax.ShapeDtypeStruct((8, LANES), jnp.int32),
         compiler_params=pltpu.CompilerParams(vmem_limit_bytes=1024 * 1024),
-        cost_estimate=pl.CostEstimate(flops=2 * 10**10, bytes_accessed=64, transcendentals=0),
+        cost_estimate=pl.CostEstimate(flops=flops, bytes_accessed=64, transcendentals=0),
     )()
 
 
@@ -190,7 +187,7 @@
     return pl.pallas_call(
         functools.partial(ffn_kernel, (capacity, heads, route_count, dev_rows), order),
         out_shape=jax.ShapeDtypeStruct((sources * heads, 8, piece), BF16),
-        in_specs=[pl.BlockSpec(memory_space=pltpu.SMEM)] + [vmem] * (len(rows) + 3),
+        in_specs=[vmem] * (len(rows) + 5),
         out_specs=vmem,
         compiler_params=pltpu.CompilerParams(vmem_limit_bytes=32 * 1024 * 1024),
         cost_estimate=pl.CostEstimate(
@@ -198,7 +195,7 @@
             bytes_accessed=hidden_size * width * 6,
             transcendentals=sources * 8 * hidden_size,
         ),
-    )(place, *rows, gate_matrix, up_matrix, down_matrix)
+    )(*place, *rows, gate_matrix, up_matrix, down_matrix)
 
 
 def combine_kernel(pieces, terms, lhs_ref, got_ref, out_ref):
@@ -236,6 +233,7 @@
     capacity = max(2, dev_rows * route_count // sources)
     pieces = 8 // capacity
 
+    my_pair, routes = lax.optimization_barrier((my_place("pair", 10**10), routes))
     labels = jnp.pad(routes, ((0, 0), (0, LANES - route_count))).astype(BF16)
     block = jnp.concatenate([expert_input, labels], axis=1)
 
@@ -249,7 +247,7 @@
     far = even[: len(even) * 2 // 3]
     near = [s + odd for s in even[len(far) :] for odd in (0, 1)] + [1]
     direct = {step: exchange(block, step) for step in far + near}
-    place = my_place()
+    place = (my_place("dp", 2 * 10**10), my_pair)
     near_rows = jnp.concatenate([block] + [direct[step] for step in near], axis=0)
     mine = [near_rows] + [direct[step] for step in far]
     mine = mine + [exchange(direct[step], 1) for step in far]

time: 45.5 us -> 43.4 us (0.954)
  other arithmetic: 2.41 us -> 0.03 us
  Pallas kernels: 7.45 us -> 6.3 us
  local copies, waits for them, and re-layouts: 0.08 us -> 0.87 us
  waiting for transfers between devices: 15.9 us -> 16.5 us
    concatenate x1, other arithmetic: 0.87 us -> 0.02 us  [body(): jnp.concatenate([block] + [direct[step] for step in near], axis=0)]
    all_to_all x1, starting transfers between devices: 6.03 us -> 5.18 us  [body(): lax.all_to_all(sent, ('dp', 'pair', 'head'), split_axis=0, concat_axis=0,...]
    ppermute x5, starting transfers between devices: 2.94 us -> 3.78 us  [other_core(): return lax.ppermute(rows, 'pair', [(i, i ^ 1) for i in range(pairs)])]
    concatenate x1, other arithmetic: 0.84 us -> 0.01 us  [body(): block = jnp.concatenate([expert_input, labels], axis=1)]
    unnamed x22 -> x24, local copies, waits for them, and re-layouts: 0.07 us -> 0.86 us
    another operation x1, other arithmetic: 0.69 us -> 0.01 us
    ppermute x5, waiting for transfers between devices: 0.19 us -> 0.83 us  [other_core(): return lax.ppermute(rows, 'pair', [(i, i ^ 1) for i in range(pairs)])]
    pallas_call x1 -> x2, Pallas kernels: 0.59 us -> 0.01 us  [my_place(): pl.pallas_call(functools.partial(place_kernel, axis), out_shape=jax.Shape...]
  transfers between devices with their start and end apart: 13 -> 13, of which waited for: 3 -> 4; matrix products, arithmetic and copies ran while one was open for 2% -> 0% of each run, Pallas kernels for 6% -> 4%
where the time goes in v5:
time: 43.4 us; the launch traced here: 43.1 us
  starting transfers between devices  18.5 us (43%)
  waiting for transfers between devices  16.5 us (38%)
  Pallas kernels  6.3 us (15%)
  local copies, waits for them, and re-layouts  0.87 us (2%)
  between operations  0.82 us (2%)
    all_to_all x1, waiting for transfers between devices, body(): lax.all_to_all(sent, ('dp', 'pair', 'head'), split_axis=0, concat_axis=0,...  13.8 us
    ppermute x7, starting transfers between devices, exchange(): return lax.ppermute(rows, 'dp', [(i, i ^ step) for i in range(steps)])  9.56 us
    all_to_all x1, starting transfers between devices, body(): lax.all_to_all(sent, ('dp', 'pair', 'head'), split_axis=0, concat_axis=0,...  5.18 us
    ppermute x5, starting transfers between devices, other_core(): return lax.ppermute(rows, 'pair', [(i, i ^ 1) for i in range(pairs)])  3.78 us
    pallas_call x1, Pallas kernels, expert_block(): pl.pallas_call(functools.partial(ffn_kernel, (capacity, heads, route_coun...  3.54 us
    pallas_call x1, Pallas kernels, attend(): pl.pallas_call(functools.partial(attend_kernel, capacity, heads), out_sha...  1.93 us
    ppermute x7, waiting for transfers between devices, exchange(): return lax.ppermute(rows, 'dp', [(i, i ^ step) for i in range(steps)])  1.9 us
  transfers between devices with their start and end apart: 13, of which 4 were waited for; matrix products, arithmetic and copies ran while one was open for 0% of the time, Pallas kernels for 4%

profile of v5, /device:TPU:1, one launch (start us, length us, event | category | flops | bytes accessed | tf_op | source)
XLA Modules:
  0.0 43.1 jit_solution(14528255489426263926)
XLA Ops:
  0.6 0.0 copy-start.3
  0.6 0.0 copy-start.11
  0.7 0.7 %copy-done.3 = s32[8,8]{1,0:T(8,128)S(1)} copy-done((s32[8,8]{1,0:T(8,128)S(1)}, s32[8,8]{1,0:T(8,128)}, u32[]{:S(2)}) %copy-start.3) | copy-done | bytes 280
  1.3 0.2 copy-done.11
  1.5 4.2 %collective-permute-start.3 = (bf16[8,4224]{1,0:T(8,128)(2,1)S(1)}, bf16[8,4224]{1,0:T(8,128)(2,1)S(1)}, u32[]{:S(2)}, u32[]{:S(2)}) collective-permute-start(bf16[8,4224]{1,0:T(8,128)(2,1)S(1)} %pad_maximum_fusion.1), channel_id=1, source_target_pairs={{0,24},{4,28},{8,16},{12,20},{16,8},{20,12},{24,0},{28,4},{1,25},{... | collective-permute-start | bytes 202760 | tf_op jit(solution)/shard_map/ppermute | solution.py:241
  5.6 0.0 collective-permute-start.4
  5.6 0.4 collective-permute-start
  6.0 2.1 %collective-permute-start.1 = (bf16[8,4224]{1,0:T(8,128)(2,1)S(1)}, bf16[8,4224]{1,0:T(8,128)(2,1)S(1)}, u32[]{:S(2)}, u32[]{:S(2)}) collective-permute-start(bf16[8,4224]{1,0:T(8,128)(2,1)S(1)} %pad_maximum_fusion.1), channel_id=1, source_target_pairs={{0,12},{4,8},{8,4},{12,0},{16,28},{20,24},{24,20},{28,16},{1,13},{... | collective-permute-start | bytes 202760 | tf_op jit(solution)/shard_map/ppermute | solution.py:241
  8.1 0.2 collective-permute-start.2
  8.3 0.0 collective-permute-done.3.refs_1_
  8.3 1.2 %collective-permute-start.5 = (bf16[8,4224]{1,0:T(8,128)(2,1)S(1)}, bf16[8,4224]{1,0:T(8,128)(2,1)S(1)}, u32[]{:S(2)}, u32[]{:S(2)}) collective-permute-start(bf16[8,4224]{1,0:T(8,128)(2,1)S(1)} %collective-permute-done.3.refs_1_), channel_id=1, source_target_pairs={{0,4},{4,0},{8,12},{12,8},{16,20},{20,16},{24,28},{28,24},{1,5},{5... | collective-permute-start | bytes 202760 | tf_op jit(solution)/shard_map/ppermute | solution.py:241
  9.5 1.9 %collective-permute-done.4.refs_2_ = bf16[8,4224]{1,0:T(8,128)(2,1)S(1)} collective-permute-done((bf16[8,4224]{1,0:T(8,128)(2,1)S(1)}, bf16[8,4224]{1,0:T(8,128)(2,1)S(1)}, u32[]{:S(2)}, u32[]{:S(2)}) %collective-permute-start.4) | collective-permute-done | bytes 67616 | tf_op jit(solution)/shard_map/ppermute | solution.py:241
  11.4 1.5 %collective-permute-start.6 = (bf16[8,4224]{1,0:T(8,128)(2,1)S(1)}, bf16[8,4224]{1,0:T(8,128)(2,1)S(1)}, u32[]{:S(2)}, u32[]{:S(2)}) collective-permute-start(bf16[8,4224]{1,0:T(8,128)(2,1)S(1)} %collective-permute-done.4.refs_2_), channel_id=1, source_target_pairs={{0,4},{4,0},{8,12},{12,8},{16,20},{20,16},{24,28},{28,24},{1,5},{5... | collective-permute-start | bytes 202760 | tf_op jit(solution)/shard_map/ppermute | solution.py:241
  12.9 0.0 collective-permute-done
  12.9 0.0 collective-permute-done.1
  12.9 0.0 collective-permute-done.2
  13.0 0.0 copy-start
  13.0 0.0 copy-start.1
  13.0 0.0 copy-start.2
  13.0 1.7 %collective-permute-start.7 = (bf16[32,4224]{1,0:T(8,128)(2,1)S(1)}, bf16[32,4224]{1,0:T(8,128)(2,1)S(1)}, u32[]{:S(2)}, u32[]{:S(2)}) collective-permute-start(bf16[32,4224]{1,0:T(8,128)(2,1)S(1)} %pad_maximum_fusion.refs_0_), channel_id=1, source_target_pairs={{0,1},{1,0},{2,3},{3,2},{4,5},{5,4},{6,7},{7,6},{8,9},{9,8},{10,11... | collective-permute-start | bytes 811016 | tf_op jit(solution)/shard_map/ppermute | solution.py:244
  14.8 0.1 collective-permute-start.8
  14.8 0.4 %collective-permute-start.9 = (bf16[8,4224]{1,0:T(8,128)(2,1)S(1)}, bf16[8,4224]{1,0:T(8,128)(2,1)S(1)}, u32[]{:S(2)}, u32[]{:S(2)}) collective-permute-start(bf16[8,4224]{1,0:T(8,128)(2,1)S(1)} %collective-permute-done.4.refs_2_), channel_id=1, source_target_pairs={{0,1},{1,0},{2,3},{3,2},{4,5},{5,4},{6,7},{7,6},{8,9},{9,8},{10,11... | collective-permute-start | bytes 202760 | tf_op jit(solution)/shard_map/ppermute | solution.py:244
  15.3 0.0 collective-permute-done.5.refs_3_
  15.3 0.8 %collective-permute-start.10 = (bf16[8,4224]{1,0:T(8,128)(2,1)S(1)}, bf16[8,4224]{1,0:T(8,128)(2,1)S(1)}, u32[]{:S(2)}, u32[]{:S(2)}) collective-permute-start(bf16[8,4224]{1,0:T(8,128)(2,1)S(1)} %collective-permute-done.5.refs_3_), channel_id=1, source_target_pairs={{0,1},{1,0},{2,3},{3,2},{4,5},{5,4},{6,7},{7,6},{8,9},{9,8},{10,11... | collective-permute-start | bytes 202760 | tf_op jit(solution)/shard_map/ppermute | solution.py:244
  16.1 0.0 collective-permute-done.6.refs_4_
  16.1 0.7 %collective-permute-start.11 = (bf16[8,4224]{1,0:T(8,128)(2,1)S(1)}, bf16[8,4224]{1,0:T(8,128)(2,1)S(1)}, u32[]{:S(2)}, u32[]{:S(2)}) collective-permute-start(bf16[8,4224]{1,0:T(8,128)(2,1)S(1)} %collective-permute-done.6.refs_4_), channel_id=1, source_target_pairs={{0,1},{1,0},{2,3},{3,2},{4,5},{5,4},{6,7},{7,6},{8,9},{9,8},{10,11... | collective-permute-start | bytes 202760 | tf_op jit(solution)/shard_map/ppermute | solution.py:244
  16.8 0.0 copy-start.7
  16.8 0.0 copy-start.8
  16.8 0.0 copy-start.9
  16.8 0.0 copy-start.10
  16.9 0.0 collective-permute-done.8.refs_6_
  16.9 0.0 collective-permute-done.9.refs_7_
  16.9 0.1 collective-permute-done.10.refs_8_
  17.0 0.7 %collective-permute-done.11.refs_9_ = bf16[8,4224]{1,0:T(8,128)(2,1)S(1)} collective-permute-done((bf16[8,4224]{1,0:T(8,128)(2,1)S(1)}, bf16[8,4224]{1,0:T(8,128)(2,1)S(1)}, u32[]{:S(2)}, u32[]{:S(2)}) %collective-permute-start.11) | collective-permute-done | bytes 67616 | tf_op jit(solution)/shard_map/ppermute | solution.py:244
  17.7 0.0 collective-permute-done.7.refs_5_
  17.7 0.0 copy-done
  17.7 0.0 copy-done.1
  17.7 0.0 copy-done.2
  17.7 3.5 %shard_map.134 = bf16[32,8,1024]{2,1,0:T(8,128)(2,1)} custom-call(s32[8,128]{1,0:T(8,128)S(1)} %shard_map.133.dp_ref, s32[8,128]{1,0:T(8,128)S(1)} %shard_map.131.pair_ref, bf16[32,4224]{1,0:T(8,128)(2,1)S(1)} %pad_maximum_fusion.refs_0_, bf16[8,4224]{1,0:T(8,128)(2,1)S(1)} %collective-permute-done.3.refs_1_, ...), custom_call_target="tpu_custom_call" | custom-call | flops 1207959552 | bytes 9437184 | tf_op jit(solution)/shard_map/pallas_call | solution.py:187
  21.3 5.2 %all-to-all-start = ((bf16[32,8,1024]{2,1,0:T(8,128)(2,1)}), bf16[32,8,1024]{2,1,0:T(8,128)(2,1)S(1)}, u32[]{:S(2)}, u32[]{:S(2)}) async-start(bf16[32,8,1024]{2,1,0:T(8,128)(2,1)} %shard_map.134), calls=%async_computation | async-start | bytes 1048576 | tf_op jit(solution)/shard_map/all_to_all | solution.py:265
  26.4 0.0 copy-done.4
  26.5 0.0 copy-done.5
  26.5 0.0 copy-done.6
  26.5 0.0 copy-done.7
  26.5 0.0 copy-done.8
  26.5 1.9 %shard_map.132 = (bf16[8,32,128]{2,1,0:T(8,128)(2,1)}, bf16[48,256]{1,0:T(8,128)(2,1)S(1)}) custom-call(s32[8]{0:T(128)S(1)} %copy-done.10, bf16[8,32,128]{2,1,0:T(8,128)(2,1)S(1)} %copy-done.6, bf16[8,2,64,128]{3,2,1,0:T(8,128)(2,1)S(1)} %copy-done.4, bf16[8,2,64,128]{3,2,1,0:T(8,128)(2,1)S(1)} %copy-done.5, bf16[8,2,128]{2,1,0:T(2,128)(2,1)S(1)} %copy-done.7, ...), custom_call_target="tpu_custom_call" | custom-call | flops 1000000000 | bytes 1000000 | tf_op jit(solution)/shard_map/pallas_call | solution.py:94
  28.5 13.8 %all-to-all-done.got_ref = bf16[32,8,1024]{2,1,0:T(8,128)(2,1)S(1)} async-done(((bf16[32,8,1024]{2,1,0:T(8,128)(2,1)}), bf16[32,8,1024]{2,1,0:T(8,128)(2,1)S(1)}, u32[]{:S(2)}, u32[]{:S(2)}) %all-to-all-start) | async-done | bytes 524320 | tf_op jit(solution)/shard_map/all_to_all | solution.py:265
  42.3 0.8 %shard_map.135 = bf16[8,2048]{1,0:T(8,128)(2,1)} custom-call(bf16[48,256]{1,0:T(8,128)(2,1)S(1)} %get-tuple-element.8.lhs_ref, bf16[32,8,1024]{2,1,0:T(8,128)(2,1)S(1)} %all-to-all-done.got_ref), custom_call_target="tpu_custom_call" | custom-call | tf_op jit(solution)/shard_map/pallas_call | solution.py:267
  (11 shorter events, 0.1 us)
Async XLA Ops:
  0.6 0.7 %copy-start.3 = (s32[8,8]{1,0:T(8,128)S(1)}, s32[8,8]{1,0:T(8,128)}, u32[]{:S(2)}) copy-start(s32[8,8]{1,0:T(8,128)} %routes_ref) | copy-start | bytes 772
  0.6 0.8 %copy-start.11 = (bf16[8,4096]{1,0:T(8,128)(2,1)S(1)}, bf16[8,4096]{1,0:T(8,128)(2,1)}, u32[]{:S(2)}) copy-start(bf16[8,4096]{1,0:T(8,128)(2,1)} %param.18) | copy-start | bytes 196612
  1.5 6.8 %collective-permute-start.3 = (bf16[8,4224]{1,0:T(8,128)(2,1)S(1)}, bf16[8,4224]{1,0:T(8,128)(2,1)S(1)}, u32[]{:S(2)}, u32[]{:S(2)}) collective-permute-start(bf16[8,4224]{1,0:T(8,128)(2,1)S(1)} %pad_maximum_fusion.1), channel_id=1, source_target_pairs={{0,24},{4,28},{8,16},{12,20},{16,8},{20,12},{24,0},{28,4},{1,25},{... | collective-permute-start | bytes 202760 | tf_op jit(solution)/shard_map/ppermute | solution.py:241
  5.6 5.8 %collective-permute-start.4 = (bf16[8,4224]{1,0:T(8,128)(2,1)S(1)}, bf16[8,4224]{1,0:T(8,128)(2,1)S(1)}, u32[]{:S(2)}, u32[]{:S(2)}) collective-permute-start(bf16[8,4224]{1,0:T(8,128)(2,1)S(1)} %pad_maximum_fusion.1), channel_id=1, source_target_pairs={{0,16},{4,20},{8,24},{12,28},{16,0},{20,4},{24,8},{28,12},{1,17},{... | collective-permute-start | bytes 202760 | tf_op jit(solution)/shard_map/ppermute | solution.py:241
  5.6 7.3 %collective-permute-start = (bf16[8,4224]{1,0:T(8,128)(2,1)S(1)}, bf16[8,4224]{1,0:T(8,128)(2,1)S(1)}, u32[]{:S(2)}, u32[]{:S(2)}) collective-permute-start(bf16[8,4224]{1,0:T(8,128)(2,1)S(1)} %pad_maximum_fusion.1), channel_id=1, source_target_pairs={{0,8},{4,12},{8,0},{12,4},{16,24},{20,28},{24,16},{28,20},{1,9},{5... | collective-permute-start | bytes 202760 | tf_op jit(solution)/shard_map/ppermute | solution.py:241
  6.0 6.9 %collective-permute-start.1 = (bf16[8,4224]{1,0:T(8,128)(2,1)S(1)}, bf16[8,4224]{1,0:T(8,128)(2,1)S(1)}, u32[]{:S(2)}, u32[]{:S(2)}) collective-permute-start(bf16[8,4224]{1,0:T(8,128)(2,1)S(1)} %pad_maximum_fusion.1), channel_id=1, source_target_pairs={{0,12},{4,8},{8,4},{12,0},{16,28},{20,24},{24,20},{28,16},{1,13},{... | collective-permute-start | bytes 202760 | tf_op jit(solution)/shard_map/ppermute | solution.py:241
  8.1 4.9 %collective-permute-start.2 = (bf16[8,4224]{1,0:T(8,128)(2,1)S(1)}, bf16[8,4224]{1,0:T(8,128)(2,1)S(1)}, u32[]{:S(2)}, u32[]{:S(2)}) collective-permute-start(bf16[8,4224]{1,0:T(8,128)(2,1)S(1)} %pad_maximum_fusion.1), channel_id=1, source_target_pairs={{0,4},{4,0},{8,12},{12,8},{16,20},{20,16},{24,28},{28,24},{1,5},{5... | collective-permute-start | bytes 202760 | tf_op jit(solution)/shard_map/ppermute | solution.py:241
  8.3 7.0 %collective-permute-start.5 = (bf16[8,4224]{1,0:T(8,128)(2,1)S(1)}, bf16[8,4224]{1,0:T(8,128)(2,1)S(1)}, u32[]{:S(2)}, u32[]{:S(2)}) collective-permute-start(bf16[8,4224]{1,0:T(8,128)(2,1)S(1)} %collective-permute-done.3.refs_1_), channel_id=1, source_target_pairs={{0,4},{4,0},{8,12},{12,8},{16,20},{20,16},{24,28},{28,24},{1,5},{5... | collective-permute-start | bytes 202760 | tf_op jit(solution)/shard_map/ppermute | solution.py:241
  11.4 4.6 %collective-permute-start.6 = (bf16[8,4224]{1,0:T(8,128)(2,1)S(1)}, bf16[8,4224]{1,0:T(8,128)(2,1)S(1)}, u32[]{:S(2)}, u32[]{:S(2)}) collective-permute-start(bf16[8,4224]{1,0:T(8,128)(2,1)S(1)} %collective-permute-done.4.refs_2_), channel_id=1, source_target_pairs={{0,4},{4,0},{8,12},{12,8},{16,20},{20,16},{24,28},{28,24},{1,5},{5... | collective-permute-start | bytes 202760 | tf_op jit(solution)/shard_map/ppermute | solution.py:241
  13.0 4.7 %copy-start = (bf16[1,384,4096]{2,1,0:T(8,128)(2,1)S(1)}, bf16[1,384,4096]{2,1,0:T(8,128)(2,1)}, u32[]{:S(2)}) copy-start(bf16[1,384,4096]{2,1,0:T(8,128)(2,1)} %refs_10_.1) | copy-start | bytes 9437188
  13.0 4.7 %copy-start.1 = (bf16[1,384,4096]{2,1,0:T(8,128)(2,1)S(1)}, bf16[1,384,4096]{2,1,0:T(8,128)(2,1)}, u32[]{:S(2)}) copy-start(bf16[1,384,4096]{2,1,0:T(8,128)(2,1)} %refs_11_.1) | copy-start | bytes 9437188
  13.0 4.7 %copy-start.2 = (bf16[1,384,4096]{2,1,0:T(8,128)(2,1)S(1)}, bf16[1,384,4096]{2,1,0:T(8,128)(2,1)}, u32[]{:S(2)}) copy-start(bf16[1,384,4096]{2,1,0:T(8,128)(2,1)} %refs_12_.1) | copy-start | bytes 9437188
  13.0 4.7 %collective-permute-start.7 = (bf16[32,4224]{1,0:T(8,128)(2,1)S(1)}, bf16[32,4224]{1,0:T(8,128)(2,1)S(1)}, u32[]{:S(2)}, u32[]{:S(2)}) collective-permute-start(bf16[32,4224]{1,0:T(8,128)(2,1)S(1)} %pad_maximum_fusion.refs_0_), channel_id=1, source_target_pairs={{0,1},{1,0},{2,3},{3,2},{4,5},{5,4},{6,7},{7,6},{8,9},{9,8},{10,11... | collective-permute-start | bytes 811016 | tf_op jit(solution)/shard_map/ppermute | solution.py:244
  14.8 2.1 %collective-permute-start.8 = (bf16[8,4224]{1,0:T(8,128)(2,1)S(1)}, bf16[8,4224]{1,0:T(8,128)(2,1)S(1)}, u32[]{:S(2)}, u32[]{:S(2)}) collective-permute-start(bf16[8,4224]{1,0:T(8,128)(2,1)S(1)} %collective-permute-done.3.refs_1_), channel_id=1, source_target_pairs={{0,1},{1,0},{2,3},{3,2},{4,5},{5,4},{6,7},{7,6},{8,9},{9,8},{10,11... | collective-permute-start | bytes 202760 | tf_op jit(solution)/shard_map/ppermute | solution.py:244
  14.8 2.0 %collective-permute-start.9 = (bf16[8,4224]{1,0:T(8,128)(2,1)S(1)}, bf16[8,4224]{1,0:T(8,128)(2,1)S(1)}, u32[]{:S(2)}, u32[]{:S(2)}) collective-permute-start(bf16[8,4224]{1,0:T(8,128)(2,1)S(1)} %collective-permute-done.4.refs_2_), channel_id=1, source_target_pairs={{0,1},{1,0},{2,3},{3,2},{4,5},{5,4},{6,7},{7,6},{8,9},{9,8},{10,11... | collective-permute-start | bytes 202760 | tf_op jit(solution)/shard_map/ppermute | solution.py:244
  15.3 1.7 %collective-permute-start.10 = (bf16[8,4224]{1,0:T(8,128)(2,1)S(1)}, bf16[8,4224]{1,0:T(8,128)(2,1)S(1)}, u32[]{:S(2)}, u32[]{:S(2)}) collective-permute-start(bf16[8,4224]{1,0:T(8,128)(2,1)S(1)} %collective-permute-done.5.refs_3_), channel_id=1, source_target_pairs={{0,1},{1,0},{2,3},{3,2},{4,5},{5,4},{6,7},{7,6},{8,9},{9,8},{10,11... | collective-permute-start | bytes 202760 | tf_op jit(solution)/shard_map/ppermute | solution.py:244
  16.1 1.6 %collective-permute-start.11 = (bf16[8,4224]{1,0:T(8,128)(2,1)S(1)}, bf16[8,4224]{1,0:T(8,128)(2,1)S(1)}, u32[]{:S(2)}, u32[]{:S(2)}) collective-permute-start(bf16[8,4224]{1,0:T(8,128)(2,1)S(1)} %collective-permute-done.6.refs_4_), channel_id=1, source_target_pairs={{0,1},{1,0},{2,3},{3,2},{4,5},{5,4},{6,7},{7,6},{8,9},{9,8},{10,11... | collective-permute-start | bytes 202760 | tf_op jit(solution)/shard_map/ppermute | solution.py:244
  16.8 9.7 %copy-start.4 = (bf16[8,2,64,128]{3,2,1,0:T(8,128)(2,1)S(1)}, bf16[8,2,64,128]{3,2,1,0:T(8,128)(2,1)}, u32[]{:S(2)}) copy-start(bf16[8,2,64,128]{3,2,1,0:T(8,128)(2,1)} %keys_ref.1) | copy-start | bytes 786436
  16.8 9.7 %copy-start.5 = (bf16[8,2,64,128]{3,2,1,0:T(8,128)(2,1)S(1)}, bf16[8,2,64,128]{3,2,1,0:T(8,128)(2,1)}, u32[]{:S(2)}) copy-start(bf16[8,2,64,128]{3,2,1,0:T(8,128)(2,1)} %values_ref.1) | copy-start | bytes 786436
  16.8 9.7 %copy-start.6 = (bf16[8,32,128]{2,1,0:T(8,128)(2,1)S(1)}, bf16[8,32,128]{2,1,0:T(8,128)(2,1)}, u32[]{:S(2)}) copy-start(bf16[8,32,128]{2,1,0:T(8,128)(2,1)} %queries_ref.1) | copy-start | bytes 196612
  16.8 9.7 %copy-start.7 = (bf16[8,2,128]{2,1,0:T(2,128)(2,1)S(1)}, bf16[8,2,128]{2,1,0:T(2,128)(2,1)}, u32[]{:S(2)}) copy-start(bf16[8,2,128]{2,1,0:T(2,128)(2,1)} %new_key_ref.1) | copy-start | bytes 12292
  16.8 9.7 %copy-start.8 = (bf16[8,2,128]{2,1,0:T(2,128)(2,1)S(1)}, bf16[8,2,128]{2,1,0:T(2,128)(2,1)}, u32[]{:S(2)}) copy-start(bf16[8,2,128]{2,1,0:T(2,128)(2,1)} %new_value_ref.1) | copy-start | bytes 12292
  16.8 9.7 %copy-start.9 = (f32[8,8]{1,0:T(8,128)S(1)}, f32[8,8]{1,0:T(8,128)}, u32[]{:S(2)}) copy-start(f32[8,8]{1,0:T(8,128)} %weights_ref.1) | copy-start | bytes 772
  16.8 9.7 %copy-start.10 = (s32[8]{0:T(128)S(1)}, s32[8]{0:T(128)}, u32[]{:S(2)}) copy-start(s32[8]{0:T(128)} %lengths_ref.1) | copy-start | bytes 100
  21.3 21.0 %all-to-all-start = ((bf16[32,8,1024]{2,1,0:T(8,128)(2,1)}), bf16[32,8,1024]{2,1,0:T(8,128)(2,1)S(1)}, u32[]{:S(2)}, u32[]{:S(2)}) async-start(bf16[32,8,1024]{2,1,0:T(8,128)(2,1)} %shard_map.134), calls=%async_computation | async-start | bytes 1048576 | tf_op jit(solution)/shard_map/all_to_all | solution.py:265

commit v6 on v5

--- a/solution.py
+++ b/solution.py
@@ -250,7 +250,7 @@
     place = (my_place("dp", 2 * 10**10), my_pair)
     near_rows = jnp.concatenate([block] + [direct[step] for step in near], axis=0)
     mine = [near_rows] + [direct[step] for step in far]
-    mine = mine + [exchange(direct[step], 1) for step in far]
+    mine = mine + [exchange(direct[far[0]], 1)] + [exchange(block, step ^ 1) for step in far[1:]]
     order = [0] + near + far + [s ^ 1 for s in far]
 
     attention, lhs = attend(

time: 43.4 us -> 42.9 us (0.988)
  waiting for transfers between devices: 16.5 us -> 15.1 us
  starting transfers between devices: 18.5 us -> 19.5 us
    ppermute x5, starting transfers between devices: 3.78 us -> 7.12 us  [other_core(): return lax.ppermute(rows, 'pair', [(i, i ^ 1) for i in range(pairs)])]
    all_to_all x1, starting transfers between devices: 5.18 us -> 2.94 us  [body(): lax.all_to_all(sent, ('dp', 'pair', 'head'), split_axis=0, concat_axis=0,...]
    ppermute x7, waiting for transfers between devices: 1.9 us -> 0.08 us  [exchange(): return lax.ppermute(rows, 'dp', [(i, i ^ step) for i in range(steps)])]
  transfers between devices with their start and end apart: 13 -> 13, of which waited for: 4 -> 5; matrix products, arithmetic and copies ran while one was open for 0% -> 0% of each run, Pallas kernels for 4% -> 5%
where the time goes in v6:
time: 42.9 us; the launch traced here: 42.6 us
  starting transfers between devices  19.5 us (45%)
  waiting for transfers between devices  15.1 us (35%)
  Pallas kernels  6.3 us (15%)
  local copies, waits for them, and re-layouts  0.88 us (2%)
  between operations  0.83 us (2%)
    all_to_all x1, waiting for transfers between devices, body(): lax.all_to_all(sent, ('dp', 'pair', 'head'), split_axis=0, concat_axis=0,...  13.8 us
    ppermute x7, starting transfers between devices, exchange(): return lax.ppermute(rows, 'dp', [(i, i ^ step) for i in range(steps)])  9.45 us
    ppermute x5, starting transfers between devices, other_core(): return lax.ppermute(rows, 'pair', [(i, i ^ 1) for i in range(pairs)])  7.12 us
    pallas_call x1, Pallas kernels, expert_block(): pl.pallas_call(functools.partial(ffn_kernel, (capacity, heads, route_coun...  3.54 us
    all_to_all x1, starting transfers between devices, body(): lax.all_to_all(sent, ('dp', 'pair', 'head'), split_axis=0, concat_axis=0,...  2.94 us
    pallas_call x1, Pallas kernels, attend(): pl.pallas_call(functools.partial(attend_kernel, capacity, heads), out_sha...  1.93 us
    ppermute x5, waiting for transfers between devices, other_core(): return lax.ppermute(rows, 'pair', [(i, i ^ 1) for i in range(pairs)])  1.16 us
    unnamed x24, local copies, waits for them, and re-layouts  0.87 us
  transfers between devices with their start and end apart: 13, of which 5 were waited for; matrix products, arithmetic and copies ran while one was open for 0% of the time, Pallas kernels for 5%

profile of v6, /device:TPU:1, one launch (start us, length us, event | category | flops | bytes accessed | tf_op | source)
XLA Modules:
  0.0 42.6 jit_solution(9095836712322160043)
XLA Ops:
  0.6 0.0 copy-start.3
  0.6 0.0 copy-start.11
  0.7 0.7 %copy-done.3 = s32[8,8]{1,0:T(8,128)S(1)} copy-done((s32[8,8]{1,0:T(8,128)S(1)}, s32[8,8]{1,0:T(8,128)}, u32[]{:S(2)}) %copy-start.3) | copy-done | bytes 280
  1.3 0.2 copy-done.11
  1.5 2.1 %collective-permute-start = (bf16[8,4224]{1,0:T(8,128)(2,1)S(1)}, bf16[8,4224]{1,0:T(8,128)(2,1)S(1)}, u32[]{:S(2)}, u32[]{:S(2)}) collective-permute-start(bf16[8,4224]{1,0:T(8,128)(2,1)S(1)} %pad_maximum_fusion.1), channel_id=1, source_target_pairs={{0,8},{4,12},{8,0},{12,4},{16,24},{20,28},{24,16},{28,20},{1,9},{5... | collective-permute-start | bytes 202760 | tf_op jit(solution)/shard_map/ppermute | solution.py:241
  3.6 2.2 %collective-permute-start.3 = (bf16[8,4224]{1,0:T(8,128)(2,1)S(1)}, bf16[8,4224]{1,0:T(8,128)(2,1)S(1)}, u32[]{:S(2)}, u32[]{:S(2)}) collective-permute-start(bf16[8,4224]{1,0:T(8,128)(2,1)S(1)} %pad_maximum_fusion.1), channel_id=1, source_target_pairs={{0,24},{4,28},{8,16},{12,20},{16,8},{20,12},{24,0},{28,4},{1,25},{... | collective-permute-start | bytes 202760 | tf_op jit(solution)/shard_map/ppermute | solution.py:241
  5.8 1.4 %collective-permute-start.1 = (bf16[8,4224]{1,0:T(8,128)(2,1)S(1)}, bf16[8,4224]{1,0:T(8,128)(2,1)S(1)}, u32[]{:S(2)}, u32[]{:S(2)}) collective-permute-start(bf16[8,4224]{1,0:T(8,128)(2,1)S(1)} %pad_maximum_fusion.1), channel_id=1, source_target_pairs={{0,12},{4,8},{8,4},{12,0},{16,28},{20,24},{24,20},{28,16},{1,13},{... | collective-permute-start | bytes 202760 | tf_op jit(solution)/shard_map/ppermute | solution.py:241
  7.2 0.2 collective-permute-start.2
  7.4 1.9 %collective-permute-start.6 = (bf16[8,4224]{1,0:T(8,128)(2,1)S(1)}, bf16[8,4224]{1,0:T(8,128)(2,1)S(1)}, u32[]{:S(2)}, u32[]{:S(2)}) collective-permute-start(bf16[8,4224]{1,0:T(8,128)(2,1)S(1)} %pad_maximum_fusion.1), channel_id=1, source_target_pairs={{0,20},{4,16},{8,28},{12,24},{16,4},{20,0},{24,12},{28,8},{1,21},{... | collective-permute-start | bytes 202760 | tf_op jit(solution)/shard_map/ppermute | solution.py:241
  9.3 0.0 collective-permute-done
  9.3 1.4 %collective-permute-start.4 = (bf16[8,4224]{1,0:T(8,128)(2,1)S(1)}, bf16[8,4224]{1,0:T(8,128)(2,1)S(1)}, u32[]{:S(2)}, u32[]{:S(2)}) collective-permute-start(bf16[8,4224]{1,0:T(8,128)(2,1)S(1)} %pad_maximum_fusion.1), channel_id=1, source_target_pairs={{0,16},{4,20},{8,24},{12,28},{16,0},{20,4},{24,8},{28,12},{1,17},{... | collective-permute-start | bytes 202760 | tf_op jit(solution)/shard_map/ppermute | solution.py:241
  10.7 0.0 collective-permute-done.3.refs_1_
  10.7 0.2 collective-permute-start.5
  11.0 0.0 collective-permute-done.1
  11.0 0.1 collective-permute-done.2
  11.1 0.0 copy-start
  11.1 0.0 copy-start.1
  11.1 0.0 copy-start.2
  11.1 3.2 %collective-permute-start.7 = (bf16[32,4224]{1,0:T(8,128)(2,1)S(1)}, bf16[32,4224]{1,0:T(8,128)(2,1)S(1)}, u32[]{:S(2)}, u32[]{:S(2)}) collective-permute-start(bf16[32,4224]{1,0:T(8,128)(2,1)S(1)} %pad_maximum_fusion.refs_0_), channel_id=1, source_target_pairs={{0,1},{1,0},{2,3},{3,2},{4,5},{5,4},{6,7},{7,6},{8,9},{9,8},{10,11... | collective-permute-start | bytes 811016 | tf_op jit(solution)/shard_map/ppermute | solution.py:244
  14.3 0.1 collective-permute-start.8
  14.4 0.0 collective-permute-done.6.refs_4_
  14.4 3.1 %collective-permute-start.11 = (bf16[8,4224]{1,0:T(8,128)(2,1)S(1)}, bf16[8,4224]{1,0:T(8,128)(2,1)S(1)}, u32[]{:S(2)}, u32[]{:S(2)}) collective-permute-start(bf16[8,4224]{1,0:T(8,128)(2,1)S(1)} %collective-permute-done.6.refs_4_), channel_id=1, source_target_pairs={{0,1},{1,0},{2,3},{3,2},{4,5},{5,4},{6,7},{7,6},{8,9},{9,8},{10,11... | collective-permute-start | bytes 202760 | tf_op jit(solution)/shard_map/ppermute | solution.py:244
  17.5 0.0 collective-permute-done.4.refs_2_
  17.6 0.7 %collective-permute-start.9 = (bf16[8,4224]{1,0:T(8,128)(2,1)S(1)}, bf16[8,4224]{1,0:T(8,128)(2,1)S(1)}, u32[]{:S(2)}, u32[]{:S(2)}) collective-permute-start(bf16[8,4224]{1,0:T(8,128)(2,1)S(1)} %collective-permute-done.4.refs_2_), channel_id=1, source_target_pairs={{0,1},{1,0},{2,3},{3,2},{4,5},{5,4},{6,7},{7,6},{8,9},{9,8},{10,11... | collective-permute-start | bytes 202760 | tf_op jit(solution)/shard_map/ppermute | solution.py:244
  18.2 0.0 collective-permute-done.5.refs_3_
  18.2 0.0 collective-permute-start.10
  18.2 0.0 copy-start.4
  18.2 0.0 copy-start.5
  18.2 0.0 copy-start.6
  18.3 0.0 copy-start.7
  18.3 0.0 copy-start.8
  18.3 0.0 copy-start.9
  18.3 0.0 copy-start.10
  18.3 0.0 collective-permute-done.8.refs_6_
  18.3 0.1 collective-permute-done.11.refs_9_
  18.5 0.7 %collective-permute-done.9.refs_7_ = bf16[8,4224]{1,0:T(8,128)(2,1)S(1)} collective-permute-done((bf16[8,4224]{1,0:T(8,128)(2,1)S(1)}, bf16[8,4224]{1,0:T(8,128)(2,1)S(1)}, u32[]{:S(2)}, u32[]{:S(2)}) %collective-permute-start.9) | collective-permute-done | bytes 67616 | tf_op jit(solution)/shard_map/ppermute | solution.py:244
  19.1 0.4 collective-permute-done.10.refs_8_
  19.5 0.0 collective-permute-done.7.refs_5_
  19.5 0.0 copy-done
  19.5 0.0 copy-done.1
  19.5 0.0 copy-done.2
  19.5 3.5 %shard_map.134 = bf16[32,8,1024]{2,1,0:T(8,128)(2,1)} custom-call(s32[8,128]{1,0:T(8,128)S(1)} %shard_map.133.dp_ref, s32[8,128]{1,0:T(8,128)S(1)} %shard_map.131.pair_ref, bf16[32,4224]{1,0:T(8,128)(2,1)S(1)} %pad_maximum_fusion.refs_0_, bf16[8,4224]{1,0:T(8,128)(2,1)S(1)} %collective-permute-done.3.refs_1_, ...), custom_call_target="tpu_custom_call" | custom-call | flops 1207959552 | bytes 9437184 | tf_op jit(solution)/shard_map/pallas_call | solution.py:187
  23.0 2.9 %all-to-all-start = ((bf16[32,8,1024]{2,1,0:T(8,128)(2,1)}), bf16[32,8,1024]{2,1,0:T(8,128)(2,1)S(1)}, u32[]{:S(2)}, u32[]{:S(2)}) async-start(bf16[32,8,1024]{2,1,0:T(8,128)(2,1)} %shard_map.134), calls=%async_computation | async-start | bytes 1048576 | tf_op jit(solution)/shard_map/all_to_all | solution.py:265
  26.0 0.0 copy-done.4
  26.0 0.0 copy-done.5
  26.0 1.9 %shard_map.132 = (bf16[8,32,128]{2,1,0:T(8,128)(2,1)}, bf16[48,256]{1,0:T(8,128)(2,1)S(1)}) custom-call(s32[8]{0:T(128)S(1)} %copy-done.10, bf16[8,32,128]{2,1,0:T(8,128)(2,1)S(1)} %copy-done.6, bf16[8,2,64,128]{3,2,1,0:T(8,128)(2,1)S(1)} %copy-done.4, bf16[8,2,64,128]{3,2,1,0:T(8,128)(2,1)S(1)} %copy-done.5, bf16[8,2,128]{2,1,0:T(2,128)(2,1)S(1)} %copy-done.7, ...), custom_call_target="tpu_custom_call" | custom-call | flops 1000000000 | bytes 1000000 | tf_op jit(solution)/shard_map/pallas_call | solution.py:94
  28.0 13.8 %all-to-all-done.got_ref = bf16[32,8,1024]{2,1,0:T(8,128)(2,1)S(1)} async-done(((bf16[32,8,1024]{2,1,0:T(8,128)(2,1)}), bf16[32,8,1024]{2,1,0:T(8,128)(2,1)S(1)}, u32[]{:S(2)}, u32[]{:S(2)}) %all-to-all-start) | async-done | bytes 524320 | tf_op jit(solution)/shard_map/all_to_all | solution.py:265
  41.8 0.8 %shard_map.135 = bf16[8,2048]{1,0:T(8,128)(2,1)} custom-call(bf16[48,256]{1,0:T(8,128)(2,1)S(1)} %get-tuple-element.8.lhs_ref, bf16[32,8,1024]{2,1,0:T(8,128)(2,1)S(1)} %all-to-all-done.got_ref), custom_call_target="tpu_custom_call" | custom-call | tf_op jit(solution)/shard_map/pallas_call | solution.py:267
  (11 shorter events, 0.1 us)
Async XLA Ops:
  0.6 0.7 %copy-start.3 = (s32[8,8]{1,0:T(8,128)S(1)}, s32[8,8]{1,0:T(8,128)}, u32[]{:S(2)}) copy-start(s32[8,8]{1,0:T(8,128)} %routes_ref) | copy-start | bytes 772
  0.6 0.8 %copy-start.11 = (bf16[8,4096]{1,0:T(8,128)(2,1)S(1)}, bf16[8,4096]{1,0:T(8,128)(2,1)}, u32[]{:S(2)}) copy-start(bf16[8,4096]{1,0:T(8,128)(2,1)} %param.18) | copy-start | bytes 196612
  1.5 7.8 %collective-permute-start = (bf16[8,4224]{1,0:T(8,128)(2,1)S(1)}, bf16[8,4224]{1,0:T(8,128)(2,1)S(1)}, u32[]{:S(2)}, u32[]{:S(2)}) collective-permute-start(bf16[8,4224]{1,0:T(8,128)(2,1)S(1)} %pad_maximum_fusion.1), channel_id=1, source_target_pairs={{0,8},{4,12},{8,0},{12,4},{16,24},{20,28},{24,16},{28,20},{1,9},{5... | collective-permute-start | bytes 202760 | tf_op jit(solution)/shard_map/ppermute | solution.py:241
  3.6 7.1 %collective-permute-start.3 = (bf16[8,4224]{1,0:T(8,128)(2,1)S(1)}, bf16[8,4224]{1,0:T(8,128)(2,1)S(1)}, u32[]{:S(2)}, u32[]{:S(2)}) collective-permute-start(bf16[8,4224]{1,0:T(8,128)(2,1)S(1)} %pad_maximum_fusion.1), channel_id=1, source_target_pairs={{0,24},{4,28},{8,16},{12,20},{16,8},{20,12},{24,0},{28,4},{1,25},{... | collective-permute-start | bytes 202760 | tf_op jit(solution)/shard_map/ppermute | solution.py:241
  5.8 5.1 %collective-permute-start.1 = (bf16[8,4224]{1,0:T(8,128)(2,1)S(1)}, bf16[8,4224]{1,0:T(8,128)(2,1)S(1)}, u32[]{:S(2)}, u32[]{:S(2)}) collective-permute-start(bf16[8,4224]{1,0:T(8,128)(2,1)S(1)} %pad_maximum_fusion.1), channel_id=1, source_target_pairs={{0,12},{4,8},{8,4},{12,0},{16,28},{20,24},{24,20},{28,16},{1,13},{... | collective-permute-start | bytes 202760 | tf_op jit(solution)/shard_map/ppermute | solution.py:241
  7.2 3.9 %collective-permute-start.2 = (bf16[8,4224]{1,0:T(8,128)(2,1)S(1)}, bf16[8,4224]{1,0:T(8,128)(2,1)S(1)}, u32[]{:S(2)}, u32[]{:S(2)}) collective-permute-start(bf16[8,4224]{1,0:T(8,128)(2,1)S(1)} %pad_maximum_fusion.1), channel_id=1, source_target_pairs={{0,4},{4,0},{8,12},{12,8},{16,20},{20,16},{24,28},{28,24},{1,5},{5... | collective-permute-start | bytes 202760 | tf_op jit(solution)/shard_map/ppermute | solution.py:241
  7.4 7.0 %collective-permute-start.6 = (bf16[8,4224]{1,0:T(8,128)(2,1)S(1)}, bf16[8,4224]{1,0:T(8,128)(2,1)S(1)}, u32[]{:S(2)}, u32[]{:S(2)}) collective-permute-start(bf16[8,4224]{1,0:T(8,128)(2,1)S(1)} %pad_maximum_fusion.1), channel_id=1, source_target_pairs={{0,20},{4,16},{8,28},{12,24},{16,4},{20,0},{24,12},{28,8},{1,21},{... | collective-permute-start | bytes 202760 | tf_op jit(solution)/shard_map/ppermute | solution.py:241
  9.3 8.2 %collective-permute-start.4 = (bf16[8,4224]{1,0:T(8,128)(2,1)S(1)}, bf16[8,4224]{1,0:T(8,128)(2,1)S(1)}, u32[]{:S(2)}, u32[]{:S(2)}) collective-permute-start(bf16[8,4224]{1,0:T(8,128)(2,1)S(1)} %pad_maximum_fusion.1), channel_id=1, source_target_pairs={{0,16},{4,20},{8,24},{12,28},{16,0},{20,4},{24,8},{28,12},{1,17},{... | collective-permute-start | bytes 202760 | tf_op jit(solution)/shard_map/ppermute | solution.py:241
  10.7 7.5 %collective-permute-start.5 = (bf16[8,4224]{1,0:T(8,128)(2,1)S(1)}, bf16[8,4224]{1,0:T(8,128)(2,1)S(1)}, u32[]{:S(2)}, u32[]{:S(2)}) collective-permute-start(bf16[8,4224]{1,0:T(8,128)(2,1)S(1)} %collective-permute-done.3.refs_1_), channel_id=1, source_target_pairs={{0,4},{4,0},{8,12},{12,8},{16,20},{20,16},{24,28},{28,24},{1,5},{5... | collective-permute-start | bytes 202760 | tf_op jit(solution)/shard_map/ppermute | solution.py:241
  11.1 8.4 %copy-start = (bf16[1,384,4096]{2,1,0:T(8,128)(2,1)S(1)}, bf16[1,384,4096]{2,1,0:T(8,128)(2,1)}, u32[]{:S(2)}) copy-start(bf16[1,384,4096]{2,1,0:T(8,128)(2,1)} %refs_10_.1) | copy-start | bytes 9437188
  11.1 8.4 %copy-start.1 = (bf16[1,384,4096]{2,1,0:T(8,128)(2,1)S(1)}, bf16[1,384,4096]{2,1,0:T(8,128)(2,1)}, u32[]{:S(2)}) copy-start(bf16[1,384,4096]{2,1,0:T(8,128)(2,1)} %refs_11_.1) | copy-start | bytes 9437188
  11.1 8.4 %copy-start.2 = (bf16[1,384,4096]{2,1,0:T(8,128)(2,1)S(1)}, bf16[1,384,4096]{2,1,0:T(8,128)(2,1)}, u32[]{:S(2)}) copy-start(bf16[1,384,4096]{2,1,0:T(8,128)(2,1)} %refs_12_.1) | copy-start | bytes 9437188
  11.1 8.4 %collective-permute-start.7 = (bf16[32,4224]{1,0:T(8,128)(2,1)S(1)}, bf16[32,4224]{1,0:T(8,128)(2,1)S(1)}, u32[]{:S(2)}, u32[]{:S(2)}) collective-permute-start(bf16[32,4224]{1,0:T(8,128)(2,1)S(1)} %pad_maximum_fusion.refs_0_), channel_id=1, source_target_pairs={{0,1},{1,0},{2,3},{3,2},{4,5},{5,4},{6,7},{7,6},{8,9},{9,8},{10,11... | collective-permute-start | bytes 811016 | tf_op jit(solution)/shard_map/ppermute | solution.py:244
  14.3 4.0 %collective-permute-start.8 = (bf16[8,4224]{1,0:T(8,128)(2,1)S(1)}, bf16[8,4224]{1,0:T(8,128)(2,1)S(1)}, u32[]{:S(2)}, u32[]{:S(2)}) collective-permute-start(bf16[8,4224]{1,0:T(8,128)(2,1)S(1)} %collective-permute-done.3.refs_1_), channel_id=1, source_target_pairs={{0,1},{1,0},{2,3},{3,2},{4,5},{5,4},{6,7},{7,6},{8,9},{9,8},{10,11... | collective-permute-start | bytes 202760 | tf_op jit(solution)/shard_map/ppermute | solution.py:244
  14.4 4.0 %collective-permute-start.11 = (bf16[8,4224]{1,0:T(8,128)(2,1)S(1)}, bf16[8,4224]{1,0:T(8,128)(2,1)S(1)}, u32[]{:S(2)}, u32[]{:S(2)}) collective-permute-start(bf16[8,4224]{1,0:T(8,128)(2,1)S(1)} %collective-permute-done.6.refs_4_), channel_id=1, source_target_pairs={{0,1},{1,0},{2,3},{3,2},{4,5},{5,4},{6,7},{7,6},{8,9},{9,8},{10,11... | collective-permute-start | bytes 202760 | tf_op jit(solution)/shard_map/ppermute | solution.py:244
  17.6 1.6 %collective-permute-start.9 = (bf16[8,4224]{1,0:T(8,128)(2,1)S(1)}, bf16[8,4224]{1,0:T(8,128)(2,1)S(1)}, u32[]{:S(2)}, u32[]{:S(2)}) collective-permute-start(bf16[8,4224]{1,0:T(8,128)(2,1)S(1)} %collective-permute-done.4.refs_2_), channel_id=1, source_target_pairs={{0,1},{1,0},{2,3},{3,2},{4,5},{5,4},{6,7},{7,6},{8,9},{9,8},{10,11... | collective-permute-start | bytes 202760 | tf_op jit(solution)/shard_map/ppermute | solution.py:244
  18.2 1.3 %collective-permute-start.10 = (bf16[8,4224]{1,0:T(8,128)(2,1)S(1)}, bf16[8,4224]{1,0:T(8,128)(2,1)S(1)}, u32[]{:S(2)}, u32[]{:S(2)}) collective-permute-start(bf16[8,4224]{1,0:T(8,128)(2,1)S(1)} %collective-permute-done.5.refs_3_), channel_id=1, source_target_pairs={{0,1},{1,0},{2,3},{3,2},{4,5},{5,4},{6,7},{7,6},{8,9},{9,8},{10,11... | collective-permute-start | bytes 202760 | tf_op jit(solution)/shard_map/ppermute | solution.py:244
  18.2 7.8 %copy-start.4 = (bf16[8,2,64,128]{3,2,1,0:T(8,128)(2,1)S(1)}, bf16[8,2,64,128]{3,2,1,0:T(8,128)(2,1)}, u32[]{:S(2)}) copy-start(bf16[8,2,64,128]{3,2,1,0:T(8,128)(2,1)} %keys_ref.1) | copy-start | bytes 786436
  18.2 7.8 %copy-start.5 = (bf16[8,2,64,128]{3,2,1,0:T(8,128)(2,1)S(1)}, bf16[8,2,64,128]{3,2,1,0:T(8,128)(2,1)}, u32[]{:S(2)}) copy-start(bf16[8,2,64,128]{3,2,1,0:T(8,128)(2,1)} %values_ref.1) | copy-start | bytes 786436
  18.2 7.8 %copy-start.6 = (bf16[8,32,128]{2,1,0:T(8,128)(2,1)S(1)}, bf16[8,32,128]{2,1,0:T(8,128)(2,1)}, u32[]{:S(2)}) copy-start(bf16[8,32,128]{2,1,0:T(8,128)(2,1)} %queries_ref.1) | copy-start | bytes 196612
  18.3 7.8 %copy-start.7 = (bf16[8,2,128]{2,1,0:T(2,128)(2,1)S(1)}, bf16[8,2,128]{2,1,0:T(2,128)(2,1)}, u32[]{:S(2)}) copy-start(bf16[8,2,128]{2,1,0:T(2,128)(2,1)} %new_key_ref.1) | copy-start | bytes 12292
  18.3 7.8 %copy-start.8 = (bf16[8,2,128]{2,1,0:T(2,128)(2,1)S(1)}, bf16[8,2,128]{2,1,0:T(2,128)(2,1)}, u32[]{:S(2)}) copy-start(bf16[8,2,128]{2,1,0:T(2,128)(2,1)} %new_value_ref.1) | copy-start | bytes 12292
  18.3 7.8 %copy-start.9 = (f32[8,8]{1,0:T(8,128)S(1)}, f32[8,8]{1,0:T(8,128)}, u32[]{:S(2)}) copy-start(f32[8,8]{1,0:T(8,128)} %weights_ref.1) | copy-start | bytes 772
  18.3 7.7 %copy-start.10 = (s32[8]{0:T(128)S(1)}, s32[8]{0:T(128)}, u32[]{:S(2)}) copy-start(s32[8]{0:T(128)} %lengths_ref.1) | copy-start | bytes 100
  23.0 18.8 %all-to-all-start = ((bf16[32,8,1024]{2,1,0:T(8,128)(2,1)}), bf16[32,8,1024]{2,1,0:T(8,128)(2,1)S(1)}, u32[]{:S(2)}, u32[]{:S(2)}) async-start(bf16[32,8,1024]{2,1,0:T(8,128)(2,1)} %shard_map.134), calls=%async_computation | async-start | bytes 1048576 | tf_op jit(solution)/shard_map/all_to_all | solution.py:265

commit v7 on v6

--- a/solution.py
+++ b/solution.py
@@ -244,14 +244,13 @@
         return lax.ppermute(rows, "pair", [(i, i ^ 1) for i in range(pairs)])
 
     even = sorted(range(2, steps, 2), reverse=True)
-    far = even[: len(even) * 2 // 3]
-    near = [s + odd for s in even[len(far) :] for odd in (0, 1)] + [1]
-    direct = {step: exchange(block, step) for step in far + near}
     place = (my_place("dp", 2 * 10**10), my_pair)
-    near_rows = jnp.concatenate([block] + [direct[step] for step in near], axis=0)
-    mine = [near_rows] + [direct[step] for step in far]
-    mine = mine + [exchange(direct[far[0]], 1)] + [exchange(block, step ^ 1) for step in far[1:]]
-    order = [0] + near + far + [s ^ 1 for s in far]
+    farthest = exchange(block, even[0])
+    both = jnp.concatenate([block, exchange(block, 1)], axis=0)
+    last = [s ^ odd for s in even[-1:] for odd in (0, 1)]
+    mine = [both, farthest] + [exchange(block, step) for step in last]
+    mine = mine + [exchange(both, step) for step in even[1:-1]] + [exchange(farthest, 1)]
+    order = [0, 1, even[0]] + last + [s ^ odd for s in even[1:-1] for odd in (0, 1)] + [even[0] ^ 1]
 
     attention, lhs = attend(
         lengths, queries, key_cache, value_cache, new_key, new_value, routes, gate_weights,

time: 42.9 us -> 42.8 us (level)
    ppermute x5 -> x6, starting transfers between devices: 7.12 us -> 7.85 us  [other_core(): return lax.ppermute(rows, 'pair', [(i, i ^ 1) for i in range(pairs)])]
    ppermute x7 -> x6, starting transfers between devices: 9.45 us -> 8.99 us  [exchange(): return lax.ppermute(rows, 'dp', [(i, i ^ step) for i in range(steps)])]
    ppermute x5 -> x6, waiting for transfers between devices: 1.16 us -> 0.98 us  [other_core(): return lax.ppermute(rows, 'pair', [(i, i ^ 1) for i in range(pairs)])]
  transfers between devices with their start and end apart: 13 -> 13, of which waited for: 5 -> 4; matrix products, arithmetic and copies ran while one was open for 0% -> 0% of each run, Pallas kernels for 5% -> 5%
where the time goes in v7:
time: 42.8 us; the launch traced here: 42.5 us
  starting transfers between devices  19.7 us (46%)
  waiting for transfers between devices  14.8 us (35%)
  Pallas kernels  6.29 us (15%)
  local copies, waits for them, and re-layouts  0.87 us (2%)
  between operations  0.8 us (2%)
    all_to_all x1, waiting for transfers between devices, body(): lax.all_to_all(sent, ('dp', 'pair', 'head'), split_axis=0, concat_axis=0,...  13.8 us
    ppermute x6, starting transfers between devices, exchange(): return lax.ppermute(rows, 'dp', [(i, i ^ step) for i in range(steps)])  8.99 us
    ppermute x6, starting transfers between devices, other_core(): return lax.ppermute(rows, 'pair', [(i, i ^ 1) for i in range(pairs)])  7.85 us
    pallas_call x1, Pallas kernels, expert_block(): pl.pallas_call(functools.partial(ffn_kernel, (capacity, heads, route_coun...  3.53 us
    all_to_all x1, starting transfers between devices, body(): lax.all_to_all(sent, ('dp', 'pair', 'head'), split_axis=0, concat_axis=0,...  2.88 us
    pallas_call x1, Pallas kernels, attend(): pl.pallas_call(functools.partial(attend_kernel, capacity, heads), out_sha...  1.93 us
    ppermute x6, waiting for transfers between devices, other_core(): return lax.ppermute(rows, 'pair', [(i, i ^ 1) for i in range(pairs)])  0.98 us
    unnamed x24, local copies, waits for them, and re-layouts  0.86 us
  transfers between devices with their start and end apart: 13, of which 4 were waited for; matrix products, arithmetic and copies ran while one was open for 0% of the time, Pallas kernels for 5%

profile of v7, /device:TPU:1, one launch (start us, length us, event | category | flops | bytes accessed | tf_op | source)
XLA Modules:
  0.0 42.5 jit_solution(4470945037563926237)
XLA Ops:
  0.6 0.0 copy-start.3
  0.6 0.0 copy-start.11
  0.7 0.7 %copy-done.3 = s32[8,8]{1,0:T(8,128)S(1)} copy-done((s32[8,8]{1,0:T(8,128)S(1)}, s32[8,8]{1,0:T(8,128)}, u32[]{:S(2)}) %copy-start.3) | copy-done | bytes 280
  1.3 0.2 copy-done.11
  1.5 2.1 %collective-permute-start = (bf16[8,4224]{1,0:T(8,128)(2,1)S(1)}, bf16[8,4224]{1,0:T(8,128)(2,1)S(1)}, u32[]{:S(2)}, u32[]{:S(2)}) collective-permute-start(bf16[8,4224]{1,0:T(8,128)(2,1)S(1)} %pad_maximum_fusion.1), channel_id=1, source_target_pairs={{0,4},{4,0},{8,12},{12,8},{16,20},{20,16},{24,28},{28,24},{1,5},{5... | collective-permute-start | bytes 202760 | tf_op jit(solution)/shard_map/ppermute | solution.py:241
  3.6 3.3 %collective-permute-start.1 = (bf16[8,4224]{1,0:T(8,128)(2,1)S(1)}, bf16[8,4224]{1,0:T(8,128)(2,1)S(1)}, u32[]{:S(2)}, u32[]{:S(2)}) collective-permute-start(bf16[8,4224]{1,0:T(8,128)(2,1)S(1)} %pad_maximum_fusion.1), channel_id=1, source_target_pairs={{0,24},{4,28},{8,16},{12,20},{16,8},{20,12},{24,0},{28,4},{1,25},{... | collective-permute-start | bytes 202760 | tf_op jit(solution)/shard_map/ppermute | solution.py:241
  6.9 0.0 collective-permute-done
  6.9 0.0 copy-start
  6.9 0.0 copy-start.1
  6.9 0.0 copy-start.2
  6.9 0.9 %collective-permute-start.4 = (bf16[16,4224]{1,0:T(8,128)(2,1)S(1)}, bf16[16,4224]{1,0:T(8,128)(2,1)S(1)}, u32[]{:S(2)}, u32[]{:S(2)}) collective-permute-start(bf16[16,4224]{1,0:T(8,128)(2,1)S(1)} %pad_maximum_fusion.refs_0_), channel_id=1, source_target_pairs={{0,16},{4,20},{8,24},{12,28},{16,0},{20,4},{24,8},{28,12},{1,17},{... | collective-permute-start | bytes 405512 | tf_op jit(solution)/shard_map/ppermute | solution.py:241
  7.9 1.3 %collective-permute-start.2 = (bf16[8,4224]{1,0:T(8,128)(2,1)S(1)}, bf16[8,4224]{1,0:T(8,128)(2,1)S(1)}, u32[]{:S(2)}, u32[]{:S(2)}) collective-permute-start(bf16[8,4224]{1,0:T(8,128)(2,1)S(1)} %pad_maximum_fusion.1), channel_id=1, source_target_pairs={{0,8},{4,12},{8,0},{12,4},{16,24},{20,28},{24,16},{28,20},{1,9},{5... | collective-permute-start | bytes 202760 | tf_op jit(solution)/shard_map/ppermute | solution.py:241
  9.2 1.1 %collective-permute-start.3 = (bf16[8,4224]{1,0:T(8,128)(2,1)S(1)}, bf16[8,4224]{1,0:T(8,128)(2,1)S(1)}, u32[]{:S(2)}, u32[]{:S(2)}) collective-permute-start(bf16[8,4224]{1,0:T(8,128)(2,1)S(1)} %pad_maximum_fusion.1), channel_id=1, source_target_pairs={{0,12},{4,8},{8,4},{12,0},{16,28},{20,24},{24,20},{28,16},{1,13},{... | collective-permute-start | bytes 202760 | tf_op jit(solution)/shard_map/ppermute | solution.py:241
  10.3 0.0 collective-permute-done.1.refs_1_
  10.3 0.2 collective-permute-start.5
  10.5 2.9 %collective-permute-start.7 = (bf16[8,4224]{1,0:T(8,128)(2,1)S(1)}, bf16[8,4224]{1,0:T(8,128)(2,1)S(1)}, u32[]{:S(2)}, u32[]{:S(2)}) collective-permute-start(bf16[8,4224]{1,0:T(8,128)(2,1)S(1)} %collective-permute-done.1.refs_1_), channel_id=1, source_target_pairs={{0,1},{1,0},{2,3},{3,2},{4,5},{5,4},{6,7},{7,6},{8,9},{9,8},{10,11... | collective-permute-start | bytes 202760 | tf_op jit(solution)/shard_map/ppermute | solution.py:244
  13.5 0.0 collective-permute-done.2.refs_2_
  13.5 3.2 %collective-permute-start.6 = (bf16[16,4224]{1,0:T(8,128)(2,1)S(1)}, bf16[16,4224]{1,0:T(8,128)(2,1)S(1)}, u32[]{:S(2)}, u32[]{:S(2)}) collective-permute-start(bf16[16,4224]{1,0:T(8,128)(2,1)S(1)} %pad_maximum_fusion.refs_0_), channel_id=1, source_target_pairs={{0,1},{1,0},{2,3},{3,2},{4,5},{5,4},{6,7},{7,6},{8,9},{9,8},{10,11... | collective-permute-start | bytes 405512 | tf_op jit(solution)/shard_map/ppermute | solution.py:244
  16.7 0.0 collective-permute-done.3.refs_3_
  16.7 0.9 %collective-permute-start.8 = (bf16[8,4224]{1,0:T(8,128)(2,1)S(1)}, bf16[8,4224]{1,0:T(8,128)(2,1)S(1)}, u32[]{:S(2)}, u32[]{:S(2)}) collective-permute-start(bf16[8,4224]{1,0:T(8,128)(2,1)S(1)} %collective-permute-done.2.refs_2_), channel_id=1, source_target_pairs={{0,1},{1,0},{2,3},{3,2},{4,5},{5,4},{6,7},{7,6},{8,9},{9,8},{10,11... | collective-permute-start | bytes 202760 | tf_op jit(solution)/shard_map/ppermute | solution.py:244
  17.6 0.0 collective-permute-done.5.refs_5_
  17.6 0.3 collective-permute-start.9
  17.9 0.0 collective-permute-done.7.refs_7_
  17.9 0.2 collective-permute-start.11
  18.1 0.0 collective-permute-done.4.refs_4_
  18.1 0.3 collective-permute-start.10
  18.4 0.0 copy-start.7
  18.4 0.0 copy-start.8
  18.4 0.0 copy-start.9
  18.5 0.0 copy-start.10
  18.5 0.0 collective-permute-done.8.refs_8_
  18.5 0.4 collective-permute-done.9.refs_9_
  18.8 0.0 collective-permute-done.6.refs_6_
  18.8 0.3 collective-permute-done.11.refs_11_
  19.2 0.3 collective-permute-done.10.refs_10_
  19.4 0.0 copy-done
  19.5 3.5 %shard_map.134 = bf16[32,8,1024]{2,1,0:T(8,128)(2,1)} custom-call(s32[8,128]{1,0:T(8,128)S(1)} %shard_map.133.dp_ref, s32[8,128]{1,0:T(8,128)S(1)} %shard_map.131.pair_ref, bf16[16,4224]{1,0:T(8,128)(2,1)S(1)} %pad_maximum_fusion.refs_0_, bf16[8,4224]{1,0:T(8,128)(2,1)S(1)} %collective-permute-done.1.refs_1_, ...), custom_call_target="tpu_custom_call" | custom-call | flops 1207959552 | bytes 9437184 | tf_op jit(solution)/shard_map/pallas_call | solution.py:187
  23.0 2.9 %all-to-all-start = ((bf16[32,8,1024]{2,1,0:T(8,128)(2,1)}), bf16[32,8,1024]{2,1,0:T(8,128)(2,1)S(1)}, u32[]{:S(2)}, u32[]{:S(2)}) async-start(bf16[32,8,1024]{2,1,0:T(8,128)(2,1)} %shard_map.134), calls=%async_computation | async-start | bytes 1048576 | tf_op jit(solution)/shard_map/all_to_all | solution.py:264
  25.9 0.0 copy-done.4
  25.9 0.0 copy-done.5
  25.9 0.0 copy-done.6
  25.9 0.0 copy-done.7
  25.9 0.0 copy-done.8
  25.9 0.0 copy-done.9
  25.9 0.0 copy-done.10
  26.0 1.9 %shard_map.132 = (bf16[8,32,128]{2,1,0:T(8,128)(2,1)}, bf16[48,256]{1,0:T(8,128)(2,1)S(1)}) custom-call(s32[8]{0:T(128)S(1)} %copy-done.10, bf16[8,32,128]{2,1,0:T(8,128)(2,1)S(1)} %copy-done.6, bf16[8,2,64,128]{3,2,1,0:T(8,128)(2,1)S(1)} %copy-done.4, bf16[8,2,64,128]{3,2,1,0:T(8,128)(2,1)S(1)} %copy-done.5, bf16[8,2,128]{2,1,0:T(2,128)(2,1)S(1)} %copy-done.7, ...), custom_call_target="tpu_custom_call" | custom-call | flops 1000000000 | bytes 1000000 | tf_op jit(solution)/shard_map/pallas_call | solution.py:94
  27.9 13.8 %all-to-all-done.got_ref = bf16[32,8,1024]{2,1,0:T(8,128)(2,1)S(1)} async-done(((bf16[32,8,1024]{2,1,0:T(8,128)(2,1)}), bf16[32,8,1024]{2,1,0:T(8,128)(2,1)S(1)}, u32[]{:S(2)}, u32[]{:S(2)}) %all-to-all-start) | async-done | bytes 524320 | tf_op jit(solution)/shard_map/all_to_all | solution.py:264
  41.7 0.8 %shard_map.135 = bf16[8,2048]{1,0:T(8,128)(2,1)} custom-call(bf16[48,256]{1,0:T(8,128)(2,1)S(1)} %get-tuple-element.8.lhs_ref, bf16[32,8,1024]{2,1,0:T(8,128)(2,1)S(1)} %all-to-all-done.got_ref), custom_call_target="tpu_custom_call" | custom-call | tf_op jit(solution)/shard_map/pallas_call | solution.py:266
  (11 shorter events, 0.0 us)
Async XLA Ops:
  0.6 0.7 %copy-start.3 = (s32[8,8]{1,0:T(8,128)S(1)}, s32[8,8]{1,0:T(8,128)}, u32[]{:S(2)}) copy-start(s32[8,8]{1,0:T(8,128)} %routes_ref) | copy-start | bytes 772
  0.6 0.8 %copy-start.11 = (bf16[8,4096]{1,0:T(8,128)(2,1)S(1)}, bf16[8,4096]{1,0:T(8,128)(2,1)}, u32[]{:S(2)}) copy-start(bf16[8,4096]{1,0:T(8,128)(2,1)} %param.18) | copy-start | bytes 196612
  1.5 5.4 %collective-permute-start = (bf16[8,4224]{1,0:T(8,128)(2,1)S(1)}, bf16[8,4224]{1,0:T(8,128)(2,1)S(1)}, u32[]{:S(2)}, u32[]{:S(2)}) collective-permute-start(bf16[8,4224]{1,0:T(8,128)(2,1)S(1)} %pad_maximum_fusion.1), channel_id=1, source_target_pairs={{0,4},{4,0},{8,12},{12,8},{16,20},{20,16},{24,28},{28,24},{1,5},{5... | collective-permute-start | bytes 202760 | tf_op jit(solution)/shard_map/ppermute | solution.py:241
  3.6 6.7 %collective-permute-start.1 = (bf16[8,4224]{1,0:T(8,128)(2,1)S(1)}, bf16[8,4224]{1,0:T(8,128)(2,1)S(1)}, u32[]{:S(2)}, u32[]{:S(2)}) collective-permute-start(bf16[8,4224]{1,0:T(8,128)(2,1)S(1)} %pad_maximum_fusion.1), channel_id=1, source_target_pairs={{0,24},{4,28},{8,16},{12,20},{16,8},{20,12},{24,0},{28,4},{1,25},{... | collective-permute-start | bytes 202760 | tf_op jit(solution)/shard_map/ppermute | solution.py:241
  6.9 12.5 %copy-start = (bf16[1,384,4096]{2,1,0:T(8,128)(2,1)S(1)}, bf16[1,384,4096]{2,1,0:T(8,128)(2,1)}, u32[]{:S(2)}) copy-start(bf16[1,384,4096]{2,1,0:T(8,128)(2,1)} %refs_12_.1) | copy-start | bytes 9437188
  6.9 12.5 %copy-start.1 = (bf16[1,384,4096]{2,1,0:T(8,128)(2,1)S(1)}, bf16[1,384,4096]{2,1,0:T(8,128)(2,1)}, u32[]{:S(2)}) copy-start(bf16[1,384,4096]{2,1,0:T(8,128)(2,1)} %refs_13_.1) | copy-start | bytes 9437188
  6.9 12.5 %copy-start.2 = (bf16[1,384,4096]{2,1,0:T(8,128)(2,1)S(1)}, bf16[1,384,4096]{2,1,0:T(8,128)(2,1)}, u32[]{:S(2)}) copy-start(bf16[1,384,4096]{2,1,0:T(8,128)(2,1)} %refs_14_.1) | copy-start | bytes 9437188
  6.9 11.2 %collective-permute-start.4 = (bf16[16,4224]{1,0:T(8,128)(2,1)S(1)}, bf16[16,4224]{1,0:T(8,128)(2,1)S(1)}, u32[]{:S(2)}, u32[]{:S(2)}) collective-permute-start(bf16[16,4224]{1,0:T(8,128)(2,1)S(1)} %pad_maximum_fusion.refs_0_), channel_id=1, source_target_pairs={{0,16},{4,20},{8,24},{12,28},{16,0},{20,4},{24,8},{28,12},{1,17},{... | collective-permute-start | bytes 405512 | tf_op jit(solution)/shard_map/ppermute | solution.py:241
  7.9 5.6 %collective-permute-start.2 = (bf16[8,4224]{1,0:T(8,128)(2,1)S(1)}, bf16[8,4224]{1,0:T(8,128)(2,1)S(1)}, u32[]{:S(2)}, u32[]{:S(2)}) collective-permute-start(bf16[8,4224]{1,0:T(8,128)(2,1)S(1)} %pad_maximum_fusion.1), channel_id=1, source_target_pairs={{0,8},{4,12},{8,0},{12,4},{16,24},{20,28},{24,16},{28,20},{1,9},{5... | collective-permute-start | bytes 202760 | tf_op jit(solution)/shard_map/ppermute | solution.py:241
  9.2 7.5 %collective-permute-start.3 = (bf16[8,4224]{1,0:T(8,128)(2,1)S(1)}, bf16[8,4224]{1,0:T(8,128)(2,1)S(1)}, u32[]{:S(2)}, u32[]{:S(2)}) collective-permute-start(bf16[8,4224]{1,0:T(8,128)(2,1)S(1)} %pad_maximum_fusion.1), channel_id=1, source_target_pairs={{0,12},{4,8},{8,4},{12,0},{16,28},{20,24},{24,20},{28,16},{1,13},{... | collective-permute-start | bytes 202760 | tf_op jit(solution)/shard_map/ppermute | solution.py:241
  10.3 7.3 %collective-permute-start.5 = (bf16[8,4224]{1,0:T(8,128)(2,1)S(1)}, bf16[8,4224]{1,0:T(8,128)(2,1)S(1)}, u32[]{:S(2)}, u32[]{:S(2)}) collective-permute-start(bf16[8,4224]{1,0:T(8,128)(2,1)S(1)} %collective-permute-done.1.refs_1_), channel_id=1, source_target_pairs={{0,4},{4,0},{8,12},{12,8},{16,20},{20,16},{24,28},{28,24},{1,5},{5... | collective-permute-start | bytes 202760 | tf_op jit(solution)/shard_map/ppermute | solution.py:241
  10.5 7.4 %collective-permute-start.7 = (bf16[8,4224]{1,0:T(8,128)(2,1)S(1)}, bf16[8,4224]{1,0:T(8,128)(2,1)S(1)}, u32[]{:S(2)}, u32[]{:S(2)}) collective-permute-start(bf16[8,4224]{1,0:T(8,128)(2,1)S(1)} %collective-permute-done.1.refs_1_), channel_id=1, source_target_pairs={{0,1},{1,0},{2,3},{3,2},{4,5},{5,4},{6,7},{7,6},{8,9},{9,8},{10,11... | collective-permute-start | bytes 202760 | tf_op jit(solution)/shard_map/ppermute | solution.py:244
  13.5 5.3 %collective-permute-start.6 = (bf16[16,4224]{1,0:T(8,128)(2,1)S(1)}, bf16[16,4224]{1,0:T(8,128)(2,1)S(1)}, u32[]{:S(2)}, u32[]{:S(2)}) collective-permute-start(bf16[16,4224]{1,0:T(8,128)(2,1)S(1)} %pad_maximum_fusion.refs_0_), channel_id=1, source_target_pairs={{0,1},{1,0},{2,3},{3,2},{4,5},{5,4},{6,7},{7,6},{8,9},{9,8},{10,11... | collective-permute-start | bytes 405512 | tf_op jit(solution)/shard_map/ppermute | solution.py:244
  16.7 1.8 %collective-permute-start.8 = (bf16[8,4224]{1,0:T(8,128)(2,1)S(1)}, bf16[8,4224]{1,0:T(8,128)(2,1)S(1)}, u32[]{:S(2)}, u32[]{:S(2)}) collective-permute-start(bf16[8,4224]{1,0:T(8,128)(2,1)S(1)} %collective-permute-done.2.refs_2_), channel_id=1, source_target_pairs={{0,1},{1,0},{2,3},{3,2},{4,5},{5,4},{6,7},{7,6},{8,9},{9,8},{10,11... | collective-permute-start | bytes 202760 | tf_op jit(solution)/shard_map/ppermute | solution.py:244
  17.6 1.3 %collective-permute-start.9 = (bf16[8,4224]{1,0:T(8,128)(2,1)S(1)}, bf16[8,4224]{1,0:T(8,128)(2,1)S(1)}, u32[]{:S(2)}, u32[]{:S(2)}) collective-permute-start(bf16[8,4224]{1,0:T(8,128)(2,1)S(1)} %collective-permute-done.3.refs_3_), channel_id=1, source_target_pairs={{0,1},{1,0},{2,3},{3,2},{4,5},{5,4},{6,7},{7,6},{8,9},{9,8},{10,11... | collective-permute-start | bytes 202760 | tf_op jit(solution)/shard_map/ppermute | solution.py:244
  17.9 1.3 %collective-permute-start.11 = (bf16[8,4224]{1,0:T(8,128)(2,1)S(1)}, bf16[8,4224]{1,0:T(8,128)(2,1)S(1)}, u32[]{:S(2)}, u32[]{:S(2)}) collective-permute-start(bf16[8,4224]{1,0:T(8,128)(2,1)S(1)} %collective-permute-done.5.refs_5_), channel_id=1, source_target_pairs={{0,1},{1,0},{2,3},{3,2},{4,5},{5,4},{6,7},{7,6},{8,9},{9,8},{10,11... | collective-permute-start | bytes 202760 | tf_op jit(solution)/shard_map/ppermute | solution.py:244
  18.1 1.4 %collective-permute-start.10 = (bf16[16,4224]{1,0:T(8,128)(2,1)S(1)}, bf16[16,4224]{1,0:T(8,128)(2,1)S(1)}, u32[]{:S(2)}, u32[]{:S(2)}) collective-permute-start(bf16[16,4224]{1,0:T(8,128)(2,1)S(1)} %collective-permute-done.4.refs_4_), channel_id=1, source_target_pairs={{0,1},{1,0},{2,3},{3,2},{4,5},{5,4},{6,7},{7,6},{8,9},{9,8},{10,11... | collective-permute-start | bytes 405512 | tf_op jit(solution)/shard_map/ppermute | solution.py:244
  18.4 7.5 %copy-start.4 = (bf16[8,2,64,128]{3,2,1,0:T(8,128)(2,1)S(1)}, bf16[8,2,64,128]{3,2,1,0:T(8,128)(2,1)}, u32[]{:S(2)}) copy-start(bf16[8,2,64,128]{3,2,1,0:T(8,128)(2,1)} %keys_ref.1) | copy-start | bytes 786436
  18.4 7.5 %copy-start.5 = (bf16[8,2,64,128]{3,2,1,0:T(8,128)(2,1)S(1)}, bf16[8,2,64,128]{3,2,1,0:T(8,128)(2,1)}, u32[]{:S(2)}) copy-start(bf16[8,2,64,128]{3,2,1,0:T(8,128)(2,1)} %values_ref.1) | copy-start | bytes 786436
  18.4 7.5 %copy-start.6 = (bf16[8,32,128]{2,1,0:T(8,128)(2,1)S(1)}, bf16[8,32,128]{2,1,0:T(8,128)(2,1)}, u32[]{:S(2)}) copy-start(bf16[8,32,128]{2,1,0:T(8,128)(2,1)} %queries_ref.1) | copy-start | bytes 196612
  18.4 7.5 %copy-start.7 = (bf16[8,2,128]{2,1,0:T(2,128)(2,1)S(1)}, bf16[8,2,128]{2,1,0:T(2,128)(2,1)}, u32[]{:S(2)}) copy-start(bf16[8,2,128]{2,1,0:T(2,128)(2,1)} %new_key_ref.1) | copy-start | bytes 12292
  18.4 7.5 %copy-start.8 = (bf16[8,2,128]{2,1,0:T(2,128)(2,1)S(1)}, bf16[8,2,128]{2,1,0:T(2,128)(2,1)}, u32[]{:S(2)}) copy-start(bf16[8,2,128]{2,1,0:T(2,128)(2,1)} %new_value_ref.1) | copy-start | bytes 12292
  18.4 7.5 %copy-start.9 = (f32[8,8]{1,0:T(8,128)S(1)}, f32[8,8]{1,0:T(8,128)}, u32[]{:S(2)}) copy-start(f32[8,8]{1,0:T(8,128)} %weights_ref.1) | copy-start | bytes 772
  18.5 7.5 %copy-start.10 = (s32[8]{0:T(128)S(1)}, s32[8]{0:T(128)}, u32[]{:S(2)}) copy-start(s32[8]{0:T(128)} %lengths_ref.1) | copy-start | bytes 100
  23.0 18.7 %all-to-all-start = ((bf16[32,8,1024]{2,1,0:T(8,128)(2,1)}), bf16[32,8,1024]{2,1,0:T(8,128)(2,1)S(1)}, u32[]{:S(2)}, u32[]{:S(2)}) async-start(bf16[32,8,1024]{2,1,0:T(8,128)(2,1)} %shard_map.134), calls=%async_computation | async-start | bytes 1048576 | tf_op jit(solution)/shard_map/all_to_all | solution.py:264

commit v8 on v7

--- a/solution.py
+++ b/solution.py
@@ -247,10 +247,8 @@
     place = (my_place("dp", 2 * 10**10), my_pair)
     farthest = exchange(block, even[0])
     both = jnp.concatenate([block, exchange(block, 1)], axis=0)
-    last = [s ^ odd for s in even[-1:] for odd in (0, 1)]
-    mine = [both, farthest] + [exchange(block, step) for step in last]
-    mine = mine + [exchange(both, step) for step in even[1:-1]] + [exchange(farthest, 1)]
-    order = [0, 1, even[0]] + last + [s ^ odd for s in even[1:-1] for odd in (0, 1)] + [even[0] ^ 1]
+    mine = [both, farthest] + [exchange(both, step) for step in even[1:]] + [exchange(farthest, 1)]
+    order = [0, 1, even[0]] + [s ^ odd for s in even[1:] for odd in (0, 1)] + [even[0] ^ 1]
 
     attention, lhs = attend(
         lengths, queries, key_cache, value_cache, new_key, new_value, routes, gate_weights,

time: 42.8 us -> 43 us (level)
    all_to_all x1, starting transfers between devices: 2.88 us -> 4.57 us  [body(): lax.all_to_all(sent, ('dp', 'pair', 'head'), split_axis=0, concat_axis=0,...]
    ppermute x6 -> x5, starting transfers between devices: 7.85 us -> 6.41 us  [other_core(): return lax.ppermute(rows, 'pair', [(i, i ^ 1) for i in range(pairs)])]
    ppermute x6 -> x5, starting transfers between devices: 8.99 us -> 8.87 us  [exchange(): return lax.ppermute(rows, 'dp', [(i, i ^ step) for i in range(steps)])]
    ppermute x6 -> x5, waiting for transfers between devices: 0.98 us -> 1.02 us  [other_core(): return lax.ppermute(rows, 'pair', [(i, i ^ 1) for i in range(pairs)])]
  transfers between devices with their start and end apart: 13 -> 11, of which waited for: 4 -> 3; matrix products, arithmetic and copies ran while one was open for 0% -> 0% of each run, Pallas kernels for 5% -> 5%
where the time goes in v8:
time: 43 us; the launch traced here: 42.7 us
  starting transfers between devices  19.9 us (46%)
  waiting for transfers between devices  14.9 us (35%)
  Pallas kernels  6.3 us (15%)
  local copies, waits for them, and re-layouts  0.87 us (2%)
  between operations  0.82 us (2%)
    all_to_all x1, waiting for transfers between devices, body(): lax.all_to_all(sent, ('dp', 'pair', 'head'), split_axis=0, concat_axis=0,...  13.8 us
    ppermute x5, starting transfers between devices, exchange(): return lax.ppermute(rows, 'dp', [(i, i ^ step) for i in range(steps)])  8.87 us
    ppermute x5, starting transfers between devices, other_core(): return lax.ppermute(rows, 'pair', [(i, i ^ 1) for i in range(pairs)])  6.41 us
    all_to_all x1, starting transfers between devices, body(): lax.all_to_all(sent, ('dp', 'pair', 'head'), split_axis=0, concat_axis=0,...  4.57 us
    pallas_call x1, Pallas kernels, expert_block(): pl.pallas_call(functools.partial(ffn_kernel, (capacity, heads, route_coun...  3.53 us
    pallas_call x1, Pallas kernels, attend(): pl.pallas_call(functools.partial(attend_kernel, capacity, heads), out_sha...  1.93 us
    ppermute x5, waiting for transfers between devices, other_core(): return lax.ppermute(rows, 'pair', [(i, i ^ 1) for i in range(pairs)])  1.02 us
    unnamed x24, local copies, waits for them, and re-layouts  0.86 us
  transfers between devices with their start and end apart: 11, of which 3 were waited for; matrix products, arithmetic and copies ran while one was open for 0% of the time, Pallas kernels for 5%

profile of v8, /device:TPU:1, one launch (start us, length us, event | category | flops | bytes accessed | tf_op | source)
XLA Modules:
  0.0 42.7 jit_solution(1601684478750601249)
XLA Ops:
  0.6 0.0 copy-start.3
  0.6 0.0 copy-start.11
  0.7 0.7 %copy-done.3 = s32[8,8]{1,0:T(8,128)S(1)} copy-done((s32[8,8]{1,0:T(8,128)S(1)}, s32[8,8]{1,0:T(8,128)}, u32[]{:S(2)}) %copy-start.3) | copy-done | bytes 280
  1.3 0.2 copy-done.11
  1.5 2.1 %collective-permute-start = (bf16[8,4224]{1,0:T(8,128)(2,1)S(1)}, bf16[8,4224]{1,0:T(8,128)(2,1)S(1)}, u32[]{:S(2)}, u32[]{:S(2)}) collective-permute-start(bf16[8,4224]{1,0:T(8,128)(2,1)S(1)} %pad_maximum_fusion.1), channel_id=1, source_target_pairs={{0,4},{4,0},{8,12},{12,8},{16,20},{20,16},{24,28},{28,24},{1,5},{5... | collective-permute-start | bytes 202760 | tf_op jit(solution)/shard_map/ppermute | solution.py:241
  3.6 3.3 %collective-permute-start.1 = (bf16[8,4224]{1,0:T(8,128)(2,1)S(1)}, bf16[8,4224]{1,0:T(8,128)(2,1)S(1)}, u32[]{:S(2)}, u32[]{:S(2)}) collective-permute-start(bf16[8,4224]{1,0:T(8,128)(2,1)S(1)} %pad_maximum_fusion.1), channel_id=1, source_target_pairs={{0,24},{4,28},{8,16},{12,20},{16,8},{20,12},{24,0},{28,4},{1,25},{... | collective-permute-start | bytes 202760 | tf_op jit(solution)/shard_map/ppermute | solution.py:241
  6.9 0.0 collective-permute-done
  6.9 0.0 copy-start
  6.9 0.0 copy-start.1
  6.9 0.0 copy-start.2
  6.9 0.9 %collective-permute-start.2 = (bf16[16,4224]{1,0:T(8,128)(2,1)S(1)}, bf16[16,4224]{1,0:T(8,128)(2,1)S(1)}, u32[]{:S(2)}, u32[]{:S(2)}) collective-permute-start(bf16[16,4224]{1,0:T(8,128)(2,1)S(1)} %pad_maximum_fusion.refs_0_), channel_id=1, source_target_pairs={{0,16},{4,20},{8,24},{12,28},{16,0},{20,4},{24,8},{28,12},{1,17},{... | collective-permute-start | bytes 405512 | tf_op jit(solution)/shard_map/ppermute | solution.py:241
  7.9 1.3 %collective-permute-start.3 = (bf16[16,4224]{1,0:T(8,128)(2,1)S(1)}, bf16[16,4224]{1,0:T(8,128)(2,1)S(1)}, u32[]{:S(2)}, u32[]{:S(2)}) collective-permute-start(bf16[16,4224]{1,0:T(8,128)(2,1)S(1)} %pad_maximum_fusion.refs_0_), channel_id=1, source_target_pairs={{0,8},{4,12},{8,0},{12,4},{16,24},{20,28},{24,16},{28,20},{1,9},{5... | collective-permute-start | bytes 405512 | tf_op jit(solution)/shard_map/ppermute | solution.py:241
  9.2 0.0 collective-permute-done.1.refs_1_
  9.2 1.2 %collective-permute-start.4 = (bf16[8,4224]{1,0:T(8,128)(2,1)S(1)}, bf16[8,4224]{1,0:T(8,128)(2,1)S(1)}, u32[]{:S(2)}, u32[]{:S(2)}) collective-permute-start(bf16[8,4224]{1,0:T(8,128)(2,1)S(1)} %collective-permute-done.1.refs_1_), channel_id=1, source_target_pairs={{0,4},{4,0},{8,12},{12,8},{16,20},{20,16},{24,28},{28,24},{1,5},{5... | collective-permute-start | bytes 202760 | tf_op jit(solution)/shard_map/ppermute | solution.py:241
  10.4 2.7 %collective-permute-start.5 = (bf16[16,4224]{1,0:T(8,128)(2,1)S(1)}, bf16[16,4224]{1,0:T(8,128)(2,1)S(1)}, u32[]{:S(2)}, u32[]{:S(2)}) collective-permute-start(bf16[16,4224]{1,0:T(8,128)(2,1)S(1)} %pad_maximum_fusion.refs_0_), channel_id=1, source_target_pairs={{0,1},{1,0},{2,3},{3,2},{4,5},{5,4},{6,7},{7,6},{8,9},{9,8},{10,11... | collective-permute-start | bytes 405512 | tf_op jit(solution)/shard_map/ppermute | solution.py:244
  13.1 0.0 collective-permute-start.6
  13.1 0.0 collective-permute-done.4.refs_4_
  13.1 2.8 %collective-permute-start.9 = (bf16[8,4224]{1,0:T(8,128)(2,1)S(1)}, bf16[8,4224]{1,0:T(8,128)(2,1)S(1)}, u32[]{:S(2)}, u32[]{:S(2)}) collective-permute-start(bf16[8,4224]{1,0:T(8,128)(2,1)S(1)} %collective-permute-done.4.refs_4_), channel_id=1, source_target_pairs={{0,1},{1,0},{2,3},{3,2},{4,5},{5,4},{6,7},{7,6},{8,9},{9,8},{10,11... | collective-permute-start | bytes 202760 | tf_op jit(solution)/shard_map/ppermute | solution.py:244
  15.9 0.0 collective-permute-done.2.refs_2_
  15.9 0.7 %collective-permute-start.7 = (bf16[16,4224]{1,0:T(8,128)(2,1)S(1)}, bf16[16,4224]{1,0:T(8,128)(2,1)S(1)}, u32[]{:S(2)}, u32[]{:S(2)}) collective-permute-start(bf16[16,4224]{1,0:T(8,128)(2,1)S(1)} %collective-permute-done.2.refs_2_), channel_id=1, source_target_pairs={{0,1},{1,0},{2,3},{3,2},{4,5},{5,4},{6,7},{7,6},{8,9},{9,8},{10,11... | collective-permute-start | bytes 405512 | tf_op jit(solution)/shard_map/ppermute | solution.py:244
  16.6 0.0 collective-permute-done.3.refs_3_
  16.6 0.2 collective-permute-start.8
  16.9 0.0 copy-start.4
  16.9 0.0 copy-start.6
  16.9 0.0 copy-start.7
  16.9 0.0 copy-start.8
  16.9 0.0 copy-start.9
  16.9 0.0 copy-start.10
  16.9 0.0 collective-permute-done.6.refs_6_
  16.9 0.0 collective-permute-done.5.refs_5_
  16.9 0.0 collective-permute-done.9.refs_9_
  16.9 0.6 %collective-permute-done.7.refs_7_ = bf16[16,4224]{1,0:T(8,128)(2,1)S(1)} collective-permute-done((bf16[16,4224]{1,0:T(8,128)(2,1)S(1)}, bf16[16,4224]{1,0:T(8,128)(2,1)S(1)}, u32[]{:S(2)}, u32[]{:S(2)}) %collective-permute-start.7) | collective-permute-done | bytes 135200 | tf_op jit(solution)/shard_map/ppermute | solution.py:244
  17.6 0.4 collective-permute-done.8.refs_8_
  18.0 0.0 copy-done
  18.0 0.0 copy-done.1
  18.0 0.0 copy-done.2
  18.0 3.5 %shard_map.134 = bf16[32,8,1024]{2,1,0:T(8,128)(2,1)} custom-call(s32[8,128]{1,0:T(8,128)S(1)} %shard_map.133.dp_ref, s32[8,128]{1,0:T(8,128)S(1)} %shard_map.131.pair_ref, bf16[16,4224]{1,0:T(8,128)(2,1)S(1)} %pad_maximum_fusion.refs_0_, bf16[8,4224]{1,0:T(8,128)(2,1)S(1)} %collective-permute-done.1.refs_1_, ...), custom_call_target="tpu_custom_call" | custom-call | flops 1207959552 | bytes 9437184 | tf_op jit(solution)/shard_map/pallas_call | solution.py:187
  21.5 4.6 %all-to-all-start = ((bf16[32,8,1024]{2,1,0:T(8,128)(2,1)}), bf16[32,8,1024]{2,1,0:T(8,128)(2,1)S(1)}, u32[]{:S(2)}, u32[]{:S(2)}) async-start(bf16[32,8,1024]{2,1,0:T(8,128)(2,1)} %shard_map.134), calls=%async_computation | async-start | bytes 1048576 | tf_op jit(solution)/shard_map/all_to_all | solution.py:262
  26.1 0.0 copy-done.4
  26.1 0.0 copy-done.5
  26.1 0.0 copy-done.6
  26.1 0.0 copy-done.7
  26.1 0.0 copy-done.8
  26.1 0.0 copy-done.9
  26.1 0.0 copy-done.10
  26.2 1.9 %shard_map.132 = (bf16[8,32,128]{2,1,0:T(8,128)(2,1)}, bf16[48,256]{1,0:T(8,128)(2,1)S(1)}) custom-call(s32[8]{0:T(128)S(1)} %copy-done.10, bf16[8,32,128]{2,1,0:T(8,128)(2,1)S(1)} %copy-done.6, bf16[8,2,64,128]{3,2,1,0:T(8,128)(2,1)S(1)} %copy-done.4, bf16[8,2,64,128]{3,2,1,0:T(8,128)(2,1)S(1)} %copy-done.5, bf16[8,2,128]{2,1,0:T(2,128)(2,1)S(1)} %copy-done.7, ...), custom_call_target="tpu_custom_call" | custom-call | flops 1000000000 | bytes 1000000 | tf_op jit(solution)/shard_map/pallas_call | solution.py:94
  28.1 13.8 %all-to-all-done.got_ref = bf16[32,8,1024]{2,1,0:T(8,128)(2,1)S(1)} async-done(((bf16[32,8,1024]{2,1,0:T(8,128)(2,1)}), bf16[32,8,1024]{2,1,0:T(8,128)(2,1)S(1)}, u32[]{:S(2)}, u32[]{:S(2)}) %all-to-all-start) | async-done | bytes 524320 | tf_op jit(solution)/shard_map/all_to_all | solution.py:262
  41.9 0.8 %shard_map.135 = bf16[8,2048]{1,0:T(8,128)(2,1)} custom-call(bf16[48,256]{1,0:T(8,128)(2,1)S(1)} %get-tuple-element.8.lhs_ref, bf16[32,8,1024]{2,1,0:T(8,128)(2,1)S(1)} %all-to-all-done.got_ref), custom_call_target="tpu_custom_call" | custom-call | tf_op jit(solution)/shard_map/pallas_call | solution.py:264
  (7 shorter events, 0.0 us)
Async XLA Ops:
  0.6 0.7 %copy-start.3 = (s32[8,8]{1,0:T(8,128)S(1)}, s32[8,8]{1,0:T(8,128)}, u32[]{:S(2)}) copy-start(s32[8,8]{1,0:T(8,128)} %routes_ref) | copy-start | bytes 772
  0.6 0.8 %copy-start.11 = (bf16[8,4096]{1,0:T(8,128)(2,1)S(1)}, bf16[8,4096]{1,0:T(8,128)(2,1)}, u32[]{:S(2)}) copy-start(bf16[8,4096]{1,0:T(8,128)(2,1)} %param.18) | copy-start | bytes 196612
  1.5 5.4 %collective-permute-start = (bf16[8,4224]{1,0:T(8,128)(2,1)S(1)}, bf16[8,4224]{1,0:T(8,128)(2,1)S(1)}, u32[]{:S(2)}, u32[]{:S(2)}) collective-permute-start(bf16[8,4224]{1,0:T(8,128)(2,1)S(1)} %pad_maximum_fusion.1), channel_id=1, source_target_pairs={{0,4},{4,0},{8,12},{12,8},{16,20},{20,16},{24,28},{28,24},{1,5},{5... | collective-permute-start | bytes 202760 | tf_op jit(solution)/shard_map/ppermute | solution.py:241
  3.6 5.6 %collective-permute-start.1 = (bf16[8,4224]{1,0:T(8,128)(2,1)S(1)}, bf16[8,4224]{1,0:T(8,128)(2,1)S(1)}, u32[]{:S(2)}, u32[]{:S(2)}) collective-permute-start(bf16[8,4224]{1,0:T(8,128)(2,1)S(1)} %pad_maximum_fusion.1), channel_id=1, source_target_pairs={{0,24},{4,28},{8,16},{12,20},{16,8},{20,12},{24,0},{28,4},{1,25},{... | collective-permute-start | bytes 202760 | tf_op jit(solution)/shard_map/ppermute | solution.py:241
  6.9 11.1 %copy-start = (bf16[1,384,4096]{2,1,0:T(8,128)(2,1)S(1)}, bf16[1,384,4096]{2,1,0:T(8,128)(2,1)}, u32[]{:S(2)}) copy-start(bf16[1,384,4096]{2,1,0:T(8,128)(2,1)} %refs_10_.1) | copy-start | bytes 9437188
  6.9 11.0 %copy-start.1 = (bf16[1,384,4096]{2,1,0:T(8,128)(2,1)S(1)}, bf16[1,384,4096]{2,1,0:T(8,128)(2,1)}, u32[]{:S(2)}) copy-start(bf16[1,384,4096]{2,1,0:T(8,128)(2,1)} %refs_11_.1) | copy-start | bytes 9437188
  6.9 11.0 %copy-start.2 = (bf16[1,384,4096]{2,1,0:T(8,128)(2,1)S(1)}, bf16[1,384,4096]{2,1,0:T(8,128)(2,1)}, u32[]{:S(2)}) copy-start(bf16[1,384,4096]{2,1,0:T(8,128)(2,1)} %refs_12_.1) | copy-start | bytes 9437188
  6.9 8.9 %collective-permute-start.2 = (bf16[16,4224]{1,0:T(8,128)(2,1)S(1)}, bf16[16,4224]{1,0:T(8,128)(2,1)S(1)}, u32[]{:S(2)}, u32[]{:S(2)}) collective-permute-start(bf16[16,4224]{1,0:T(8,128)(2,1)S(1)} %pad_maximum_fusion.refs_0_), channel_id=1, source_target_pairs={{0,16},{4,20},{8,24},{12,28},{16,0},{20,4},{24,8},{28,12},{1,17},{... | collective-permute-start | bytes 405512 | tf_op jit(solution)/shard_map/ppermute | solution.py:241
  7.9 8.7 %collective-permute-start.3 = (bf16[16,4224]{1,0:T(8,128)(2,1)S(1)}, bf16[16,4224]{1,0:T(8,128)(2,1)S(1)}, u32[]{:S(2)}, u32[]{:S(2)}) collective-permute-start(bf16[16,4224]{1,0:T(8,128)(2,1)S(1)} %pad_maximum_fusion.refs_0_), channel_id=1, source_target_pairs={{0,8},{4,12},{8,0},{12,4},{16,24},{20,28},{24,16},{28,20},{1,9},{5... | collective-permute-start | bytes 405512 | tf_op jit(solution)/shard_map/ppermute | solution.py:241
  9.2 3.9 %collective-permute-start.4 = (bf16[8,4224]{1,0:T(8,128)(2,1)S(1)}, bf16[8,4224]{1,0:T(8,128)(2,1)S(1)}, u32[]{:S(2)}, u32[]{:S(2)}) collective-permute-start(bf16[8,4224]{1,0:T(8,128)(2,1)S(1)} %collective-permute-done.1.refs_1_), channel_id=1, source_target_pairs={{0,4},{4,0},{8,12},{12,8},{16,20},{20,16},{24,28},{28,24},{1,5},{5... | collective-permute-start | bytes 202760 | tf_op jit(solution)/shard_map/ppermute | solution.py:241
  10.4 6.5 %collective-permute-start.5 = (bf16[16,4224]{1,0:T(8,128)(2,1)S(1)}, bf16[16,4224]{1,0:T(8,128)(2,1)S(1)}, u32[]{:S(2)}, u32[]{:S(2)}) collective-permute-start(bf16[16,4224]{1,0:T(8,128)(2,1)S(1)} %pad_maximum_fusion.refs_0_), channel_id=1, source_target_pairs={{0,1},{1,0},{2,3},{3,2},{4,5},{5,4},{6,7},{7,6},{8,9},{9,8},{10,11... | collective-permute-start | bytes 405512 | tf_op jit(solution)/shard_map/ppermute | solution.py:244
  13.1 3.8 %collective-permute-start.6 = (bf16[8,4224]{1,0:T(8,128)(2,1)S(1)}, bf16[8,4224]{1,0:T(8,128)(2,1)S(1)}, u32[]{:S(2)}, u32[]{:S(2)}) collective-permute-start(bf16[8,4224]{1,0:T(8,128)(2,1)S(1)} %collective-permute-done.1.refs_1_), channel_id=1, source_target_pairs={{0,1},{1,0},{2,3},{3,2},{4,5},{5,4},{6,7},{7,6},{8,9},{9,8},{10,11... | collective-permute-start | bytes 202760 | tf_op jit(solution)/shard_map/ppermute | solution.py:244
  13.1 3.8 %collective-permute-start.9 = (bf16[8,4224]{1,0:T(8,128)(2,1)S(1)}, bf16[8,4224]{1,0:T(8,128)(2,1)S(1)}, u32[]{:S(2)}, u32[]{:S(2)}) collective-permute-start(bf16[8,4224]{1,0:T(8,128)(2,1)S(1)} %collective-permute-done.4.refs_4_), channel_id=1, source_target_pairs={{0,1},{1,0},{2,3},{3,2},{4,5},{5,4},{6,7},{7,6},{8,9},{9,8},{10,11... | collective-permute-start | bytes 202760 | tf_op jit(solution)/shard_map/ppermute | solution.py:244
  15.9 1.7 %collective-permute-start.7 = (bf16[16,4224]{1,0:T(8,128)(2,1)S(1)}, bf16[16,4224]{1,0:T(8,128)(2,1)S(1)}, u32[]{:S(2)}, u32[]{:S(2)}) collective-permute-start(bf16[16,4224]{1,0:T(8,128)(2,1)S(1)} %collective-permute-done.2.refs_2_), channel_id=1, source_target_pairs={{0,1},{1,0},{2,3},{3,2},{4,5},{5,4},{6,7},{7,6},{8,9},{9,8},{10,11... | collective-permute-start | bytes 405512 | tf_op jit(solution)/shard_map/ppermute | solution.py:244
  16.6 1.4 %collective-permute-start.8 = (bf16[16,4224]{1,0:T(8,128)(2,1)S(1)}, bf16[16,4224]{1,0:T(8,128)(2,1)S(1)}, u32[]{:S(2)}, u32[]{:S(2)}) collective-permute-start(bf16[16,4224]{1,0:T(8,128)(2,1)S(1)} %collective-permute-done.3.refs_3_), channel_id=1, source_target_pairs={{0,1},{1,0},{2,3},{3,2},{4,5},{5,4},{6,7},{7,6},{8,9},{9,8},{10,11... | collective-permute-start | bytes 405512 | tf_op jit(solution)/shard_map/ppermute | solution.py:244
  16.9 9.2 %copy-start.4 = (bf16[8,2,64,128]{3,2,1,0:T(8,128)(2,1)S(1)}, bf16[8,2,64,128]{3,2,1,0:T(8,128)(2,1)}, u32[]{:S(2)}) copy-start(bf16[8,2,64,128]{3,2,1,0:T(8,128)(2,1)} %keys_ref.1) | copy-start | bytes 786436
  16.9 9.2 %copy-start.5 = (bf16[8,2,64,128]{3,2,1,0:T(8,128)(2,1)S(1)}, bf16[8,2,64,128]{3,2,1,0:T(8,128)(2,1)}, u32[]{:S(2)}) copy-start(bf16[8,2,64,128]{3,2,1,0:T(8,128)(2,1)} %values_ref.1) | copy-start | bytes 786436
  16.9 9.2 %copy-start.6 = (bf16[8,32,128]{2,1,0:T(8,128)(2,1)S(1)}, bf16[8,32,128]{2,1,0:T(8,128)(2,1)}, u32[]{:S(2)}) copy-start(bf16[8,32,128]{2,1,0:T(8,128)(2,1)} %queries_ref.1) | copy-start | bytes 196612
  16.9 9.3 %copy-start.7 = (bf16[8,2,128]{2,1,0:T(2,128)(2,1)S(1)}, bf16[8,2,128]{2,1,0:T(2,128)(2,1)}, u32[]{:S(2)}) copy-start(bf16[8,2,128]{2,1,0:T(2,128)(2,1)} %new_key_ref.1) | copy-start | bytes 12292
  16.9 9.2 %copy-start.8 = (bf16[8,2,128]{2,1,0:T(2,128)(2,1)S(1)}, bf16[8,2,128]{2,1,0:T(2,128)(2,1)}, u32[]{:S(2)}) copy-start(bf16[8,2,128]{2,1,0:T(2,128)(2,1)} %new_value_ref.1) | copy-start | bytes 12292
  16.9 9.2 %copy-start.9 = (f32[8,8]{1,0:T(8,128)S(1)}, f32[8,8]{1,0:T(8,128)}, u32[]{:S(2)}) copy-start(f32[8,8]{1,0:T(8,128)} %weights_ref.1) | copy-start | bytes 772
  16.9 9.2 %copy-start.10 = (s32[8]{0:T(128)S(1)}, s32[8]{0:T(128)}, u32[]{:S(2)}) copy-start(s32[8]{0:T(128)} %lengths_ref.1) | copy-start | bytes 100
  21.5 20.4 %all-to-all-start = ((bf16[32,8,1024]{2,1,0:T(8,128)(2,1)}), bf16[32,8,1024]{2,1,0:T(8,128)(2,1)S(1)}, u32[]{:S(2)}, u32[]{:S(2)}) async-start(bf16[32,8,1024]{2,1,0:T(8,128)(2,1)} %shard_map.134), calls=%async_computation | async-start | bytes 1048576 | tf_op jit(solution)/shard_map/all_to_all | solution.py:262

commit v9 on v8

--- a/solution.py
+++ b/solution.py
@@ -246,8 +246,9 @@
     even = sorted(range(2, steps, 2), reverse=True)
     place = (my_place("dp", 2 * 10**10), my_pair)
     farthest = exchange(block, even[0])
-    both = jnp.concatenate([block, exchange(block, 1)], axis=0)
-    mine = [both, farthest] + [exchange(both, step) for step in even[1:]] + [exchange(farthest, 1)]
+    beside = exchange(block, 1)
+    both = jnp.concatenate([block, beside], axis=0)
+    mine = [block, beside, farthest] + [exchange(both, step) for step in even[1:]] + [exchange(farthest, 1)]
     order = [0, 1, even[0]] + [s ^ odd for s in even[1:] for odd in (0, 1)] + [even[0] ^ 1]
 
     attention, lhs = attend(

time: 43 us -> 43 us (level)
  starting transfers between devices: 19.9 us -> 17.8 us
  waiting for transfers between devices: 14.9 us -> 16.9 us
    ppermute x5 -> x6, starting transfers between devices: 6.41 us -> 4.4 us  [other_core(): return lax.ppermute(rows, 'pair', [(i, i ^ 1) for i in range(pairs)])]
    ppermute x5, waiting for transfers between devices: 0.01 us -> 2.02 us  [exchange(): return lax.ppermute(rows, 'dp', [(i, i ^ step) for i in range(steps)])]
    ppermute x5 -> x6, waiting for transfers between devices: 1.02 us -> 1.03 us  [other_core(): return lax.ppermute(rows, 'pair', [(i, i ^ 1) for i in range(pairs)])]
  transfers between devices with their start and end apart: 11 -> 12, of which waited for: 3 -> 5; matrix products, arithmetic and copies ran while one was open for 0% -> 0% of each run, Pallas kernels for 5% -> 5%
where the time goes in v9:
time: 43 us; the launch traced here: 42.7 us
  starting transfers between devices  17.8 us (41%)
  waiting for transfers between devices  16.9 us (39%)
  Pallas kernels  6.3 us (15%)
  local copies, waits for them, and re-layouts  0.87 us (2%)
  between operations  0.82 us (2%)
    all_to_all x1, waiting for transfers between devices, body(): lax.all_to_all(sent, ('dp', 'pair', 'head'), split_axis=0, concat_axis=0,...  13.8 us
    ppermute x5, starting transfers between devices, exchange(): return lax.ppermute(rows, 'dp', [(i, i ^ step) for i in range(steps)])  8.87 us
    all_to_all x1, starting transfers between devices, body(): lax.all_to_all(sent, ('dp', 'pair', 'head'), split_axis=0, concat_axis=0,...  4.56 us
    ppermute x6, starting transfers between devices, other_core(): return lax.ppermute(rows, 'pair', [(i, i ^ 1) for i in range(pairs)])  4.4 us
    pallas_call x1, Pallas kernels, expert_block(): pl.pallas_call(functools.partial(ffn_kernel, (capacity, heads, route_coun...  3.54 us
    ppermute x5, waiting for transfers between devices, exchange(): return lax.ppermute(rows, 'dp', [(i, i ^ step) for i in range(steps)])  2.02 us
    pallas_call x1, Pallas kernels, attend(): pl.pallas_call(functools.partial(attend_kernel, capacity, heads), out_sha...  1.93 us
    ppermute x6, waiting for transfers between devices, other_core(): return lax.ppermute(rows, 'pair', [(i, i ^ 1) for i in range(pairs)])  1.03 us
  transfers between devices with their start and end apart: 12, of which 5 were waited for; matrix products, arithmetic and copies ran while one was open for 0% of the time, Pallas kernels for 5%

profile of v9, /device:TPU:1, one launch (start us, length us, event | category | flops | bytes accessed | tf_op | source)
XLA Modules:
  0.0 42.7 jit_solution(18166185362480975098)
XLA Ops:
  0.6 0.0 copy-start.3
  0.6 0.0 copy-start.11
  0.7 0.7 %copy-done.3 = s32[8,8]{1,0:T(8,128)S(1)} copy-done((s32[8,8]{1,0:T(8,128)S(1)}, s32[8,8]{1,0:T(8,128)}, u32[]{:S(2)}) %copy-start.3) | copy-done | bytes 280
  1.3 0.2 copy-done.11
  1.5 2.1 %collective-permute-start = (bf16[8,4224]{1,0:T(8,128)(2,1)S(1)}, bf16[8,4224]{1,0:T(8,128)(2,1)S(1)}, u32[]{:S(2)}, u32[]{:S(2)}) collective-permute-start(bf16[8,4224]{1,0:T(8,128)(2,1)S(1)} %pad_maximum_fusion.1.refs_0_), channel_id=1, source_target_pairs={{0,4},{4,0},{8,12},{12,8},{16,20},{20,16},{24,28},{28,24},{1,5},{5... | collective-permute-start | bytes 202760 | tf_op jit(solution)/shard_map/ppermute | solution.py:241
  3.6 3.3 %collective-permute-start.1 = (bf16[8,4224]{1,0:T(8,128)(2,1)S(1)}, bf16[8,4224]{1,0:T(8,128)(2,1)S(1)}, u32[]{:S(2)}, u32[]{:S(2)}) collective-permute-start(bf16[8,4224]{1,0:T(8,128)(2,1)S(1)} %pad_maximum_fusion.1.refs_0_), channel_id=1, source_target_pairs={{0,24},{4,28},{8,16},{12,20},{16,8},{20,12},{24,0},{28,4},{1,25},{... | collective-permute-start | bytes 202760 | tf_op jit(solution)/shard_map/ppermute | solution.py:241
  6.9 0.0 collective-permute-done.refs_1_
  6.9 0.0 copy-start
  6.9 0.0 copy-start.1
  6.9 0.0 copy-start.2
  6.9 0.9 %collective-permute-start.2 = (bf16[16,4224]{1,0:T(8,128)(2,1)S(1)}, bf16[16,4224]{1,0:T(8,128)(2,1)S(1)}, u32[]{:S(2)}, u32[]{:S(2)}) collective-permute-start(bf16[16,4224]{1,0:T(8,128)(2,1)S(1)} %pad_maximum_fusion), channel_id=1, source_target_pairs={{0,16},{4,20},{8,24},{12,28},{16,0},{20,4},{24,8},{28,12},{1,17},{... | collective-permute-start | bytes 405512 | tf_op jit(solution)/shard_map/ppermute | solution.py:241
  7.9 1.3 %collective-permute-start.3 = (bf16[16,4224]{1,0:T(8,128)(2,1)S(1)}, bf16[16,4224]{1,0:T(8,128)(2,1)S(1)}, u32[]{:S(2)}, u32[]{:S(2)}) collective-permute-start(bf16[16,4224]{1,0:T(8,128)(2,1)S(1)} %pad_maximum_fusion), channel_id=1, source_target_pairs={{0,8},{4,12},{8,0},{12,4},{16,24},{20,28},{24,16},{28,20},{1,9},{5... | collective-permute-start | bytes 405512 | tf_op jit(solution)/shard_map/ppermute | solution.py:241
  9.2 2.4 %collective-permute-start.5 = (bf16[8,4224]{1,0:T(8,128)(2,1)S(1)}, bf16[8,4224]{1,0:T(8,128)(2,1)S(1)}, u32[]{:S(2)}, u32[]{:S(2)}) collective-permute-start(bf16[8,4224]{1,0:T(8,128)(2,1)S(1)} %pad_maximum_fusion.1.refs_0_), channel_id=1, source_target_pairs={{0,1},{1,0},{2,3},{3,2},{4,5},{5,4},{6,7},{7,6},{8,9},{9,8},{10,11... | collective-permute-start | bytes 202760 | tf_op jit(solution)/shard_map/ppermute | solution.py:244
  11.6 0.0 collective-permute-done.1.refs_2_
  11.6 1.2 %collective-permute-start.4 = (bf16[8,4224]{1,0:T(8,128)(2,1)S(1)}, bf16[8,4224]{1,0:T(8,128)(2,1)S(1)}, u32[]{:S(2)}, u32[]{:S(2)}) collective-permute-start(bf16[8,4224]{1,0:T(8,128)(2,1)S(1)} %collective-permute-done.1.refs_2_), channel_id=1, source_target_pairs={{0,4},{4,0},{8,12},{12,8},{16,20},{20,16},{24,28},{28,24},{1,5},{5... | collective-permute-start | bytes 202760 | tf_op jit(solution)/shard_map/ppermute | solution.py:241
  12.8 0.3 collective-permute-start.6
  13.1 0.0 collective-permute-done.5.refs_6_
  13.1 0.2 collective-permute-start.7
  13.3 2.0 %collective-permute-done.4.refs_5_ = bf16[8,4224]{1,0:T(8,128)(2,1)S(1)} collective-permute-done((bf16[8,4224]{1,0:T(8,128)(2,1)S(1)}, bf16[8,4224]{1,0:T(8,128)(2,1)S(1)}, u32[]{:S(2)}, u32[]{:S(2)}) %collective-permute-start.4) | collective-permute-done | bytes 67616 | tf_op jit(solution)/shard_map/ppermute | solution.py:241
  15.3 0.8 %collective-permute-start.10 = (bf16[8,4224]{1,0:T(8,128)(2,1)S(1)}, bf16[8,4224]{1,0:T(8,128)(2,1)S(1)}, u32[]{:S(2)}, u32[]{:S(2)}) collective-permute-start(bf16[8,4224]{1,0:T(8,128)(2,1)S(1)} %collective-permute-done.4.refs_5_), channel_id=1, source_target_pairs={{0,1},{1,0},{2,3},{3,2},{4,5},{5,4},{6,7},{7,6},{8,9},{9,8},{10,11... | collective-permute-start | bytes 202760 | tf_op jit(solution)/shard_map/ppermute | solution.py:244
  16.1 0.0 collective-permute-done.2.refs_3_
  16.1 0.5 %collective-permute-start.8 = (bf16[16,4224]{1,0:T(8,128)(2,1)S(1)}, bf16[16,4224]{1,0:T(8,128)(2,1)S(1)}, u32[]{:S(2)}, u32[]{:S(2)}) collective-permute-start(bf16[16,4224]{1,0:T(8,128)(2,1)S(1)} %collective-permute-done.2.refs_3_), channel_id=1, source_target_pairs={{0,1},{1,0},{2,3},{3,2},{4,5},{5,4},{6,7},{7,6},{8,9},{9,8},{10,11... | collective-permute-start | bytes 405512 | tf_op jit(solution)/shard_map/ppermute | solution.py:244
  16.6 0.0 collective-permute-done.3.refs_4_
  16.6 0.2 collective-permute-start.9
  16.9 0.0 copy-start.7
  16.9 0.0 copy-start.8
  16.9 0.0 copy-start.9
  16.9 0.0 copy-start.10
  16.9 0.0 collective-permute-done.6.refs_7_
  16.9 0.0 collective-permute-done.7.refs_8_
  16.9 0.1 collective-permute-done.10.refs_11_
  17.0 0.6 %collective-permute-done.8.refs_9_ = bf16[16,4224]{1,0:T(8,128)(2,1)S(1)} collective-permute-done((bf16[16,4224]{1,0:T(8,128)(2,1)S(1)}, bf16[16,4224]{1,0:T(8,128)(2,1)S(1)}, u32[]{:S(2)}, u32[]{:S(2)}) %collective-permute-start.8) | collective-permute-done | bytes 135200 | tf_op jit(solution)/shard_map/ppermute | solution.py:244
  17.6 0.4 collective-permute-done.9.refs_10_
  18.0 0.0 copy-done
  18.0 0.0 copy-done.1
  18.0 0.0 copy-done.2
  18.0 3.5 %shard_map.134 = bf16[32,8,1024]{2,1,0:T(8,128)(2,1)} custom-call(s32[8,128]{1,0:T(8,128)S(1)} %shard_map.133.dp_ref, s32[8,128]{1,0:T(8,128)S(1)} %shard_map.131.pair_ref, bf16[8,4224]{1,0:T(8,128)(2,1)S(1)} %pad_maximum_fusion.1.refs_0_, bf16[8,4224]{1,0:T(8,128)(2,1)S(1)} %collective-permute-done.refs_1_, ...), custom_call_target="tpu_custom_call" | custom-call | flops 1207959552 | bytes 9437184 | tf_op jit(solution)/shard_map/pallas_call | solution.py:187
  21.5 4.6 %all-to-all-start = ((bf16[32,8,1024]{2,1,0:T(8,128)(2,1)}), bf16[32,8,1024]{2,1,0:T(8,128)(2,1)S(1)}, u32[]{:S(2)}, u32[]{:S(2)}) async-start(bf16[32,8,1024]{2,1,0:T(8,128)(2,1)} %shard_map.134), calls=%async_computation | async-start | bytes 1048576 | tf_op jit(solution)/shard_map/all_to_all | solution.py:263
  26.1 0.0 copy-done.4
  26.1 0.0 copy-done.5
  26.1 0.0 copy-done.6
  26.1 0.0 copy-done.7
  26.1 0.0 copy-done.8
  26.1 0.0 copy-done.9
  26.1 0.0 copy-done.10
  26.1 1.9 %shard_map.132 = (bf16[8,32,128]{2,1,0:T(8,128)(2,1)}, bf16[48,256]{1,0:T(8,128)(2,1)S(1)}) custom-call(s32[8]{0:T(128)S(1)} %copy-done.10, bf16[8,32,128]{2,1,0:T(8,128)(2,1)S(1)} %copy-done.6, bf16[8,2,64,128]{3,2,1,0:T(8,128)(2,1)S(1)} %copy-done.4, bf16[8,2,64,128]{3,2,1,0:T(8,128)(2,1)S(1)} %copy-done.5, bf16[8,2,128]{2,1,0:T(2,128)(2,1)S(1)} %copy-done.7, ...), custom_call_target="tpu_custom_call" | custom-call | flops 1000000000 | bytes 1000000 | tf_op jit(solution)/shard_map/pallas_call | solution.py:94
  28.1 13.8 %all-to-all-done.got_ref = bf16[32,8,1024]{2,1,0:T(8,128)(2,1)S(1)} async-done(((bf16[32,8,1024]{2,1,0:T(8,128)(2,1)}), bf16[32,8,1024]{2,1,0:T(8,128)(2,1)S(1)}, u32[]{:S(2)}, u32[]{:S(2)}) %all-to-all-start) | async-done | bytes 524320 | tf_op jit(solution)/shard_map/all_to_all | solution.py:263
  41.9 0.8 %shard_map.135 = bf16[8,2048]{1,0:T(8,128)(2,1)} custom-call(bf16[48,256]{1,0:T(8,128)(2,1)S(1)} %get-tuple-element.8.lhs_ref, bf16[32,8,1024]{2,1,0:T(8,128)(2,1)S(1)} %all-to-all-done.got_ref), custom_call_target="tpu_custom_call" | custom-call | tf_op jit(solution)/shard_map/pallas_call | solution.py:265
  (9 shorter events, 0.0 us)
Async XLA Ops:
  0.6 0.7 %copy-start.3 = (s32[8,8]{1,0:T(8,128)S(1)}, s32[8,8]{1,0:T(8,128)}, u32[]{:S(2)}) copy-start(s32[8,8]{1,0:T(8,128)} %routes_ref) | copy-start | bytes 772
  0.6 0.8 %copy-start.11 = (bf16[8,4096]{1,0:T(8,128)(2,1)S(1)}, bf16[8,4096]{1,0:T(8,128)(2,1)}, u32[]{:S(2)}) copy-start(bf16[8,4096]{1,0:T(8,128)(2,1)} %param.18) | copy-start | bytes 196612
  1.5 5.4 %collective-permute-start = (bf16[8,4224]{1,0:T(8,128)(2,1)S(1)}, bf16[8,4224]{1,0:T(8,128)(2,1)S(1)}, u32[]{:S(2)}, u32[]{:S(2)}) collective-permute-start(bf16[8,4224]{1,0:T(8,128)(2,1)S(1)} %pad_maximum_fusion.1.refs_0_), channel_id=1, source_target_pairs={{0,4},{4,0},{8,12},{12,8},{16,20},{20,16},{24,28},{28,24},{1,5},{5... | collective-permute-start | bytes 202760 | tf_op jit(solution)/shard_map/ppermute | solution.py:241
  3.6 8.0 %collective-permute-start.1 = (bf16[8,4224]{1,0:T(8,128)(2,1)S(1)}, bf16[8,4224]{1,0:T(8,128)(2,1)S(1)}, u32[]{:S(2)}, u32[]{:S(2)}) collective-permute-start(bf16[8,4224]{1,0:T(8,128)(2,1)S(1)} %pad_maximum_fusion.1.refs_0_), channel_id=1, source_target_pairs={{0,24},{4,28},{8,16},{12,20},{16,8},{20,12},{24,0},{28,4},{1,25},{... | collective-permute-start | bytes 202760 | tf_op jit(solution)/shard_map/ppermute | solution.py:241
  6.9 11.1 %copy-start = (bf16[1,384,4096]{2,1,0:T(8,128)(2,1)S(1)}, bf16[1,384,4096]{2,1,0:T(8,128)(2,1)}, u32[]{:S(2)}) copy-start(bf16[1,384,4096]{2,1,0:T(8,128)(2,1)} %refs_12_.1) | copy-start | bytes 9437188
  6.9 11.0 %copy-start.1 = (bf16[1,384,4096]{2,1,0:T(8,128)(2,1)S(1)}, bf16[1,384,4096]{2,1,0:T(8,128)(2,1)}, u32[]{:S(2)}) copy-start(bf16[1,384,4096]{2,1,0:T(8,128)(2,1)} %refs_13_.1) | copy-start | bytes 9437188
  6.9 11.0 %copy-start.2 = (bf16[1,384,4096]{2,1,0:T(8,128)(2,1)S(1)}, bf16[1,384,4096]{2,1,0:T(8,128)(2,1)}, u32[]{:S(2)}) copy-start(bf16[1,384,4096]{2,1,0:T(8,128)(2,1)} %refs_14_.1) | copy-start | bytes 9437188
  6.9 9.2 %collective-permute-start.2 = (bf16[16,4224]{1,0:T(8,128)(2,1)S(1)}, bf16[16,4224]{1,0:T(8,128)(2,1)S(1)}, u32[]{:S(2)}, u32[]{:S(2)}) collective-permute-start(bf16[16,4224]{1,0:T(8,128)(2,1)S(1)} %pad_maximum_fusion), channel_id=1, source_target_pairs={{0,16},{4,20},{8,24},{12,28},{16,0},{20,4},{24,8},{28,12},{1,17},{... | collective-permute-start | bytes 405512 | tf_op jit(solution)/shard_map/ppermute | solution.py:241
  7.9 8.7 %collective-permute-start.3 = (bf16[16,4224]{1,0:T(8,128)(2,1)S(1)}, bf16[16,4224]{1,0:T(8,128)(2,1)S(1)}, u32[]{:S(2)}, u32[]{:S(2)}) collective-permute-start(bf16[16,4224]{1,0:T(8,128)(2,1)S(1)} %pad_maximum_fusion), channel_id=1, source_target_pairs={{0,8},{4,12},{8,0},{12,4},{16,24},{20,28},{24,16},{28,20},{1,9},{5... | collective-permute-start | bytes 405512 | tf_op jit(solution)/shard_map/ppermute | solution.py:241
  9.2 3.9 %collective-permute-start.5 = (bf16[8,4224]{1,0:T(8,128)(2,1)S(1)}, bf16[8,4224]{1,0:T(8,128)(2,1)S(1)}, u32[]{:S(2)}, u32[]{:S(2)}) collective-permute-start(bf16[8,4224]{1,0:T(8,128)(2,1)S(1)} %pad_maximum_fusion.1.refs_0_), channel_id=1, source_target_pairs={{0,1},{1,0},{2,3},{3,2},{4,5},{5,4},{6,7},{7,6},{8,9},{9,8},{10,11... | collective-permute-start | bytes 202760 | tf_op jit(solution)/shard_map/ppermute | solution.py:244
  11.6 3.8 %collective-permute-start.4 = (bf16[8,4224]{1,0:T(8,128)(2,1)S(1)}, bf16[8,4224]{1,0:T(8,128)(2,1)S(1)}, u32[]{:S(2)}, u32[]{:S(2)}) collective-permute-start(bf16[8,4224]{1,0:T(8,128)(2,1)S(1)} %collective-permute-done.1.refs_2_), channel_id=1, source_target_pairs={{0,4},{4,0},{8,12},{12,8},{16,20},{20,16},{24,28},{28,24},{1,5},{5... | collective-permute-start | bytes 202760 | tf_op jit(solution)/shard_map/ppermute | solution.py:241
  12.8 4.1 %collective-permute-start.6 = (bf16[8,4224]{1,0:T(8,128)(2,1)S(1)}, bf16[8,4224]{1,0:T(8,128)(2,1)S(1)}, u32[]{:S(2)}, u32[]{:S(2)}) collective-permute-start(bf16[8,4224]{1,0:T(8,128)(2,1)S(1)} %collective-permute-done.refs_1_), channel_id=1, source_target_pairs={{0,1},{1,0},{2,3},{3,2},{4,5},{5,4},{6,7},{7,6},{8,9},{9,8},{10,11... | collective-permute-start | bytes 202760 | tf_op jit(solution)/shard_map/ppermute | solution.py:244
  13.1 3.8 %collective-permute-start.7 = (bf16[8,4224]{1,0:T(8,128)(2,1)S(1)}, bf16[8,4224]{1,0:T(8,128)(2,1)S(1)}, u32[]{:S(2)}, u32[]{:S(2)}) collective-permute-start(bf16[8,4224]{1,0:T(8,128)(2,1)S(1)} %collective-permute-done.1.refs_2_), channel_id=1, source_target_pairs={{0,1},{1,0},{2,3},{3,2},{4,5},{5,4},{6,7},{7,6},{8,9},{9,8},{10,11... | collective-permute-start | bytes 202760 | tf_op jit(solution)/shard_map/ppermute | solution.py:244
  15.3 1.7 %collective-permute-start.10 = (bf16[8,4224]{1,0:T(8,128)(2,1)S(1)}, bf16[8,4224]{1,0:T(8,128)(2,1)S(1)}, u32[]{:S(2)}, u32[]{:S(2)}) collective-permute-start(bf16[8,4224]{1,0:T(8,128)(2,1)S(1)} %collective-permute-done.4.refs_5_), channel_id=1, source_target_pairs={{0,1},{1,0},{2,3},{3,2},{4,5},{5,4},{6,7},{7,6},{8,9},{9,8},{10,11... | collective-permute-start | bytes 202760 | tf_op jit(solution)/shard_map/ppermute | solution.py:244
  16.1 1.5 %collective-permute-start.8 = (bf16[16,4224]{1,0:T(8,128)(2,1)S(1)}, bf16[16,4224]{1,0:T(8,128)(2,1)S(1)}, u32[]{:S(2)}, u32[]{:S(2)}) collective-permute-start(bf16[16,4224]{1,0:T(8,128)(2,1)S(1)} %collective-permute-done.2.refs_3_), channel_id=1, source_target_pairs={{0,1},{1,0},{2,3},{3,2},{4,5},{5,4},{6,7},{7,6},{8,9},{9,8},{10,11... | collective-permute-start | bytes 405512 | tf_op jit(solution)/shard_map/ppermute | solution.py:244
  16.6 1.4 %collective-permute-start.9 = (bf16[16,4224]{1,0:T(8,128)(2,1)S(1)}, bf16[16,4224]{1,0:T(8,128)(2,1)S(1)}, u32[]{:S(2)}, u32[]{:S(2)}) collective-permute-start(bf16[16,4224]{1,0:T(8,128)(2,1)S(1)} %collective-permute-done.3.refs_4_), channel_id=1, source_target_pairs={{0,1},{1,0},{2,3},{3,2},{4,5},{5,4},{6,7},{7,6},{8,9},{9,8},{10,11... | collective-permute-start | bytes 405512 | tf_op jit(solution)/shard_map/ppermute | solution.py:244
  16.9 9.2 %copy-start.4 = (bf16[8,2,64,128]{3,2,1,0:T(8,128)(2,1)S(1)}, bf16[8,2,64,128]{3,2,1,0:T(8,128)(2,1)}, u32[]{:S(2)}) copy-start(bf16[8,2,64,128]{3,2,1,0:T(8,128)(2,1)} %keys_ref.1) | copy-start | bytes 786436
  16.9 9.2 %copy-start.5 = (bf16[8,2,64,128]{3,2,1,0:T(8,128)(2,1)S(1)}, bf16[8,2,64,128]{3,2,1,0:T(8,128)(2,1)}, u32[]{:S(2)}) copy-start(bf16[8,2,64,128]{3,2,1,0:T(8,128)(2,1)} %values_ref.1) | copy-start | bytes 786436
  16.9 9.2 %copy-start.6 = (bf16[8,32,128]{2,1,0:T(8,128)(2,1)S(1)}, bf16[8,32,128]{2,1,0:T(8,128)(2,1)}, u32[]{:S(2)}) copy-start(bf16[8,32,128]{2,1,0:T(8,128)(2,1)} %queries_ref.1) | copy-start | bytes 196612
  16.9 9.2 %copy-start.7 = (bf16[8,2,128]{2,1,0:T(2,128)(2,1)S(1)}, bf16[8,2,128]{2,1,0:T(2,128)(2,1)}, u32[]{:S(2)}) copy-start(bf16[8,2,128]{2,1,0:T(2,128)(2,1)} %new_key_ref.1) | copy-start | bytes 12292
  16.9 9.2 %copy-start.8 = (bf16[8,2,128]{2,1,0:T(2,128)(2,1)S(1)}, bf16[8,2,128]{2,1,0:T(2,128)(2,1)}, u32[]{:S(2)}) copy-start(bf16[8,2,128]{2,1,0:T(2,128)(2,1)} %new_value_ref.1) | copy-start | bytes 12292
  16.9 9.2 %copy-start.9 = (f32[8,8]{1,0:T(8,128)S(1)}, f32[8,8]{1,0:T(8,128)}, u32[]{:S(2)}) copy-start(f32[8,8]{1,0:T(8,128)} %weights_ref.1) | copy-start | bytes 772
  16.9 9.2 %copy-start.10 = (s32[8]{0:T(128)S(1)}, s32[8]{0:T(128)}, u32[]{:S(2)}) copy-start(s32[8]{0:T(128)} %lengths_ref.1) | copy-start | bytes 100
  21.5 20.4 %all-to-all-start = ((bf16[32,8,1024]{2,1,0:T(8,128)(2,1)}), bf16[32,8,1024]{2,1,0:T(8,128)(2,1)S(1)}, u32[]{:S(2)}, u32[]{:S(2)}) async-start(bf16[32,8,1024]{2,1,0:T(8,128)(2,1)} %shard_map.134), calls=%async_computation | async-start | bytes 1048576 | tf_op jit(solution)/shard_map/all_to_all | solution.py:263
